TPU v7x, 256 devices: a whole 4x4x8 slice. The times are simulated.
256 devices in a mesh: dom: 128 (over y, x, z), grp: 2 (over core).
Axes of the slice: x: 4, y: 4, z: 8, core: 2. Of those that a mesh axis runs over, the one named last changes fastest.
Arguments:
- features: bfloat16 [65536, 512], P(('dom', 'grp')), may hold values from -6 to 6
- hub_feat: bfloat16 [2048, 512], P(('dom', 'grp')), may hold values from -6 to 6
- adjacency: bfloat16 [6144, 128, 128], P(('dom', 'grp')), may hold values from 0 to 1
- block_row: int32 [256, 24], P(('dom', 'grp')), may hold values from 0 to 1
- block_col: int32 [256, 24], P(('dom', 'grp')), may hold values from 0 to 18
- block_count: int32 [256], P(('dom', 'grp')), may hold values from 18 to 24, as said below
- halo_send: int32 [256, 128], P(('dom', 'grp')), may hold values from 0 to 255
- w_self: bfloat16 [512, 512], replicated, may hold values from -0.25 to 0.25
- w_neigh: bfloat16 [512, 512], replicated, may hold values from -0.25 to 0.25
- out_grad: bfloat16 [65536, 512], P(('dom', 'grp')), may hold values from -6 to 6
Outputs:
- activations: bfloat16 [65536, 512], P(('dom', 'grp'))
- grad_features: float32 [65536, 512], P(('dom', 'grp'))
- grad_hub: float32 [2048, 512], P(('dom', 'grp'))
- grad_w_self: float32 [512, 512], replicated
- grad_w_neigh: float32 [512, 512], replicated
Inputs may be any that keep to these rules, and one draw needn't show every extreme that they name: `block_count`: slots at or past a partition's count are padding and are ignored; some partition uses all 24 slots.
All inputs are finite; a program needn't handle non-finite values.
Results may differ from a plain program's by a relative error of at most 0.015.
Values may be sent and summed in bfloat16 or wider, within the bound.
No kernel may reach another device: no remote copies, remote signals or barrier semaphores. Data moves between devices by JAX's collectives and lax.ppermute only.
A program may use at most 64 MiB of HBM per device.

v0:
```python
import math

import jax
import jax.numpy as jnp
from jax import lax
from jax.sharding import PartitionSpec as P

D = 512
BLOCKS_PER_ROW = 12


def shifted(value, axis, steps):
    count = lax.axis_size(axis)
    pairs = [(source, (source + steps) % count) for source in range(count)]
    return lax.ppermute(value, axis, pairs)


def per_device(
    features,
    hub_feat,
    adjacency,
    block_row,
    block_col,
    block_count,
    halo_send,
    w_self,
    w_neigh,
    out_grad,
):
    local_rows = features.shape[0]
    tile_size = adjacency.shape[1]
    row_blocks = local_rows // tile_size
    slot_total = adjacency.shape[0]
    group_slots = BLOCKS_PER_ROW
    group_count = slot_total // group_slots
    rows_index = block_row[0]
    cols_index = block_col[0]
    send_rows = halo_send[0]
    usable = jnp.arange(slot_total, dtype=jnp.int32) < block_count[0]
    outgoing = features[send_rows]
    halo_rows = shifted(outgoing, "dom", 1)
    hub_table = lax.all_gather(hub_feat, ("dom", "grp"), axis=0, tiled=True)
    sources = jnp.concatenate([features, halo_rows, hub_table], 0).reshape(-1, tile_size, D)
    col_blocks = sources.shape[0]
    row_onehot = jnp.where(
        (rows_index[None, :] == jnp.arange(row_blocks, dtype=jnp.int32)[:, None]) & usable[None, :],
        1.0,
        0.0,
    ).astype(jnp.float32)
    col_onehot = jnp.where(
        (cols_index[None, :] == jnp.arange(col_blocks, dtype=jnp.int32)[:, None]) & usable[None, :],
        1.0,
        0.0,
    ).astype(jnp.float32)
    tile_groups = adjacency.reshape(group_count, group_slots, tile_size, tile_size)
    row_groups = rows_index.reshape(group_count, group_slots)
    col_groups = cols_index.reshape(group_count, group_slots)
    row_masks = jnp.transpose(row_onehot.reshape(row_blocks, group_count, group_slots), (1, 0, 2))
    col_masks = jnp.transpose(col_onehot.reshape(col_blocks, group_count, group_slots), (1, 0, 2))

    def forward_group(total, items):
        tiles, cols_here, mask_here = items
        picked = sources[cols_here]
        products = jnp.einsum("nij,njd->nid", tiles, picked, preferred_element_type=jnp.float32)
        return (total + jnp.einsum("rn,nid->rid", mask_here, products), None)

    summed, _ = lax.scan(
        forward_group,
        jnp.zeros((row_blocks, tile_size, D), jnp.float32),
        (tile_groups, col_groups, row_masks),
    )
    summed = summed.reshape(local_rows, D)
    row_weights = jnp.sum(adjacency, axis=2, dtype=jnp.float32)
    degree = jnp.einsum("rn,ni->ri", row_onehot, row_weights).reshape(local_rows)
    norm_scale = (1.0 / jnp.sqrt(1.0 + degree))[:, None]
    aggregate = (summed * norm_scale).astype(jnp.bfloat16)
    preact = jnp.dot(features, w_self, preferred_element_type=jnp.float32) + jnp.dot(
        aggregate, w_neigh, preferred_element_type=jnp.float32
    )
    activations = jax.nn.silu(preact).astype(jnp.bfloat16)
    sigmoid_val = jax.nn.sigmoid(preact)
    grad_pre = (
        out_grad.astype(jnp.float32) * sigmoid_val * (1.0 + preact * (1.0 - sigmoid_val))
    ).astype(jnp.bfloat16)
    lead_dims = (((0,), (0,)), ((), ()))
    grad_self_w = lax.dot_general(features, grad_pre, lead_dims, preferred_element_type=jnp.float32)
    grad_neigh_w = lax.dot_general(
        aggregate, grad_pre, lead_dims, preferred_element_type=jnp.float32
    )
    total_self, total_neigh = lax.psum((grad_self_w, grad_neigh_w), ("dom", "grp"))
    factor = 1.0 / math.sqrt(local_rows * lax.axis_size("dom") * lax.axis_size("grp"))
    trail_dims = (((1,), (1,)), ((), ()))
    grad_input = lax.dot_general(grad_pre, w_self, trail_dims, preferred_element_type=jnp.float32)
    grad_agg = (
        lax.dot_general(grad_pre, w_neigh, trail_dims, preferred_element_type=jnp.float32)
        * norm_scale
    ).astype(jnp.bfloat16)
    grad_tiles = grad_agg.reshape(row_blocks, tile_size, D)

    def backward_group(total, items):
        tiles, rows_here, mask_here = items
        grad_blocks = grad_tiles[rows_here]
        grad_products = jnp.einsum(
            "nji,njd->nid", tiles, grad_blocks, preferred_element_type=jnp.float32
        )
        return (total + jnp.einsum("cn,nid->cid", mask_here, grad_products), None)

    grad_sources, _ = lax.scan(
        backward_group,
        jnp.zeros((col_blocks, tile_size, D), jnp.float32),
        (tile_groups, row_groups, col_masks),
    )
    grad_sources = grad_sources.reshape(-1, D)
    halo_grad = grad_sources[local_rows : local_rows + tile_size]
    hub_partial = grad_sources[local_rows + tile_size :]
    returned = shifted(halo_grad.astype(jnp.bfloat16), "dom", -1).astype(halo_grad.dtype)
    grad_hub = lax.psum_scatter(hub_partial, ("dom", "grp"), scatter_dimension=0, tiled=True)
    grad_features = (grad_input + grad_sources[:local_rows]).at[send_rows].add(returned)
    return (activations, grad_features, grad_hub, total_self * factor, total_neigh * factor)


def solution(mesh):
    in_specs = (
        P(("dom", "grp"), None),
        P(("dom", "grp"), None),
        P(("dom", "grp"), None, None),
        P(("dom", "grp"), None),
        P(("dom", "grp"), None),
        P(("dom", "grp")),
        P(("dom", "grp"), None),
        P(),
        P(),
        P(("dom", "grp"), None),
    )
    out_specs = (
        P(("dom", "grp"), None),
        P(("dom", "grp"), None),
        P(("dom", "grp"), None),
        P(),
        P(),
    )
    return jax.shard_map(
        per_device, mesh=mesh, in_specs=in_specs, out_specs=out_specs, check_vma=False
    )
```

profile of v0, /device:TPU:1, one launch (start us, length us, event | category | flops | bytes accessed | tf_op | source)
XLA Modules:
  0.0 1681.9 jit_solution(10637159338401424930)
XLA Ops:
  8.7 1.9 gather_fusion.2
  10.5 2.5 collective-permute-start
  14.2 1.3 reduce.6
  15.6 1.3 reduce.7
  17.0 1.4 convert_reduce_fusion
  19.8 5.1 collective-permute-done
  24.9 95.2 %all-gather.2.cloned.1.call-done = bf16[2048,512]{1,0:T(8,128)(2,1)} async-done(((bf16[8,512]{1,0:T(8,128)(2,1)}), bf16[2048,512]{1,0:T(8,128)(2,1)}) %all-gather.2.cloned.1.call-update) | async-done | bytes 2097168 | tf_op jit(solution)/shard_map/all_gather | solution.py:42
  120.0 3.3 pad_maximum_fusion
  123.3 15.0 while.22
  123.3 2.4 gather_fusion
  125.7 1.8 fusion.79
  127.5 3.3 fusion.80
  130.8 2.3 gather_fusion
  133.1 1.8 fusion.79
  134.9 3.4 fusion.80
  139.5 2.3 multiply_convert_fusion
  143.5 1.3 fusion.45
  145.1 13.7 while.23
  146.4 4.1 select_add_fusion.2
  151.8 6.9 select_add_fusion.2
  158.8 3.8 slice.20
  162.6 4.4 copy.18
  167.1 1.8 slice.17
  168.9 5.6 copy.17
  174.6 6.5 collective-permute-start.1
  181.4 2.6 collective-permute-done.1
  184.0 1.6 scatter_custom_fusion
  185.6 218.7 %all-reduce.3.cloned.1.call-done = (f32[512,512]{0,1:T(8,128)}, f32[512,512]{0,1:T(8,128)}) async-done(((f32[512,512]{0,1:T(8,128)}, f32[512,512]{0,1:T(8,128)}), (f32[512,512]{0,1:T(8,128)}, f32[512,512]{0,1:T(8,128)})) %all-reduce.3.cloned.1.call-update) | async-done | bytes 2097168 | tf_op jit(solution)/shard_map/psum | solution.py:90
  404.3 1.8 broadcast_multiply_fusion
  406.1 1.3 copy.20
  407.4 1.3 copy.21
  408.7 1266.7 %reduce-scatter.2.cloned.1.call-done = f32[8,512]{1,0:T(8,128)} async-done(((f32[2048,512]{1,0:T(8,128)}), f32[8,512]{1,0:T(8,128)}) %reduce-scatter.2.cloned.1.call-update) | async-done | bytes 16400 | tf_op jit(solution)/shard_map/reduce_scatter | solution.py:117
  (52 shorter events, 9.7 us)
Async XLA Ops:
  7.2 132.4 %copy-start = (bf16[512,512]{1,0:T(8,128)(2,1)S(1)}, bf16[512,512]{1,0:T(8,128)(2,1)}, u32[]{:S(2)}) copy-start(bf16[512,512]{1,0:T(8,128)(2,1)} %param.22) | copy-start | bytes 1572868
  7.2 11.4 copy-start.2
  7.2 12.5 copy-start.6
  7.2 11.4 copy-start.3
  7.2 112.8 %all-gather.2.cloned.1.call-start = ((), (), s32[]{:S(2)}) async-start(), calls=%async_computation.1 | async-start | bytes 2105344 | tf_op jit(solution)/shard_map/all_gather | solution.py:42
  8.0 396.3 %all-reduce.3.cloned.1.call-start = ((), (), s32[]{:S(2)}) async-start(), calls=%async_computation.3 | async-start | bytes 4194304 | tf_op jit(solution)/shard_map/psum | solution.py:90
  10.5 14.4 collective-permute-start
  19.8 103.5 %copy-start.1 = (bf16[24,128,128]{2,1,0:T(8,128)(2,1)S(1)}, bf16[24,128,128]{2,1,0:T(8,128)(2,1)}, u32[]{:S(2)}) copy-start(bf16[24,128,128]{2,1,0:T(8,128)(2,1)} %param.16) | copy-start | bytes 2359300
  144.8 1530.6 %reduce-scatter.2.cloned.1.call-start = ((), (), s32[]{:S(2)}) async-start(), calls=%async_computation.2 | async-start | bytes 4210688 | tf_op jit(solution)/shard_map/reduce_scatter | solution.py:117
  168.9 12.2 copy-start.4
  174.6 9.5 collective-permute-start.1
  185.6 220.5 %copy-start.5 = (f32[256,512]{1,0:T(8,128)}, f32[256,512]{1,0:T(8,128)S(1)}, u32[]{:S(2)}) copy-start(f32[256,512]{1,0:T(8,128)S(1)} %scatter_custom_fusion) | copy-start | bytes 1572868
Sparse Core Ops, SparseCore 0:
  11.8 108.2 all-gather.1
  145.0 259.2 all-reduce.2
  407.4 1267.9 reduce-scatter.1
where the time goes:
time: 1690 us; the launch traced here: 1680 us
  waiting for transfers between devices  1590 us (94%)
  matrix products  29.3 us (2%)
  local copies, waits for them, and re-layouts  28.1 us (2%)
    reduce_scatter x1, waiting for transfers between devices, per_device(): lax.psum_scatter(hub_partial, ('dom', 'grp'), scatter_dimension=0, tiled=...  1270 us
    psum x1, waiting for transfers between devices, per_device(): lax.psum((grad_self_w, grad_neigh_w), ('dom', 'grp'))  219 us
    all_gather x1, waiting for transfers between devices, per_device(): hub_table = lax.all_gather(hub_feat, ('dom', 'grp'), axis=0, tiled=True)  95.2 us
  transfers between devices with their start and end apart: 5, of which 5 were waited for; matrix products, arithmetic and copies ran while one was open for 3% of the time, Pallas kernels for 0%

commit v1 on v0

--- a/solution.py
+++ b/solution.py
@@ -3,16 +3,70 @@
 import jax
 import jax.numpy as jnp
 from jax import lax
+from jax.sharding import Mesh
 from jax.sharding import PartitionSpec as P
 
 D = 512
 BLOCKS_PER_ROW = 12
-
-
-def shifted(value, axis, steps):
-    count = lax.axis_size(axis)
+ALL = ("y", "x", "z", "c")
+PLANE = ("y", "x")
+
+
+def swap_cores(value):
+    return lax.ppermute(value, "c", [(0, 1), (1, 0)])
+
+
+def ring_shift(value, steps):
+    count = 1
+    for axis in ("y", "x", "z"):
+        count *= lax.axis_size(axis)
     pairs = [(source, (source + steps) % count) for source in range(count)]
-    return lax.ppermute(value, axis, pairs)
+    return lax.ppermute(value, ("y", "x", "z"), pairs)
+
+
+def exchange(value, axes):
+    return lax.all_to_all(value, axes, 0, 0, tiled=True)
+
+
+def spread(value, axes, count):
+    return exchange(jnp.broadcast_to(value[None], (count,) + value.shape), axes)
+
+
+def gather_hubs(hub_feat, zs, planes):
+    core = lax.axis_index("c")
+    column = spread(hub_feat, "z", zs)
+    mine = spread(column, PLANE, planes)
+    other = swap_cores(mine)
+    low = jnp.where(core == 0, mine, other)
+    high = jnp.where(core == 0, other, mine)
+    return jnp.stack([low, high], 2).reshape(-1, D)
+
+
+def reduce_all(hub_partial, self_partial, neigh_partial, zs, planes):
+    core = lax.axis_index("c")
+    hubs = hub_partial.astype(jnp.bfloat16).reshape(planes, zs, 2, -1, D)
+    hubs = jnp.transpose(hubs, (2, 0, 1, 3, 4)).reshape(2, planes, -1, D)
+    weights = jnp.stack([self_partial, neigh_partial]).astype(jnp.bfloat16)
+    weights = weights.reshape(2, planes, -1, D)
+    both = jnp.concatenate([hubs, weights], 2)
+    mine = jnp.where(core == 0, both[0], both[1])
+    theirs = jnp.where(core == 0, both[1], both[0])
+    got = swap_cores(theirs)
+    chip = (mine.astype(jnp.float32) + got.astype(jnp.float32)).astype(jnp.bfloat16)
+    plane = jnp.sum(exchange(chip, PLANE).astype(jnp.float32), 0).astype(jnp.bfloat16)
+    hub_rows = hubs.shape[2]
+    hub_part = plane[:hub_rows].reshape(zs, -1, D)
+    weight_part = plane[hub_rows:]
+    packed = jnp.concatenate(
+        [hub_part, jnp.broadcast_to(weight_part[None], (zs,) + weight_part.shape)], 1
+    )
+    total = jnp.sum(exchange(packed, "z").astype(jnp.float32), 0)
+    own = hub_part.shape[1]
+    weight_mine = spread(total[own:].astype(jnp.bfloat16), PLANE, planes).reshape(-1, D)
+    weight_other = swap_cores(weight_mine)
+    total_self = jnp.where(core == 0, weight_mine, weight_other).astype(jnp.float32)
+    total_neigh = jnp.where(core == 0, weight_other, weight_mine).astype(jnp.float32)
+    return total[:own], total_self, total_neigh
 
 
 def per_device(
@@ -27,6 +81,8 @@
     w_neigh,
     out_grad,
 ):
+    zs = lax.axis_size("z")
+    planes = lax.axis_size("y") * lax.axis_size("x")
     local_rows = features.shape[0]
     tile_size = adjacency.shape[1]
     row_blocks = local_rows // tile_size
@@ -38,8 +94,8 @@
     send_rows = halo_send[0]
     usable = jnp.arange(slot_total, dtype=jnp.int32) < block_count[0]
     outgoing = features[send_rows]
-    halo_rows = shifted(outgoing, "dom", 1)
-    hub_table = lax.all_gather(hub_feat, ("dom", "grp"), axis=0, tiled=True)
+    halo_rows = ring_shift(outgoing, 1)
+    hub_table = gather_hubs(hub_feat, zs, planes)
     sources = jnp.concatenate([features, halo_rows, hub_table], 0).reshape(-1, tile_size, D)
     col_blocks = sources.shape[0]
     row_onehot = jnp.where(
@@ -87,8 +143,7 @@
     grad_neigh_w = lax.dot_general(
         aggregate, grad_pre, lead_dims, preferred_element_type=jnp.float32
     )
-    total_self, total_neigh = lax.psum((grad_self_w, grad_neigh_w), ("dom", "grp"))
-    factor = 1.0 / math.sqrt(local_rows * lax.axis_size("dom") * lax.axis_size("grp"))
+    factor = 1.0 / math.sqrt(local_rows * 2 * zs * planes)
     trail_dims = (((1,), (1,)), ((), ()))
     grad_input = lax.dot_general(grad_pre, w_self, trail_dims, preferred_element_type=jnp.float32)
     grad_agg = (
@@ -113,32 +168,35 @@
     grad_sources = grad_sources.reshape(-1, D)
     halo_grad = grad_sources[local_rows : local_rows + tile_size]
     hub_partial = grad_sources[local_rows + tile_size :]
-    returned = shifted(halo_grad.astype(jnp.bfloat16), "dom", -1).astype(halo_grad.dtype)
-    grad_hub = lax.psum_scatter(hub_partial, ("dom", "grp"), scatter_dimension=0, tiled=True)
+    returned = ring_shift(halo_grad.astype(jnp.bfloat16), -1).astype(halo_grad.dtype)
+    grad_hub, total_self, total_neigh = reduce_all(
+        hub_partial, grad_self_w, grad_neigh_w, zs, planes
+    )
     grad_features = (grad_input + grad_sources[:local_rows]).at[send_rows].add(returned)
     return (activations, grad_features, grad_hub, total_self * factor, total_neigh * factor)
 
 
 def solution(mesh):
+    inner = Mesh(mesh.devices.reshape(4, 4, 8, 2), ALL)
     in_specs = (
-        P(("dom", "grp"), None),
-        P(("dom", "grp"), None),
-        P(("dom", "grp"), None, None),
-        P(("dom", "grp"), None),
-        P(("dom", "grp"), None),
-        P(("dom", "grp")),
-        P(("dom", "grp"), None),
-        P(),
-        P(),
-        P(("dom", "grp"), None),
+        P(ALL, None),
+        P(ALL, None),
+        P(ALL, None, None),
+        P(ALL, None),
+        P(ALL, None),
+        P(ALL),
+        P(ALL, None),
+        P(),
+        P(),
+        P(ALL, None),
     )
     out_specs = (
-        P(("dom", "grp"), None),
-        P(("dom", "grp"), None),
-        P(("dom", "grp"), None),
+        P(ALL, None),
+        P(ALL, None),
+        P(ALL, None),
         P(),
         P(),
     )
     return jax.shard_map(
-        per_device, mesh=mesh, in_specs=in_specs, out_specs=out_specs, check_vma=False
-    )
+        per_device, mesh=inner, in_specs=in_specs, out_specs=out_specs, check_vma=False
+    )

time: 1690 us -> 169 us (0.10)
  waiting for transfers between devices: 1590 us -> 21 us
  blocking collectives: 0 us -> 69 us
    reduce_scatter x1 -> x0, waiting for transfers between devices: 1270 us -> none  [per_device(): lax.psum_scatter(hub_partial, ('dom', 'grp'), scatter_dimension=0, tiled=...]
    psum x1 -> x0, waiting for transfers between devices: 219 us -> none  [per_device(): lax.psum((grad_self_w, grad_neigh_w), ('dom', 'grp'))]
    all_gather x1 -> x0, waiting for transfers between devices: 95.2 us -> none  [per_device(): hub_table = lax.all_gather(hub_feat, ('dom', 'grp'), axis=0, tiled=True)]
    all_to_all x0 -> x4, blocking collectives: none -> 69 us  [exchange(): return lax.all_to_all(value, axes, 0, 0, tiled=True)]
  transfers between devices with their start and end apart: 5 -> 6, of which waited for: 5 -> 4; matrix products, arithmetic and copies ran while one was open for 3% -> 6% of each run, Pallas kernels for 0% -> 0%
where the time goes in v1:
time: 169 us; the launch traced here: 168 us
  blocking collectives  69 us (41%)
  matrix products  29.1 us (17%)
  local copies, waits for them, and re-layouts  21.9 us (13%)
  waiting for transfers between devices  21 us (12%)
  starting transfers between devices  14 us (8%)
  other arithmetic  11.2 us (7%)
    all_to_all x4, blocking collectives, exchange(): return lax.all_to_all(value, axes, 0, 0, tiled=True)  69 us
    all_to_all x1, waiting for transfers between devices, exchange(): return lax.all_to_all(value, axes, 0, 0, tiled=True)  12.6 us
    dot_general x2, matrix products, backward_group(): return (total + jnp.einsum('cn,nid->cid', mask_here, grad_products), None)  11.1 us
    ppermute x3, starting transfers between devices, swap_cores(): return lax.ppermute(value, 'c', [(0, 1), (1, 0)])  6.81 us
    all_to_all x1, starting transfers between devices, exchange(): return lax.all_to_all(value, axes, 0, 0, tiled=True)  6.75 us
    dot_general x2, matrix products, forward_group(): return (total + jnp.einsum('rn,nid->rid', mask_here, products), None)  6.74 us
    while x1, local copies, waits for them, and re-layouts, per_device(): lax.scan(backward_group, jnp.zeros((col_blocks, tile_size, D), jnp.float3...  5.49 us
    ppermute x2, waiting for transfers between devices, ring_shift(): return lax.ppermute(value, ('y', 'x', 'z'), pairs)  4.77 us
  transfers between devices with their start and end apart: 6, of which 4 were waited for; matrix products, arithmetic and copies ran while one was open for 6% of the time, Pallas kernels for 0%

profile of v1, /device:TPU:1, one launch (start us, length us, event | category | flops | bytes accessed | tf_op | source)
XLA Modules:
  0.0 167.9 jit_solution(4248851586939644744)
XLA Ops:
  1.4 16.0 %all_to_all.25 = bf16[8,8,512]{2,1,0:T(8,128)(2,1)S(1)} all-to-all(bf16[8,8,512]{2,1,0:T(8,128)(2,1)S(1)} %broadcast_in_dim.62), channel_id=1, replica_groups=mesh['y'=4,'x'=4,'z'=8,'c'=2] {'z'}, dimensions={0} | all-to-all | bytes 131072 | tf_op jit(solution)/shard_map/all_to_all | solution.py:28
  18.6 6.8 %all-to-all-start.1 = ((bf16[16,8,8,512]{3,2,1,0:T(8,128)(2,1)}), bf16[16,8,8,512]{3,2,1,0:T(8,128)(2,1)S(1)}, u32[]{:S(2)}, u32[]{:S(2)}) async-start(bf16[16,8,8,512]{3,2,1,0:T(8,128)(2,1)} %broadcast_in_dim.63), calls=%async_computation.1 | async-start | bytes 2097152 | tf_op jit(solution)/shard_map/all_to_all | solution.py:28
  29.2 1.2 copy.28
  30.4 12.6 %all-to-all-done.1 = bf16[16,8,8,512]{3,2,1,0:T(8,128)(2,1)S(1)} async-done(((bf16[16,8,8,512]{3,2,1,0:T(8,128)(2,1)}), bf16[16,8,8,512]{3,2,1,0:T(8,128)(2,1)S(1)}, u32[]{:S(2)}, u32[]{:S(2)}) %all-to-all-start.1) | async-done | bytes 1048608 | tf_op jit(solution)/shard_map/all_to_all | solution.py:28
  43.0 3.3 %collective-permute-start.1 = (bf16[16,8,8,512]{3,2,1,0:T(8,128)(2,1)S(1)}, bf16[16,8,8,512]{3,2,1,0:T(8,128)(2,1)S(1)}, u32[]{:S(2)}, u32[]{:S(2)}) collective-permute-start(bf16[16,8,8,512]{3,2,1,0:T(8,128)(2,1)S(1)} %all-to-all-done.1), channel_id=1, source_target_pairs={{0,1},{1,0},{2,3},{3,2},{4,5},{5,4},{6,7},{7,6},{8,9},{9,8},{10,11... | collective-permute-start | bytes 3145736 | tf_op jit(solution)/shard_map/ppermute | solution.py:16
  46.8 1.1 fusion.46
  48.9 1.7 pad_maximum_fusion
  50.5 15.0 %while.22 = (s32[]{:T(128)}, f32[2,128,512]{2,0,1:T(2,128)}, bf16[2,2,12]{2,1,0:T(2,128)(2,1)S(1)}, bf16[2,12,128,128]{3,2,1,0:T(8,128)(2,1)S(1)}, s32[2,12]{1,0...) while((s32[]{:T(128)}, f32[2,128,512]{2,0,1:T(2,128)}, ...), condition=%wide.region_1.2_spmd.clone, body=%wide.region_0.1_spmd.clone.sunk | while | flops 204735520 | bytes 9311027 | solution.py:123
  50.6 2.3 %gather_fusion = bf16[12,128,512]{2,1,0:T(8,128)(2,1)S(1)} fusion(bf16[19,128,512]{2,1,0:T(8,128)(2,1)} %get-tuple-element.244, s32[1024]{0:T(1024)S(1)} %pad_clamp_fusion.5), kind=kCustom, calls=%fused_computation.clone.clone.1 | custom fusion | bytes 3145776 | tf_op jit(solution)/shard_map/while/body/eval_jaxpr/gather | solution.py:119
  52.9 1.7 %fusion.79 = bf16[12,128,512]{2,1,0:T(8,128)(2,1)} fusion(bf16[12,128,512]{2,1,0:T(8,128)(2,1)S(1)} %gather_fusion, bf16[2,12,128,128]{3,2,1,0:T(8,128)(2,1)S(1)} %get-tuple-element.242, s32[]{:T(128)S(6)} %copy.55), kind=kOutput, calls=%fused_computation.7.clone.1 | convolution fusion | flops 201326592 | bytes 3538948 | tf_op jit(solution)/shard_map/while/body/eval_jaxpr/nij,njd->nid/dot_general | solution.py:120
  54.7 3.3 %fusion.80 = f32[2,128,512]{2,0,1:T(2,128)} fusion(bf16[12,128,512]{2,1,0:T(8,128)(2,1)} %fusion.79, f32[2,128,512]{2,0,1:T(2,128)} %get-tuple-element.232, pred[]{:T(512)S(6)} %compare.6, bf16[2,2,12]{2,1,0:T(2,128)(2,1)S(1)} %get-tuple-element.241, s32[]{:T(128)S(6)} %copy.55), kind=kOutput, calls=%fused_computation.6.clone.1 | convolution fusion | flops 3407872 | bytes 2621957 | tf_op jit(solution)/shard_map/while/body/eval_jaxpr/rn,nid->rid/dot_general | solution.py:121
  58.0 2.3 %gather_fusion = bf16[12,128,512]{2,1,0:T(8,128)(2,1)S(1)} fusion(bf16[19,128,512]{2,1,0:T(8,128)(2,1)} %get-tuple-element.244, s32[1024]{0:T(1024)S(1)} %pad_clamp_fusion.5), kind=kCustom, calls=%fused_computation.clone.clone.1 | custom fusion | bytes 3145776 | tf_op jit(solution)/shard_map/while/body/eval_jaxpr/gather | solution.py:119
  60.3 1.7 %fusion.79 = bf16[12,128,512]{2,1,0:T(8,128)(2,1)} fusion(bf16[12,128,512]{2,1,0:T(8,128)(2,1)S(1)} %gather_fusion, bf16[2,12,128,128]{3,2,1,0:T(8,128)(2,1)S(1)} %get-tuple-element.242, s32[]{:T(128)S(6)} %copy.55), kind=kOutput, calls=%fused_computation.7.clone.1 | convolution fusion | flops 201326592 | bytes 3538948 | tf_op jit(solution)/shard_map/while/body/eval_jaxpr/nij,njd->nid/dot_general | solution.py:120
  62.1 3.4 %fusion.80 = f32[2,128,512]{2,0,1:T(2,128)} fusion(bf16[12,128,512]{2,1,0:T(8,128)(2,1)} %fusion.79, f32[2,128,512]{2,0,1:T(2,128)} %get-tuple-element.232, pred[]{:T(512)S(6)} %compare.6, bf16[2,2,12]{2,1,0:T(2,128)(2,1)S(1)} %get-tuple-element.241, s32[]{:T(128)S(6)} %copy.55), kind=kOutput, calls=%fused_computation.6.clone.1 | convolution fusion | flops 3407872 | bytes 2621957 | tf_op jit(solution)/shard_map/while/body/eval_jaxpr/rn,nid->rid/dot_general | solution.py:121
  65.5 1.1 copy.31
  66.8 2.4 %multiply_convert_fusion = (bf16[256,512]{1,0:T(8,128)(2,1)S(1)}, bf16[256,512]{1,0:T(8,128)(2,1)}) fusion(bf16[256,512]{1,0:T(8,128)(2,1)} %param.23, f32[256,512]{1,0:T(8,128)} %fusion.46, bf16[256,512]{1,0:T(8,128)(2,1)S(1)} %fusion.32, bf16[512,512]{1,0:T(8,128)(2,1)S(1)} %copy-done), kind=kOutput, calls=%fused_computation.60 | convolution fusion | flops 135921664 | bytes 2097152 | tf_op jit(solution)/shard_map/dot_general | solution.py:133
  69.6 1.1 convolution_convert_fusion.1
  70.7 13.5 %while.23 = (s32[]{:T(128)}, f32[19,128,512]{2,0,1:T(8,128)}, bf16[2,19,12]{1,2,0:T(8,128)(2,1)S(1)}, bf16[2,12,128,128]{2,3,1,0:T(8,128)(2,1)S(1)}, s32[2,12]{1...) while((s32[]{:T(128)}, f32[19,128,512]{2,0,1:T(8,128)}, ...), condition=%wide.region_4.5_spmd.clone, body=%wide.region_3.4_spmd.clone.sunk | while | flops 233702432 | bytes 18227508 | solution.py:163
  72.0 4.1 %select_add_fusion.2 = f32[19,128,512]{2,0,1:T(8,128)} fusion(f32[19,128,512]{2,0,1:T(8,128)} %get-tuple-element.256, pred[]{:T(512)S(6)} %compare.7, bf16[12,128,512]{2,1,0:T(8,128)(2,1)S(1)} %fusion.86, bf16[2,19,12]{1,2,0:T(8,128)(2,1)S(1)} %get-tuple-element.265, s32[]{:T(128)S(6)} %copy.61), kind=kOutput, calls=%fused_computation.19.clone.1 | convolution fusion | flops 32374784 | bytes 11538437 | tf_op jit(solution)/shard_map/while/body/eval_jaxpr/cn,nid->cid/dot_general | solution.py:161
  77.3 6.9 %select_add_fusion.2 = f32[19,128,512]{2,0,1:T(8,128)} fusion(f32[19,128,512]{2,0,1:T(8,128)} %get-tuple-element.256, pred[]{:T(512)S(6)} %compare.7, bf16[12,128,512]{2,1,0:T(8,128)(2,1)S(1)} %fusion.86, bf16[2,19,12]{1,2,0:T(8,128)(2,1)S(1)} %get-tuple-element.265, s32[]{:T(128)S(6)} %copy.61), kind=kOutput, calls=%fused_computation.19.clone.1 | convolution fusion | flops 32374784 | bytes 11538437 | tf_op jit(solution)/shard_map/while/body/eval_jaxpr/cn,nid->cid/dot_general | solution.py:161
  84.2 5.5 %copy.47 = bf16[19,128,512]{2,1,0:T(8,128)(2,1)S(1)} copy(f32[19,128,512]{2,0,1:T(8,128)} %get-tuple-element.70) | data formatting | bytes 7471104 | tf_op jit(solution)/shard_map/while | solution.py:163
  90.6 1.2 fusion.28
  94.0 3.0 %collective-permute-done.3 = bf16[16,96,512]{2,1,0:T(8,128)(2,1)S(1)} collective-permute-done((bf16[16,96,512]{2,1,0:T(8,128)(2,1)S(1)}, bf16[16,96,512]{2,1,0:T(8,128)(2,1)S(1)}, u32[]{:S(2)}, u32[]{:S(2)}) %collective-permute-start.3) | collective-permute-done | bytes 1572896 | tf_op jit(solution)/shard_map/ppermute | solution.py:16
  97.8 25.6 %all_to_all.26 = bf16[16,96,512]{2,1,0:T(8,128)(2,1)} all-to-all(bf16[16,96,512]{2,1,0:T(8,128)(2,1)S(1)} %fusion.27), channel_id=1, replica_groups=mesh['y'=4,'x'=4,'z'=8,'c'=2] {'y','x'}, dimensions={0} | all-to-all | bytes 3145728 | tf_op jit(solution)/shard_map/all_to_all | solution.py:28
  123.5 1.6 reduce_sum.31
  125.2 13.4 %all_to_all.27 = bf16[8,40,512]{2,1,0:T(8,128)(2,1)S(1)} all-to-all(bf16[8,40,512]{2,1,0:T(8,128)(2,1)S(1)} %pad_maximum_fusion.2), channel_id=1, replica_groups=mesh['y'=4,'x'=4,'z'=8,'c'=2] {'z'}, dimensions={0} | all-to-all | bytes 655360 | tf_op jit(solution)/shard_map/all_to_all | solution.py:28
  138.7 13.9 %all_to_all.28 = bf16[16,32,512]{2,1,0:T(8,128)(2,1)} all-to-all(bf16[16,32,512]{2,1,0:T(8,128)(2,1)S(1)} %broadcast_in_dim.70), channel_id=1, replica_groups=mesh['y'=4,'x'=4,'z'=8,'c'=2] {'y','x'}, dimensions={0} | all-to-all | bytes 1048576 | tf_op jit(solution)/shard_map/all_to_all | solution.py:28
  152.6 3.1 %collective-permute-start.4 = (bf16[512,512]{1,0:T(8,128)(2,1)}, bf16[512,512]{1,0:T(8,128)(2,1)}, u32[]{:S(2)}, u32[]{:S(2)}) collective-permute-start(bf16[512,512]{1,0:T(8,128)(2,1)} %bitcast.28), channel_id=1, source_target_pairs={{0,1},{1,0},{2,3},{3,2},{4,5},{5,4},{6,7},{7,6},{8,9},{9,8},{10,11... | collective-permute-start | bytes 1572872 | tf_op jit(solution)/shard_map/ppermute | solution.py:16
  155.7 1.8 %slice.37 = f32[2,128,512]{2,0,1:T(2,128)S(1)} slice(f32[19,128,512]{2,0,1:T(8,128)} %get-tuple-element.70), slice={[0:2], [0:128], [0:512]} | slice | bytes 1048576 | tf_op jit(solution)/shard_map/slice | solution.py:175
  158.1 4.8 %collective-permute-done.2 = bf16[128,512]{1,0:T(8,128)(2,1)S(1)} collective-permute-done((bf16[128,512]{1,0:T(8,128)(2,1)S(1)}, bf16[128,512]{1,0:T(8,128)(2,1)S(1)}, u32[]{:S(2)}, u32[]{:S(2)}) %collective-permute-start.2) | collective-permute-done | bytes 131104 | tf_op jit(solution)/shard_map/ppermute | solution.py:24
  162.8 1.6 scatter_custom_fusion
  165.1 2.8 %convert_multiply_fusion = (f32[512,512]{1,0:T(8,128)}, f32[512,512]{1,0:T(8,128)}) fusion(bf16[512,512]{1,0:T(8,128)(2,1)} %collective-permute-done.4, pred[]{:T(512)S(6)} %eq.52, bf16[16,32,512]{2,1,0:T(8,128)(2,1)} %all_to_all.28), kind=kLoop, calls=%fused_computation.53 | loop fusion | flops 1572864 | bytes 3145729 | tf_op jit(solution)/shard_map/mul | solution.py:176
  (87 shorter events, 14.7 us)
Async XLA Ops:
  0.6 66.1 %copy-start = (bf16[512,512]{1,0:T(8,128)(2,1)S(1)}, bf16[512,512]{1,0:T(8,128)(2,1)}, u32[]{:S(2)}) copy-start(bf16[512,512]{1,0:T(8,128)(2,1)} %param.22) | copy-start | bytes 1572868
  0.6 24.7 %copy-start.12 = (s32[1,128]{1,0:T(1,128)S(1)}, s32[1,128]{1,0:T(1,128)}, u32[]{:S(2)}) copy-start(s32[1,128]{1,0:T(1,128)} %param.20) | copy-start | bytes 1540
  0.7 24.7 %copy-start.2 = (bf16[256,512]{1,0:T(8,128)(2,1)S(1)}, bf16[256,512]{1,0:T(8,128)(2,1)}, u32[]{:S(2)}) copy-start(bf16[256,512]{1,0:T(8,128)(2,1)} %param.14) | copy-start | bytes 786436
  17.5 10.3 %copy-start.14 = (s32[1,24]{1,0:T(1,128)S(1)}, s32[1,24]{1,0:T(1,128)}, u32[]{:S(2)}) copy-start(s32[1,24]{1,0:T(1,128)} %param.17) | copy-start | bytes 292
  17.5 11.0 %copy-start.13 = (s32[1,24]{1,0:T(1,128)S(1)}, s32[1,24]{1,0:T(1,128)}, u32[]{:S(2)}) copy-start(s32[1,24]{1,0:T(1,128)} %param.18) | copy-start | bytes 292
  17.5 11.8 %copy-start.1 = (bf16[24,128,128]{2,1,0:T(8,128)(2,1)S(1)}, bf16[24,128,128]{2,1,0:T(8,128)(2,1)}, u32[]{:S(2)}) copy-start(bf16[24,128,128]{2,1,0:T(8,128)(2,1)} %param.16) | copy-start | bytes 2359300
  18.6 24.4 %all-to-all-start.1 = ((bf16[16,8,8,512]{3,2,1,0:T(8,128)(2,1)}), bf16[16,8,8,512]{3,2,1,0:T(8,128)(2,1)S(1)}, u32[]{:S(2)}, u32[]{:S(2)}) async-start(bf16[16,8,8,512]{3,2,1,0:T(8,128)(2,1)} %broadcast_in_dim.63), calls=%async_computation.1 | async-start | bytes 2097152 | tf_op jit(solution)/shard_map/all_to_all | solution.py:28
  25.3 21.4 %copy-start.6 = (bf16[512,512]{1,0:T(8,128)(2,1)S(1)}, bf16[512,512]{1,0:T(8,128)(2,1)}, u32[]{:S(2)}) copy-start(bf16[512,512]{1,0:T(8,128)(2,1)} %param.21) | copy-start | bytes 1572868
  26.2 22.6 %collective-permute-start = (bf16[128,512]{1,0:T(8,128)(2,1)S(1)}, bf16[128,512]{1,0:T(8,128)(2,1)S(1)}, u32[]{:S(2)}, u32[]{:S(2)}) collective-permute-start(bf16[128,512]{1,0:T(8,128)(2,1)S(1)} %gather_fusion.2), channel_id=1, source_target_pairs={{0,2},{2,4},{4,6},{6,8},{8,10},{10,12},{12,14},{14,16},{16,18},{18... | collective-permute-start | bytes 393224 | tf_op jit(solution)/shard_map/ppermute | solution.py:24
  43.0 5.5 %collective-permute-start.1 = (bf16[16,8,8,512]{3,2,1,0:T(8,128)(2,1)S(1)}, bf16[16,8,8,512]{3,2,1,0:T(8,128)(2,1)S(1)}, u32[]{:S(2)}, u32[]{:S(2)}) collective-permute-start(bf16[16,8,8,512]{3,2,1,0:T(8,128)(2,1)S(1)} %all-to-all-done.1), channel_id=1, source_target_pairs={{0,1},{1,0},{2,3},{3,2},{4,5},{5,4},{6,7},{7,6},{8,9},{9,8},{10,11... | collective-permute-start | bytes 3145736 | tf_op jit(solution)/shard_map/ppermute | solution.py:16
  66.8 2.5 %copy-start.9 = (bf16[256,512]{1,0:T(8,128)(2,1)}, bf16[256,512]{1,0:T(8,128)(2,1)S(1)}, u32[]{:S(2)}) copy-start(bf16[256,512]{1,0:T(8,128)(2,1)S(1)} %fusion.32) | copy-start | bytes 786436
  66.8 3.9 %copy-start.3 = (bf16[24,128,128]{1,2,0:T(8,128)(2,1)S(1)}, bf16[24,128,128]{1,2,0:T(8,128)(2,1)}, u32[]{:S(2)}) copy-start(bf16[24,128,128]{1,2,0:T(8,128)(2,1)} %copy.28) | copy-start | bytes 2359300
  69.2 1.5 copy-start.4
  84.2 5.5 %copy-start.10 = (bf16[256,512]{1,0:T(8,128)(2,1)S(1)}, bf16[256,512]{1,0:T(8,128)(2,1)}, u32[]{:S(2)}) copy-start(bf16[256,512]{1,0:T(8,128)(2,1)} %copy-done.9) | copy-start | bytes 786436
  84.2 6.3 %copy-start.5 = (bf16[256,512]{1,0:T(8,128)(2,1)S(1)}, bf16[256,512]{1,0:T(8,128)(2,1)}, u32[]{:S(2)}) copy-start(bf16[256,512]{1,0:T(8,128)(2,1)} %copy-done.4) | copy-start | bytes 786436
  92.0 1.0 copy-start.8
  93.6 3.5 %collective-permute-start.3 = (bf16[16,96,512]{2,1,0:T(8,128)(2,1)S(1)}, bf16[16,96,512]{2,1,0:T(8,128)(2,1)S(1)}, u32[]{:S(2)}, u32[]{:S(2)}) collective-permute-start(bf16[16,96,512]{2,1,0:T(8,128)(2,1)S(1)} %select_bitcast_fusion), channel_id=1, source_target_pairs={{0,1},{1,0},{2,3},{3,2},{4,5},{5,4},{6,7},{7,6},{8,9},{9,8},{10,11... | collective-permute-start | bytes 4718600 | tf_op jit(solution)/shard_map/ppermute | solution.py:16
  138.6 19.1 %copy-start.7 = (bf16[512,512]{1,0:T(8,128)(2,1)S(1)}, bf16[512,512]{1,0:T(8,128)(2,1)}, u32[]{:S(2)}) copy-start(bf16[512,512]{1,0:T(8,128)(2,1)} %param.21) | copy-start | bytes 1572868
  152.6 12.4 %collective-permute-start.4 = (bf16[512,512]{1,0:T(8,128)(2,1)}, bf16[512,512]{1,0:T(8,128)(2,1)}, u32[]{:S(2)}, u32[]{:S(2)}) collective-permute-start(bf16[512,512]{1,0:T(8,128)(2,1)} %bitcast.28), channel_id=1, source_target_pairs={{0,1},{1,0},{2,3},{3,2},{4,5},{5,4},{6,7},{7,6},{8,9},{9,8},{10,11... | collective-permute-start | bytes 1572872 | tf_op jit(solution)/shard_map/ppermute | solution.py:16
  157.6 5.2 %collective-permute-start.2 = (bf16[128,512]{1,0:T(8,128)(2,1)S(1)}, bf16[128,512]{1,0:T(8,128)(2,1)S(1)}, u32[]{:S(2)}, u32[]{:S(2)}) collective-permute-start(bf16[128,512]{1,0:T(8,128)(2,1)S(1)} %slice_bitcast_fusion), channel_id=1, source_target_pairs={{0,254},{2,0},{4,2},{6,4},{8,6},{10,8},{12,10},{14,12},{16,14},{18... | collective-permute-start | bytes 393224 | tf_op jit(solution)/shard_map/ppermute | solution.py:24
  164.4 3.5 %copy-start.11 = (f32[256,512]{1,0:T(8,128)}, f32[256,512]{1,0:T(8,128)S(1)}, u32[]{:S(2)}) copy-start(f32[256,512]{1,0:T(8,128)S(1)} %scatter_custom_fusion) | copy-start | bytes 1572868

commit v2 on v1

v2 whole, which is shorter than its diff:
```python
import functools
import math

import jax
import jax.numpy as jnp
from jax import lax
from jax.experimental import pallas as pl
from jax.experimental.pallas import tpu as pltpu
from jax.sharding import Mesh
from jax.sharding import PartitionSpec as P

D = 512
TILE = 128
ROW_BLOCKS = 2
LOCAL_ROWS = ROW_BLOCKS * TILE
OWN = 8
F32 = jnp.float32
BF16 = jnp.bfloat16
ALL = ("y", "x", "z", "c")
PLANE = ("y", "x")


def dot(a, b, contract=((1,), (0,))):
    return lax.dot_general(a, b, (contract, ((), ())), preferred_element_type=F32)


def layer_kernel(
    count_ref,
    row_ref,
    col_ref,
    core_ref,
    feat_ref,
    halo_ref,
    mine_ref,
    other_ref,
    adj_ref,
    ws_ref,
    wn_ref,
    og_ref,
    act_ref,
    base_ref,
    back_ref,
    keep_ref,
    send_ref,
    table,
    wide,
    wide_t,
    gathered,
    acc,
):
    slots = adj_ref.shape[0]
    hub_tiles, column_rows, _ = mine_ref.shape
    first_hub = ROW_BLOCKS + 1
    count = count_ref[0]
    low_core = core_ref[0] == 0
    weight_rows = D // hub_tiles

    table[:LOCAL_ROWS] = feat_ref[...]
    table[LOCAL_ROWS : LOCAL_ROWS + TILE] = halo_ref[...]

    def fill(t, carry):
        here = mine_ref[t].astype(F32)
        there = other_ref[t].astype(F32)
        low = jnp.where(low_core, here, there)
        high = jnp.where(low_core, there, here)
        pieces = []
        for at in range(0, column_rows, OWN):
            pieces += [low[at : at + OWN], high[at : at + OWN]]
        start = pl.multiple_of((first_hub + t) * TILE, TILE)
        table[pl.ds(start, TILE)] = jnp.concatenate(pieces, 0).astype(BF16)
        return carry

    lax.fori_loop(0, hub_tiles, fill, 0)

    for s in range(slots):
        span = pl.ds(s * TILE, TILE)
        tile = adj_ref[s]
        flipped = tile.T
        blank = jnp.zeros_like(tile)
        for r in range(ROW_BLOCKS):
            on = (row_ref[0, s] == r) & (s < count)
            wide[r * TILE : (r + 1) * TILE, span] = jnp.where(on, tile, blank)
            wide_t[span, r * TILE : (r + 1) * TILE] = jnp.where(on, flipped, blank)
        start = pl.multiple_of(col_ref[0, s] * TILE, TILE)
        gathered[span] = table[pl.ds(start, TILE)]

    degree = dot(wide[...], jnp.ones((slots * TILE, TILE), BF16))
    norm = 1.0 / jnp.sqrt(1.0 + degree)
    norm = jnp.concatenate([norm] * (D // TILE), 1)
    summed = dot(wide[...], gathered[...])
    aggregate = (summed * norm).astype(BF16)
    own = feat_ref[...]
    preact = dot(own, ws_ref[...]) + dot(aggregate, wn_ref[...])
    gate = jax.nn.sigmoid(preact)
    act_ref[...] = (preact * gate).astype(BF16)
    grad_pre = (og_ref[...].astype(F32) * gate * (1.0 + preact * (1.0 - gate))).astype(BF16)
    grad_agg = (dot(grad_pre, wn_ref[...], ((1,), (1,))) * norm).astype(BF16)

    acc[...] = jnp.zeros_like(acc)
    for s in range(slots):
        into = pl.ds(pl.multiple_of(col_ref[0, s] * TILE, TILE), TILE)
        acc[into] += dot(wide_t[s * TILE : (s + 1) * TILE], grad_agg)

    def ship(t, carry):
        start = pl.multiple_of((first_hub + t) * TILE, TILE)
        grads = acc[pl.ds(start, TILE)]
        low = jnp.concatenate([grads[at : at + OWN] for at in range(0, TILE, 2 * OWN)], 0)
        high = jnp.concatenate([grads[at + OWN : at + 2 * OWN] for at in range(0, TILE, 2 * OWN)], 0)
        keep_ref[t, :column_rows] = jnp.where(low_core, low, high).astype(BF16)
        send_ref[t, :column_rows] = jnp.where(low_core, high, low).astype(BF16)
        return carry

    lax.fori_loop(0, hub_tiles, ship, 0)

    grad_self_w = dot(own, grad_pre, ((0,), (0,)))
    grad_neigh_w = dot(aggregate, grad_pre, ((0,), (0,)))
    keep = jnp.where(low_core, grad_self_w, grad_neigh_w).astype(BF16)
    send = jnp.where(low_core, grad_neigh_w, grad_self_w).astype(BF16)
    keep_ref[:, column_rows:] = keep.reshape(hub_tiles, weight_rows, D)
    send_ref[:, column_rows:] = send.reshape(hub_tiles, weight_rows, D)
    base_ref[...] = dot(grad_pre, ws_ref[...], ((1,), (1,))) + acc[:LOCAL_ROWS]
    back_ref[...] = acc[LOCAL_ROWS : LOCAL_ROWS + TILE].astype(BF16)


def layer(count, rows, cols, core, feat, halo, mine, other, adj, ws, wn, og):
    slots = adj.shape[0]
    hub_tiles, column_rows, _ = mine.shape
    sources = (ROW_BLOCKS + 1 + hub_tiles) * TILE
    parcel = jax.ShapeDtypeStruct((hub_tiles, column_rows + D // hub_tiles, D), BF16)
    smem = pl.BlockSpec(memory_space=pltpu.SMEM)
    vmem = pl.BlockSpec(memory_space=pltpu.VMEM)
    return pl.pallas_call(
        layer_kernel,
        out_shape=(
            jax.ShapeDtypeStruct((LOCAL_ROWS, D), BF16),
            jax.ShapeDtypeStruct((LOCAL_ROWS, D), F32),
            jax.ShapeDtypeStruct((TILE, D), BF16),
            parcel,
            parcel,
        ),
        in_specs=[smem] * 4 + [vmem] * 8,
        out_specs=(vmem,) * 5,
        scratch_shapes=[
            pltpu.VMEM((sources, D), BF16),
            pltpu.VMEM((LOCAL_ROWS, slots * TILE), BF16),
            pltpu.VMEM((slots * TILE, LOCAL_ROWS), BF16),
            pltpu.VMEM((slots * TILE, D), BF16),
            pltpu.VMEM((sources, D), F32),
        ],
        compiler_params=pltpu.CompilerParams(vmem_limit_bytes=48 * 1024 * 1024),
        name="layer",
    )(count, rows, cols, core, feat, halo, mine, other, adj, ws, wn, og)


def swap_cores(value):
    return lax.ppermute(value, "c", [(0, 1), (1, 0)])


def ring_shift(value, steps):
    count = 1
    for axis in ("y", "x", "z"):
        count *= lax.axis_size(axis)
    pairs = [(source, (source + steps) % count) for source in range(count)]
    return lax.ppermute(value, ("y", "x", "z"), pairs)


def exchange(value, axes):
    return lax.all_to_all(value, axes, 0, 0, tiled=True)


def spread(value, axes, count):
    return exchange(jnp.broadcast_to(value[None], (count,) + value.shape), axes)


def per_device(
    features,
    hub_feat,
    adjacency,
    block_row,
    block_col,
    block_count,
    halo_send,
    w_self,
    w_neigh,
    out_grad,
):
    zs = lax.axis_size("z")
    planes = lax.axis_size("y") * lax.axis_size("x")
    core = lax.axis_index("c").astype(jnp.int32)
    picks = halo_send[0]
    halo = ring_shift(features[picks], 1)
    column = spread(hub_feat, "z", zs).reshape(zs * OWN, D)
    mine = spread(column, PLANE, planes)
    other = swap_cores(mine)
    activations, base, back, keep, send = layer(
        block_count,
        block_row,
        block_col,
        core.reshape(1),
        features,
        halo,
        mine,
        other,
        adjacency,
        w_self,
        w_neigh,
        out_grad,
    )
    returned = ring_shift(back, -1)
    chip = (keep.astype(F32) + swap_cores(send).astype(F32)).astype(BF16)
    plane = jnp.sum(exchange(chip, PLANE).astype(F32), 0).astype(BF16)
    column_rows = zs * OWN
    hub_part = plane[:column_rows].reshape(zs, OWN, D)
    weight_part = plane[column_rows:]
    packed = jnp.concatenate(
        [hub_part, jnp.broadcast_to(weight_part[None], (zs,) + weight_part.shape)], 1
    )
    total = jnp.sum(exchange(packed, "z").astype(F32), 0)
    factor = 1.0 / math.sqrt(LOCAL_ROWS * 2 * zs * planes)
    weight_mine = spread((total[OWN:] * factor).astype(BF16), PLANE, planes).reshape(-1, D)
    weight_other = swap_cores(weight_mine)
    grad_w_self = jnp.where(core == 0, weight_mine, weight_other).astype(F32)
    grad_w_neigh = jnp.where(core == 0, weight_other, weight_mine).astype(F32)
    grad_features = base.at[picks].add(returned.astype(F32))
    return (activations, grad_features, total[:OWN], grad_w_self, grad_w_neigh)


def solution(mesh):
    inner = Mesh(mesh.devices.reshape(4, 4, 8, 2), ALL)
    in_specs = (
        P(ALL, None),
        P(ALL, None),
        P(ALL, None, None),
        P(ALL, None),
        P(ALL, None),
        P(ALL),
        P(ALL, None),
        P(),
        P(),
        P(ALL, None),
    )
    out_specs = (
        P(ALL, None),
        P(ALL, None),
        P(ALL, None),
        P(),
        P(),
    )
    return jax.shard_map(
        per_device, mesh=inner, in_specs=in_specs, out_specs=out_specs, check_vma=False
    )
```

time: 169 us -> 135 us (0.80)
  matrix products: 29.1 us -> 0 us
  blocking collectives: 69 us -> 90.5 us
  local copies, waits for them, and re-layouts: 21.9 us -> 5.15 us
  Pallas kernels: 0 us -> 7.02 us
  starting transfers between devices: 14 us -> 7.08 us
  other arithmetic: 11.2 us -> 5.26 us
  waiting for transfers between devices: 21 us -> 18.2 us
    dot_general x15 -> x0, matrix products: 29.1 us -> none  [the longest x2 11.1 us: backward_group(): return (total + jnp.einsum('cn,nid->cid', mask_here, grad_products), None)]
    all_to_all x4 -> x5, blocking collectives: 69 us -> 90.5 us  [exchange(): return lax.all_to_all(value, axes, 0, 0, tiled=True)]
    all_to_all x1 -> x0, waiting for transfers between devices: 12.6 us -> none  [exchange(): return lax.all_to_all(value, axes, 0, 0, tiled=True)]
    ppermute x2, waiting for transfers between devices: 4.77 us -> 15 us  [ring_shift(): return lax.ppermute(value, ('y', 'x', 'z'), pairs)]
    pallas_call x0 -> x1, Pallas kernels: none -> 7.02 us  [layer(): pl.pallas_call(layer_kernel, out_shape=(jax.ShapeDtypeStruct((LOCAL_ROWS,...]
    all_to_all x1 -> x0, starting transfers between devices: 6.75 us -> none  [exchange(): return lax.all_to_all(value, axes, 0, 0, tiled=True)]
    while x2 -> x0, local copies, waits for them, and re-layouts: 6.63 us -> none  [the longest x1 5.49 us: per_device(): lax.scan(backward_group, jnp.zeros((col_blocks, tile_size, D), jnp.float3...]
    gather x5 -> x1, local copies, waits for them, and re-layouts: 6.84 us -> 1.5 us  [per_device(): halo = ring_shift(features[picks], 1)]
  transfers between devices with their start and end apart: 6 -> 5, of which waited for: 4 -> 3; matrix products, arithmetic and copies ran while one was open for 6% -> 3% of each run, Pallas kernels for 0% -> 0%
where the time goes in v2:
time: 135 us
  blocking collectives  90.5 us (67%)
  waiting for transfers between devices  18.2 us (13%)
  starting transfers between devices  7.08 us (5%)
  Pallas kernels  7.02 us (5%)
  other arithmetic  5.26 us (4%)
  local copies, waits for them, and re-layouts  5.15 us (4%)
  between operations  1.47 us (1%)
    all_to_all x5, blocking collectives, exchange(): return lax.all_to_all(value, axes, 0, 0, tiled=True)  90.5 us
    ppermute x2, waiting for transfers between devices, ring_shift(): return lax.ppermute(value, ('y', 'x', 'z'), pairs)  15 us
    pallas_call x1, Pallas kernels, layer(): pl.pallas_call(layer_kernel, out_shape=(jax.ShapeDtypeStruct((LOCAL_ROWS,...  7.02 us
    ppermute x3, starting transfers between devices, swap_cores(): return lax.ppermute(value, 'c', [(0, 1), (1, 0)])  6.81 us
    ppermute x3, waiting for transfers between devices, swap_cores(): return lax.ppermute(value, 'c', [(0, 1), (1, 0)])  3.25 us
  transfers between devices with their start and end apart: 5, of which 3 were waited for; matrix products, arithmetic and copies ran while one was open for 3% of the time, Pallas kernels for 0%

profile of v2, /device:TPU:1, one launch (start us, length us, event | category | flops | bytes accessed | tf_op | source)
XLA Modules:
  0.0 134.7 jit_solution(6008664554643222102)
XLA Ops:
  0.6 0.7 broadcast_in_dim.10
  1.3 16.0 %all_to_all.25 = bf16[8,8,512]{2,1,0:T(8,128)(2,1)S(1)} all-to-all(bf16[8,8,512]{2,1,0:T(8,128)(2,1)S(1)} %broadcast_in_dim.10), channel_id=1, replica_groups=mesh['y'=4,'x'=4,'z'=8,'c'=2] {'z'}, dimensions={0} | all-to-all | bytes 131072 | tf_op jit(solution)/shard_map/all_to_all | solution.py:168
  17.4 0.1 broadcast_in_dim.12
  17.5 0.0 copy-start.1
  17.5 0.0 copy-start.4
  17.5 0.0 copy-start.5
  17.5 0.0 copy-start.6
  17.5 22.3 %all_to_all.26.mine_ref = bf16[16,64,512]{2,1,0:T(8,128)(2,1)S(1)} all-to-all(bf16[16,64,512]{2,1,0:T(8,128)(2,1)S(1)} %broadcast_in_dim.12), channel_id=1, replica_groups=mesh['y'=4,'x'=4,'z'=8,'c'=2] {'y','x'}, dimensions={0} | all-to-all | bytes 2097152 | tf_op jit(solution)/shard_map/all_to_all | solution.py:168
  39.8 2.9 %collective-permute-start.1 = (bf16[16,64,512]{2,1,0:T(8,128)(2,1)S(1)}, bf16[16,64,512]{2,1,0:T(8,128)(2,1)S(1)}, u32[]{:S(2)}, u32[]{:S(2)}) collective-permute-start(bf16[16,64,512]{2,1,0:T(8,128)(2,1)S(1)} %all_to_all.26.mine_ref), channel_id=1, source_target_pairs={{0,1},{1,0},{2,3},{3,2},{4,5},{5,4},{6,7},{7,6},{8,9},{9,8},{10,11... | collective-permute-start | bytes 3145736 | tf_op jit(solution)/shard_map/ppermute | solution.py:156
  42.7 1.5 %gather_fusion = bf16[128,512]{1,0:T(8,128)(2,1)} fusion(bf16[256,512]{1,0:T(8,128)(2,1)S(1)} %copy-done, s32[1024]{0:T(1024)S(1)} %pad_clamp_fusion), kind=kCustom, calls=%fused_computation | custom fusion | bytes 262656 | tf_op jit(solution)/shard_map/gather | solution.py:191
  44.2 0.3 collective-permute-start
  45.2 9.9 %collective-permute-done.halo_ref = bf16[128,512]{1,0:T(8,128)(2,1)S(1)} collective-permute-done((bf16[128,512]{1,0:T(8,128)(2,1)}, bf16[128,512]{1,0:T(8,128)(2,1)S(1)}, u32[]{:S(2)}, u32[]{:S(2)}) %collective-permute-start) | collective-permute-done | bytes 131104 | tf_op jit(solution)/shard_map/ppermute | solution.py:164
  55.0 0.0 copy-start.2
  55.1 1.0 copy-done.2
  56.1 1.0 copy-done.3
  57.1 7.0 %layer.1 = (bf16[256,512]{1,0:T(8,128)(2,1)}, f32[256,512]{1,0:T(8,128)}, bf16[128,512]{1,0:T(8,128)(2,1)S(1)}, bf16[16,96,512]{2,1,0:T(8,128)(2,1)}, bf16[16,96,512]{2,1,0:T(8,128)(2,1)}) custom-call(s32[1]{0:T(128)S(6)} %copy.16.count_ref, s32[1,24]{1,0:T(1,128)S(1)} %copy-done.5, s32[1,24]{1,0:T(1,128)S(1)} %copy-done.6, s32[1]{0:T(128)} %bitcast.core_ref, ...), custom_call_target="tpu_custom_call" | custom-call | tf_op jit(solution)/shard_map/layer/pallas_call | solution.py:132
  64.2 0.8 collective-permute-start.3
  64.9 3.2 %collective-permute-done.3 = bf16[16,96,512]{2,1,0:T(8,128)(2,1)S(1)} collective-permute-done((bf16[16,96,512]{2,1,0:T(8,128)(2,1)}, bf16[16,96,512]{2,1,0:T(8,128)(2,1)S(1)}, u32[]{:S(2)}, u32[]{:S(2)}) %collective-permute-start.3) | collective-permute-done | bytes 1572896 | tf_op jit(solution)/shard_map/ppermute | solution.py:156
  68.2 1.9 %add_convert_fusion = bf16[16,96,512]{2,1,0:T(8,128)(2,1)S(1)} fusion(bf16[16,96,512]{2,1,0:T(8,128)(2,1)S(1)} %collective-permute-done.3, bf16[16,96,512]{2,1,0:T(8,128)(2,1)} %get-tuple-element.13), kind=kLoop, calls=%fused_computation.2 | loop fusion | flops 3145728 | bytes 4718592 | tf_op jit(solution)/shard_map/convert_element_type | solution.py:210
  70.1 24.9 %all_to_all.27 = bf16[16,96,512]{2,1,0:T(8,128)(2,1)S(1)} all-to-all(bf16[16,96,512]{2,1,0:T(8,128)(2,1)S(1)} %add_convert_fusion), channel_id=1, replica_groups=mesh['y'=4,'x'=4,'z'=8,'c'=2] {'y','x'}, dimensions={0} | all-to-all | bytes 3145728 | tf_op jit(solution)/shard_map/all_to_all | solution.py:168
  95.0 0.2 reduce_sum.21
  95.3 0.0 copy-start.8
  95.3 0.0 copy-start.9
  95.4 13.5 %all_to_all.28 = bf16[8,40,512]{2,1,0:T(8,128)(2,1)S(1)} all-to-all(bf16[8,40,512]{2,1,0:T(8,128)(2,1)S(1)} %pad_maximum_fusion), channel_id=1, replica_groups=mesh['y'=4,'x'=4,'z'=8,'c'=2] {'z'}, dimensions={0} | all-to-all | bytes 655360 | tf_op jit(solution)/shard_map/all_to_all | solution.py:168
  109.0 13.7 %all_to_all.29 = bf16[16,32,512]{2,1,0:T(8,128)(2,1)S(1)} all-to-all(bf16[16,32,512]{2,1,0:T(8,128)(2,1)S(1)} %broadcast_in_dim.14), channel_id=1, replica_groups=mesh['y'=4,'x'=4,'z'=8,'c'=2] {'y','x'}, dimensions={0} | all-to-all | bytes 1048576 | tf_op jit(solution)/shard_map/all_to_all | solution.py:168
  122.7 3.1 %collective-permute-start.4 = (bf16[512,512]{1,0:T(8,128)(2,1)S(1)}, bf16[512,512]{1,0:T(8,128)(2,1)S(1)}, u32[]{:S(2)}, u32[]{:S(2)}) collective-permute-start(bf16[512,512]{1,0:T(8,128)(2,1)S(1)} %bitcast.11), channel_id=1, source_target_pairs={{0,1},{1,0},{2,3},{3,2},{4,5},{5,4},{6,7},{7,6},{8,9},{9,8},{10,11... | collective-permute-start | bytes 1572872 | tf_op jit(solution)/shard_map/ppermute | solution.py:156
  125.8 0.0 collective-permute-start.2
  125.8 5.1 %collective-permute-done.2 = bf16[128,512]{1,0:T(8,128)(2,1)S(1)} collective-permute-done((bf16[128,512]{1,0:T(8,128)(2,1)S(1)}, bf16[128,512]{1,0:T(8,128)(2,1)S(1)}, u32[]{:S(2)}, u32[]{:S(2)}) %collective-permute-start.2) | collective-permute-done | bytes 131104 | tf_op jit(solution)/shard_map/ppermute | solution.py:164
  130.9 1.6 %scatter_custom_fusion = f32[256,512]{1,0:T(8,128)S(1)} fusion(f32[256,512]{1,0:T(8,128)S(1)} %copy-done.9, s32[128]{0:T(128)S(1)} %fusion.3, bf16[128,512]{1,0:T(8,128)(2,1)S(1)} %collective-permute-done.2), kind=kCustom, calls=%fused_computation.7 | custom fusion | flops 131072 | bytes 655360 | tf_op jit(solution)/shard_map/scatter-add | solution.py:224
  132.5 0.0 copy-start.10
  132.5 0.6 slice.20
  133.2 1.5 %select_convert_fusion = (f32[512,512]{1,0:T(8,128)}, f32[512,512]{1,0:T(8,128)}) fusion(bf16[512,512]{1,0:T(8,128)(2,1)S(1)} %collective-permute-done.4, pred[]{:T(512)S(6)} %eq.4, bf16[16,32,512]{2,1,0:T(8,128)(2,1)S(1)} %all_to_all.29), kind=kLoop, calls=%fused_computation.4 | loop fusion | flops 1048576 | bytes 3145729 | tf_op jit(solution)/shard_map/convert_element_type | solution.py:223
  (25 shorter events, 0.2 us)
Async XLA Ops:
  17.4 25.4 %copy-start.11 = (s32[1,128]{1,0:T(1,128)S(1)}, s32[1,128]{1,0:T(1,128)}, u32[]{:S(2)}) copy-start(s32[1,128]{1,0:T(1,128)} %param.16) | copy-start | bytes 1540
  17.4 25.4 %copy-start = (bf16[256,512]{1,0:T(8,128)(2,1)S(1)}, bf16[256,512]{1,0:T(8,128)(2,1)}, u32[]{:S(2)}) copy-start(bf16[256,512]{1,0:T(8,128)(2,1)} %feat_ref.1) | copy-start | bytes 786436
  17.5 37.5 %copy-start.1 = (bf16[24,128,128]{2,1,0:T(8,128)(2,1)S(1)}, bf16[24,128,128]{2,1,0:T(8,128)(2,1)}, u32[]{:S(2)}) copy-start(bf16[24,128,128]{2,1,0:T(8,128)(2,1)} %adj_ref.1) | copy-start | bytes 2359300
  17.5 37.5 %copy-start.4 = (bf16[256,512]{1,0:T(8,128)(2,1)S(1)}, bf16[256,512]{1,0:T(8,128)(2,1)}, u32[]{:S(2)}) copy-start(bf16[256,512]{1,0:T(8,128)(2,1)} %og_ref.1) | copy-start | bytes 786436
  17.5 37.5 %copy-start.5 = (s32[1,24]{1,0:T(1,128)S(1)}, s32[1,24]{1,0:T(1,128)}, u32[]{:S(2)}) copy-start(s32[1,24]{1,0:T(1,128)} %row_ref.1) | copy-start | bytes 292
  17.5 37.5 %copy-start.6 = (s32[1,24]{1,0:T(1,128)S(1)}, s32[1,24]{1,0:T(1,128)}, u32[]{:S(2)}) copy-start(s32[1,24]{1,0:T(1,128)} %col_ref.1) | copy-start | bytes 292
  39.8 15.2 %collective-permute-start.1 = (bf16[16,64,512]{2,1,0:T(8,128)(2,1)S(1)}, bf16[16,64,512]{2,1,0:T(8,128)(2,1)S(1)}, u32[]{:S(2)}, u32[]{:S(2)}) collective-permute-start(bf16[16,64,512]{2,1,0:T(8,128)(2,1)S(1)} %all_to_all.26.mine_ref), channel_id=1, source_target_pairs={{0,1},{1,0},{2,3},{3,2},{4,5},{5,4},{6,7},{7,6},{8,9},{9,8},{10,11... | collective-permute-start | bytes 3145736 | tf_op jit(solution)/shard_map/ppermute | solution.py:156
  44.2 10.8 %collective-permute-start = (bf16[128,512]{1,0:T(8,128)(2,1)}, bf16[128,512]{1,0:T(8,128)(2,1)S(1)}, u32[]{:S(2)}, u32[]{:S(2)}) collective-permute-start(bf16[128,512]{1,0:T(8,128)(2,1)} %gather_fusion), channel_id=1, source_target_pairs={{0,2},{2,4},{4,6},{6,8},{8,10},{10,12},{12,14},{14,16},{16,18},{18... | collective-permute-start | bytes 393224 | tf_op jit(solution)/shard_map/ppermute | solution.py:164
  55.0 1.0 copy-start.2
  56.1 1.0 copy-start.3
  64.2 5.9 %copy-start.7 = (bf16[128,512]{1,0:T(8,128)(2,1)}, bf16[128,512]{1,0:T(8,128)(2,1)S(1)}, u32[]{:S(2)}) copy-start(bf16[128,512]{1,0:T(8,128)(2,1)S(1)} %get-tuple-element.12) | copy-start | bytes 393220
  64.2 4.0 %collective-permute-start.3 = (bf16[16,96,512]{2,1,0:T(8,128)(2,1)}, bf16[16,96,512]{2,1,0:T(8,128)(2,1)S(1)}, u32[]{:S(2)}, u32[]{:S(2)}) collective-permute-start(bf16[16,96,512]{2,1,0:T(8,128)(2,1)} %get-tuple-element.14), channel_id=1, source_target_pairs={{0,1},{1,0},{2,3},{3,2},{4,5},{5,4},{6,7},{7,6},{8,9},{9,8},{10,11... | collective-permute-start | bytes 4718600 | tf_op jit(solution)/shard_map/ppermute | solution.py:156
  95.3 30.5 %copy-start.8 = (bf16[128,512]{1,0:T(8,128)(2,1)S(1)}, bf16[128,512]{1,0:T(8,128)(2,1)}, u32[]{:S(2)}) copy-start(bf16[128,512]{1,0:T(8,128)(2,1)} %copy-done.7) | copy-start | bytes 393220
  95.3 35.6 %copy-start.9 = (f32[256,512]{1,0:T(8,128)S(1)}, f32[256,512]{1,0:T(8,128)}, u32[]{:S(2)}) copy-start(f32[256,512]{1,0:T(8,128)} %get-tuple-element.11) | copy-start | bytes 1572868
  122.7 10.5 %collective-permute-start.4 = (bf16[512,512]{1,0:T(8,128)(2,1)S(1)}, bf16[512,512]{1,0:T(8,128)(2,1)S(1)}, u32[]{:S(2)}, u32[]{:S(2)}) collective-permute-start(bf16[512,512]{1,0:T(8,128)(2,1)S(1)} %bitcast.11), channel_id=1, source_target_pairs={{0,1},{1,0},{2,3},{3,2},{4,5},{5,4},{6,7},{7,6},{8,9},{9,8},{10,11... | collective-permute-start | bytes 1572872 | tf_op jit(solution)/shard_map/ppermute | solution.py:156
  125.8 5.1 %collective-permute-start.2 = (bf16[128,512]{1,0:T(8,128)(2,1)S(1)}, bf16[128,512]{1,0:T(8,128)(2,1)S(1)}, u32[]{:S(2)}, u32[]{:S(2)}) collective-permute-start(bf16[128,512]{1,0:T(8,128)(2,1)S(1)} %copy-done.8), channel_id=1, source_target_pairs={{0,254},{2,0},{4,2},{6,4},{8,6},{10,8},{12,10},{14,12},{16,14},{18... | collective-permute-start | bytes 393224 | tf_op jit(solution)/shard_map/ppermute | solution.py:164
  132.5 2.2 %copy-start.10 = (f32[256,512]{1,0:T(8,128)}, f32[256,512]{1,0:T(8,128)S(1)}, u32[]{:S(2)}) copy-start(f32[256,512]{1,0:T(8,128)S(1)} %scatter_custom_fusion) | copy-start | bytes 1572868

commit v3 on v2

v3 whole, which is shorter than its diff:
```python
import math

import jax
import jax.numpy as jnp
from jax import lax
from jax.experimental import pallas as pl
from jax.experimental.pallas import tpu as pltpu
from jax.sharding import Mesh
from jax.sharding import PartitionSpec as P

D = 512
TILE = 128
ROW_BLOCKS = 2
LOCAL_ROWS = ROW_BLOCKS * TILE
OWN = 8
F32 = jnp.float32
BF16 = jnp.bfloat16
ALL = ("y", "x", "z", "c")
CHIPS = ("y", "x", "z")


def dot(a, b, contract=((1,), (0,))):
    return lax.dot_general(a, b, (contract, ((), ())), preferred_element_type=F32)


def prepare_kernel(
    count_ref, row_ref, adj_ref, feat_ref, ws_ref, wide_ref, flip_ref, norm_ref, pre_ref
):
    slots = adj_ref.shape[0]
    count = count_ref[0]
    degree = jnp.zeros((LOCAL_ROWS, TILE), F32)
    for s in range(slots):
        span = pl.ds(s * TILE, TILE)
        tile = adj_ref[s]
        flipped = tile.T
        blank = jnp.zeros_like(tile)
        parts = []
        for r in range(ROW_BLOCKS):
            on = (row_ref[0, s] == r) & (s < count)
            part = jnp.where(on, tile, blank)
            wide_ref[r * TILE : (r + 1) * TILE, span] = part
            flip_ref[span, r * TILE : (r + 1) * TILE] = jnp.where(on, flipped, blank)
            parts.append(part.astype(F32))
        degree += jnp.concatenate(parts, 0)
    norm = 1.0 / jnp.sqrt(1.0 + jnp.sum(degree, 1, keepdims=True))
    norm_ref[...] = jnp.broadcast_to(norm, (LOCAL_ROWS, TILE))
    pre_ref[...] = dot(feat_ref[...], ws_ref[...])


def layer_kernel(
    col_ref,
    core_ref,
    feat_ref,
    halo_ref,
    mine_ref,
    other_ref,
    wide_ref,
    flip_ref,
    norm_ref,
    pre_ref,
    ws_ref,
    wn_ref,
    og_ref,
    act_ref,
    base_ref,
    back_ref,
    keep_ref,
    send_ref,
    table,
    gathered,
    acc,
):
    slots = flip_ref.shape[0] // TILE
    hub_tiles, column_rows, _ = mine_ref.shape
    first_hub = ROW_BLOCKS + 1
    low_core = core_ref[0] == 0
    weight_rows = D // hub_tiles
    half = D * weight_rows // column_rows

    table[:LOCAL_ROWS] = feat_ref[...]
    table[LOCAL_ROWS : LOCAL_ROWS + TILE] = halo_ref[...]

    def fill(t, carry):
        here = mine_ref[t].astype(F32)
        there = other_ref[t].astype(F32)
        low = jnp.where(low_core, here, there)
        high = jnp.where(low_core, there, here)
        pieces = []
        for at in range(0, column_rows, OWN):
            pieces += [low[at : at + OWN], high[at : at + OWN]]
        start = pl.multiple_of((first_hub + t) * TILE, TILE)
        table[pl.ds(start, TILE)] = jnp.concatenate(pieces, 0).astype(BF16)
        return carry

    lax.fori_loop(0, hub_tiles, fill, 0)

    for s in range(slots):
        start = pl.multiple_of(col_ref[0, s] * TILE, TILE)
        gathered[s * TILE : (s + 1) * TILE] = table[pl.ds(start, TILE)]

    norm = jnp.concatenate([norm_ref[...]] * (D // TILE), 1)
    summed = dot(wide_ref[...], gathered[...])
    aggregate = (summed * norm).astype(BF16)
    own = feat_ref[...]
    preact = pre_ref[...] + dot(aggregate, wn_ref[...])
    gate = jax.nn.sigmoid(preact)
    act_ref[...] = (preact * gate).astype(BF16)
    grad_pre = (og_ref[...].astype(F32) * gate * (1.0 + preact * (1.0 - gate))).astype(BF16)
    grad_agg = (dot(grad_pre, wn_ref[...], ((1,), (1,))) * norm).astype(BF16)

    acc[...] = jnp.zeros_like(acc)
    for s in range(slots):
        into = pl.ds(pl.multiple_of(col_ref[0, s] * TILE, TILE), TILE)
        acc[into] += dot(flip_ref[s * TILE : (s + 1) * TILE], grad_agg)

    def ship(t, carry):
        start = pl.multiple_of((first_hub + t) * TILE, TILE)
        grads = acc[pl.ds(start, TILE)]
        low = jnp.concatenate([grads[at : at + OWN] for at in range(0, TILE, 2 * OWN)], 0)
        high = jnp.concatenate([grads[at + OWN : at + 2 * OWN] for at in range(0, TILE, 2 * OWN)], 0)
        keep_ref[t, :, :D] = jnp.where(low_core, low, high).astype(BF16)
        send_ref[t, :, :D] = jnp.where(low_core, high, low).astype(BF16)
        return carry

    lax.fori_loop(0, hub_tiles, ship, 0)

    grad_self_w = dot(own, grad_pre, ((0,), (0,)))
    grad_neigh_w = dot(aggregate, grad_pre, ((0,), (0,)))
    keep = jnp.where(low_core, grad_self_w, grad_neigh_w)
    send = jnp.where(low_core, grad_neigh_w, grad_self_w)
    for t in range(hub_tiles):
        for value, ref in ((keep, keep_ref), (send, send_ref)):
            pieces = []
            for z in range(column_rows // OWN):
                row = t * weight_rows + (z // 2) * OWN
                pieces.append(value[row : row + OWN, (z % 2) * half : (z % 2 + 1) * half])
            ref[t, :, D:] = jnp.concatenate(pieces, 0).astype(BF16)
    base_ref[...] = dot(grad_pre, ws_ref[...], ((1,), (1,))) + acc[:LOCAL_ROWS]
    back_ref[...] = acc[LOCAL_ROWS : LOCAL_ROWS + TILE].astype(BF16)


SMEM = pl.BlockSpec(memory_space=pltpu.SMEM)
VMEM = pl.BlockSpec(memory_space=pltpu.VMEM)


def prepare(count, rows, adj, feat, ws):
    wide = adj.shape[0] * TILE
    return pl.pallas_call(
        prepare_kernel,
        out_shape=(
            jax.ShapeDtypeStruct((LOCAL_ROWS, wide), BF16),
            jax.ShapeDtypeStruct((wide, LOCAL_ROWS), BF16),
            jax.ShapeDtypeStruct((LOCAL_ROWS, TILE), F32),
            jax.ShapeDtypeStruct((LOCAL_ROWS, D), F32),
        ),
        in_specs=[SMEM] * 2 + [VMEM] * 3,
        out_specs=(VMEM,) * 4,
        compiler_params=pltpu.CompilerParams(vmem_limit_bytes=16 * 1024 * 1024),
        cost_estimate=pl.CostEstimate(
            flops=2 * LOCAL_ROWS * D * D, bytes_accessed=5 * 1024 * 1024, transcendentals=0
        ),
        name="prepare",
    )(count, rows, adj, feat, ws)


def layer(cols, core, feat, halo, mine, other, wide, flip, norm, pre, ws, wn, og):
    hub_tiles, column_rows, _ = mine.shape
    sources = (ROW_BLOCKS + 1 + hub_tiles) * TILE
    parcel = jax.ShapeDtypeStruct((hub_tiles, column_rows, D + D * D // hub_tiles // column_rows), BF16)
    return pl.pallas_call(
        layer_kernel,
        out_shape=(
            jax.ShapeDtypeStruct((LOCAL_ROWS, D), BF16),
            jax.ShapeDtypeStruct((LOCAL_ROWS, D), F32),
            jax.ShapeDtypeStruct((TILE, D), BF16),
            parcel,
            parcel,
        ),
        in_specs=[SMEM] * 2 + [VMEM] * 11,
        out_specs=(VMEM,) * 5,
        scratch_shapes=[
            pltpu.VMEM((sources, D), BF16),
            pltpu.VMEM((wide.shape[1], D), BF16),
            pltpu.VMEM((sources, D), F32),
        ],
        compiler_params=pltpu.CompilerParams(vmem_limit_bytes=32 * 1024 * 1024),
        name="layer",
    )(cols, core, feat, halo, mine, other, wide, flip, norm, pre, ws, wn, og)


def swap_cores(value):
    return lax.ppermute(value, "c", [(0, 1), (1, 0)])


def ring_shift(value, steps):
    count = 1
    for axis in CHIPS:
        count *= lax.axis_size(axis)
    pairs = [(source, (source + steps) % count) for source in range(count)]
    return lax.ppermute(value, CHIPS, pairs)


def exchange(value):
    return lax.all_to_all(value, CHIPS, 0, 0, tiled=True)


def spread(value, count):
    return exchange(jnp.broadcast_to(value[None], (count,) + value.shape))


def per_device(
    features,
    hub_feat,
    adjacency,
    block_row,
    block_col,
    block_count,
    halo_send,
    w_self,
    w_neigh,
    out_grad,
):
    zs = lax.axis_size("z")
    planes = lax.axis_size("y") * lax.axis_size("x")
    chips = zs * planes
    core = lax.axis_index("c").astype(jnp.int32)
    picks = halo_send[0]
    chosen = (picks[:, None] == jnp.arange(LOCAL_ROWS, dtype=jnp.int32)[None, :]).astype(BF16)
    mine = spread(hub_feat, chips).reshape(planes, zs * OWN, D)
    halo = ring_shift(dot(chosen, features).astype(BF16), 1)
    wide, flip, norm, pre = prepare(block_count, block_row, adjacency, features, w_self)
    other = swap_cores(mine)
    activations, base, back, keep, send = layer(
        block_col,
        core.reshape(1),
        features,
        halo,
        mine,
        other,
        wide,
        flip,
        norm,
        pre,
        w_self,
        w_neigh,
        out_grad,
    )
    returned = ring_shift(back, -1)
    chip = (keep.astype(F32) + swap_cores(send).astype(F32)).astype(BF16)
    chip, returned = lax.optimization_barrier((chip, returned))
    total = jnp.sum(exchange(chip.reshape(chips, OWN, -1)).astype(F32), 0)
    factor = 1.0 / math.sqrt(LOCAL_ROWS * 2 * chips)
    weight_mine = spread((total[:, D:] * factor).astype(BF16), chips)
    weight_other = swap_cores(weight_mine)

    def unpack(value):
        rows = value.reshape(chips // 2, 2, OWN, -1)
        return jnp.transpose(rows, (0, 2, 1, 3)).reshape(D, D).astype(F32)

    grad_w_self = unpack(jnp.where(core == 0, weight_mine, weight_other))
    grad_w_neigh = unpack(jnp.where(core == 0, weight_other, weight_mine))
    grad_features = base + dot(chosen, returned, ((0,), (0,)))
    return (activations, grad_features, total[:, :D], grad_w_self, grad_w_neigh)


def solution(mesh):
    inner = Mesh(mesh.devices.reshape(4, 4, 8, 2), ALL)
    in_specs = (
        P(ALL, None),
        P(ALL, None),
        P(ALL, None, None),
        P(ALL, None),
        P(ALL, None),
        P(ALL),
        P(ALL, None),
        P(),
        P(),
        P(ALL, None),
    )
    out_specs = (
        P(ALL, None),
        P(ALL, None),
        P(ALL, None),
        P(),
        P(),
    )
    return jax.shard_map(
        per_device, mesh=inner, in_specs=in_specs, out_specs=out_specs, check_vma=False
    )
```

time: 135 us -> 156 us (1.16)
  blocking collectives: 90.5 us -> 120 us
  waiting for transfers between devices: 18.2 us -> 11.9 us
  local copies, waits for them, and re-layouts: 5.15 us -> 2.65 us
    all_to_all x5 -> x3, blocking collectives: 90.5 us -> 120 us  [exchange(): return lax.all_to_all(value, CHIPS, 0, 0, tiled=True)]
    ppermute x2, waiting for transfers between devices: 15 us -> 8.86 us  [ring_shift(): return lax.ppermute(value, CHIPS, pairs)]
    pallas_call x1, Pallas kernels: 7.02 us -> 5.25 us  [layer(): pl.pallas_call(layer_kernel, out_shape=(jax.ShapeDtypeStruct((LOCAL_ROWS,...]
    scatter-add x1 -> x0, other arithmetic: 1.57 us -> none  [per_device(): grad_features = base.at[picks].add(returned.astype(F32))]
  transfers between devices with their start and end apart: 5 -> 5, of which waited for: 3 -> 3; matrix products, arithmetic and copies ran while one was open for 3% -> 2% of each run, Pallas kernels for 0% -> 1%
where the time goes in v3:
time: 156 us
  blocking collectives  120 us (77%)
  waiting for transfers between devices  11.9 us (8%)
  starting transfers between devices  7.94 us (5%)
  Pallas kernels  6.61 us (4%)
  other arithmetic  3.97 us (3%)
  local copies, waits for them, and re-layouts  2.65 us (2%)
    all_to_all x3, blocking collectives, exchange(): return lax.all_to_all(value, CHIPS, 0, 0, tiled=True)  120 us
    ppermute x2, waiting for transfers between devices, ring_shift(): return lax.ppermute(value, CHIPS, pairs)  8.86 us
    ppermute x3, starting transfers between devices, swap_cores(): return lax.ppermute(value, 'c', [(0, 1), (1, 0)])  7.65 us
    pallas_call x1, Pallas kernels, layer(): pl.pallas_call(layer_kernel, out_shape=(jax.ShapeDtypeStruct((LOCAL_ROWS,...  5.25 us
  transfers between devices with their start and end apart: 5, of which 3 were waited for; matrix products, arithmetic and copies ran while one was open for 2% of the time, Pallas kernels for 1%

profile of v3, /device:TPU:1, one launch (start us, length us, event | category | flops | bytes accessed | tf_op | source)
XLA Modules:
  0.0 155.8 jit_solution(15496686489183659795)
XLA Ops:
  0.6 0.0 copy-start
  0.7 0.8 broadcast_in_dim.4
  1.5 0.0 copy-start.3
  1.5 0.0 copy-start.8
  1.5 46.5 %all_to_all.15 = bf16[128,8,512]{2,1,0:T(8,128)(2,1)S(1)} all-to-all(bf16[128,8,512]{2,1,0:T(8,128)(2,1)S(1)} %broadcast_in_dim.4), channel_id=1, replica_groups=mesh['y'=4,'x'=4,'z'=8,'c'=2] {'y','x','z'}, dimensions={0} | all-to-all | bytes 2097152 | tf_op jit(solution)/shard_map/all_to_all | solution.py:204
  48.0 2.6 %collective-permute-start.1 = (bf16[16,64,512]{2,1,0:T(8,128)(2,1)S(1)}, bf16[16,64,512]{2,1,0:T(8,128)(2,1)S(1)}, u32[]{:S(2)}, u32[]{:S(2)}) collective-permute-start(bf16[16,64,512]{2,1,0:T(8,128)(2,1)S(1)} %bitcast.16), channel_id=1, source_target_pairs={{0,1},{1,0},{2,3},{3,2},{4,5},{5,4},{6,7},{7,6},{8,9},{9,8},{10,11... | collective-permute-start | bytes 3145736 | tf_op jit(solution)/shard_map/ppermute | solution.py:192
  50.7 0.9 convolution_convert_fusion
  51.6 0.3 collective-permute-start
  52.5 0.0 copy-start.2
  52.5 1.1 copy-done.2
  53.7 1.4 prepare.1
  55.0 7.3 %collective-permute-done.halo_ref = bf16[128,512]{1,0:T(8,128)(2,1)S(1)} collective-permute-done((bf16[128,512]{1,0:T(8,128)(2,1)}, bf16[128,512]{1,0:T(8,128)(2,1)S(1)}, u32[]{:S(2)}, u32[]{:S(2)}) %collective-permute-start) | collective-permute-done | bytes 131104 | tf_op jit(solution)/shard_map/ppermute | solution.py:200
  62.3 0.0 collective-permute-done.1.other_ref
  62.3 0.0 copy-done.3
  62.4 5.2 %layer.1 = (bf16[256,512]{1,0:T(8,128)(2,1)}, f32[256,512]{1,0:T(8,128)S(1)}, bf16[128,512]{1,0:T(8,128)(2,1)S(1)}, bf16[16,64,768]{2,1,0:T(8,128)(2,1)S(1)}, bf16[16,64,768]{2,1,0:T(8,128)(2,1)S(1)}) custom-call(s32[1,24]{1,0:T(1,128)S(1)} %copy-done.8, s32[1]{0:T(128)} %bitcast.core_ref, bf16[256,512]{1,0:T(8,128)(2,1)S(1)} %copy-done, ...), custom_call_target="tpu_custom_call" | custom-call | tf_op jit(solution)/shard_map/layer/pallas_call | solution.py:170
  67.6 0.8 collective-permute-start.2
  68.4 0.0 collective-permute-start.3
  68.4 3.0 %collective-permute-done.2 = bf16[16,64,768]{2,1,0:T(8,128)(2,1)S(1)} collective-permute-done((bf16[16,64,768]{2,1,0:T(8,128)(2,1)S(1)}, bf16[16,64,768]{2,1,0:T(8,128)(2,1)S(1)}, u32[]{:S(2)}, u32[]{:S(2)}) %collective-permute-start.2) | collective-permute-done | bytes 1572896 | tf_op jit(solution)/shard_map/ppermute | solution.py:192
  71.4 0.5 add_convert_fusion
  72.0 1.6 %collective-permute-done.3 = bf16[128,512]{1,0:T(8,128)(2,1)S(1)} collective-permute-done((bf16[128,512]{1,0:T(8,128)(2,1)S(1)}, bf16[128,512]{1,0:T(8,128)(2,1)S(1)}, u32[]{:S(2)}, u32[]{:S(2)}) %collective-permute-start.3) | collective-permute-done | bytes 131104 | tf_op jit(solution)/shard_map/ppermute | solution.py:200
  73.5 50.6 %all_to_all.16 = bf16[128,8,768]{2,1,0:T(8,128)(2,1)S(1)} all-to-all(bf16[128,8,768]{2,1,0:T(8,128)(2,1)S(1)} %bitcast.18), channel_id=1, replica_groups=mesh['y'=4,'x'=4,'z'=8,'c'=2] {'y','x','z'}, dimensions={0} | all-to-all | bytes 3145728 | tf_op jit(solution)/shard_map/all_to_all | solution.py:204
  124.2 0.3 convert_reduce_fusion
  124.5 23.0 %all_to_all.17 = bf16[128,8,256]{2,1,0:T(8,128)(2,1)S(1)} all-to-all(bf16[128,8,256]{2,1,0:T(8,128)(2,1)S(1)} %broadcast_in_dim.5), channel_id=1, replica_groups=mesh['y'=4,'x'=4,'z'=8,'c'=2] {'y','x','z'}, dimensions={0} | all-to-all | bytes 1048576 | tf_op jit(solution)/shard_map/all_to_all | solution.py:204
  147.5 4.2 %collective-permute-start.4 = (bf16[128,8,256]{2,1,0:T(8,128)(2,1)S(1)}, bf16[128,8,256]{2,1,0:T(8,128)(2,1)S(1)}, u32[]{:S(2)}, u32[]{:S(2)}) collective-permute-start(bf16[128,8,256]{2,1,0:T(8,128)(2,1)S(1)} %all_to_all.17), channel_id=1, source_target_pairs={{0,1},{1,0},{2,3},{3,2},{4,5},{5,4},{6,7},{7,6},{8,9},{9,8},{10,11... | collective-permute-start | bytes 1572872 | tf_op jit(solution)/shard_map/ppermute | solution.py:192
  151.7 0.3 fusion
  152.0 0.0 copy-done.5
  152.0 0.9 add.7
  152.9 0.6 slice.8
  153.5 0.0 collective-permute-done.4
  153.5 0.1 broadcast_select_fusion
  153.6 1.1 convert.6
  154.7 1.1 convert.7
  (15 shorter events, 0.1 us)
Async XLA Ops:
  0.6 50.0 %copy-start = (bf16[256,512]{1,0:T(8,128)(2,1)S(1)}, bf16[256,512]{1,0:T(8,128)(2,1)}, u32[]{:S(2)}) copy-start(bf16[256,512]{1,0:T(8,128)(2,1)} %feat_ref.3) | copy-start | bytes 786436
  0.6 50.0 %copy-start.9 = (s32[1,128]{1,0:T(1,128)S(1)}, s32[1,128]{1,0:T(1,128)}, u32[]{:S(2)}) copy-start(s32[1,128]{1,0:T(1,128)} %param.16) | copy-start | bytes 1540
  0.7 51.9 %copy-start.7 = (s32[1,24]{1,0:T(1,128)S(1)}, s32[1,24]{1,0:T(1,128)}, u32[]{:S(2)}) copy-start(s32[1,24]{1,0:T(1,128)} %row_ref.1) | copy-start | bytes 292
  0.7 51.9 %copy-start.1 = (bf16[512,512]{1,0:T(8,128)(2,1)S(1)}, bf16[512,512]{1,0:T(8,128)(2,1)}, u32[]{:S(2)}) copy-start(bf16[512,512]{1,0:T(8,128)(2,1)} %ws_ref.3) | copy-start | bytes 1572868
  1.5 60.8 %copy-start.3 = (bf16[512,512]{1,0:T(8,128)(2,1)S(1)}, bf16[512,512]{1,0:T(8,128)(2,1)}, u32[]{:S(2)}) copy-start(bf16[512,512]{1,0:T(8,128)(2,1)} %wn_ref.1) | copy-start | bytes 1572868
  1.5 60.8 %copy-start.8 = (s32[1,24]{1,0:T(1,128)S(1)}, s32[1,24]{1,0:T(1,128)}, u32[]{:S(2)}) copy-start(s32[1,24]{1,0:T(1,128)} %col_ref.1) | copy-start | bytes 292
  48.0 14.3 %collective-permute-start.1 = (bf16[16,64,512]{2,1,0:T(8,128)(2,1)S(1)}, bf16[16,64,512]{2,1,0:T(8,128)(2,1)S(1)}, u32[]{:S(2)}, u32[]{:S(2)}) collective-permute-start(bf16[16,64,512]{2,1,0:T(8,128)(2,1)S(1)} %bitcast.16), channel_id=1, source_target_pairs={{0,1},{1,0},{2,3},{3,2},{4,5},{5,4},{6,7},{7,6},{8,9},{9,8},{10,11... | collective-permute-start | bytes 3145736 | tf_op jit(solution)/shard_map/ppermute | solution.py:192
  51.6 10.8 %collective-permute-start = (bf16[128,512]{1,0:T(8,128)(2,1)}, bf16[128,512]{1,0:T(8,128)(2,1)S(1)}, u32[]{:S(2)}, u32[]{:S(2)}) collective-permute-start(bf16[128,512]{1,0:T(8,128)(2,1)} %convolution_convert_fusion), channel_id=1, source_target_pairs={{0,2},{2,4},{4,6},{6,8},{8,10},{10,12},{12,14},{14,16},{16,18},{18... | collective-permute-start | bytes 393224 | tf_op jit(solution)/shard_map/ppermute | solution.py:200
  52.5 1.1 copy-start.2
  53.7 8.7 %copy-start.6 = (bf16[256,512]{1,0:T(8,128)(2,1)S(1)}, bf16[256,512]{1,0:T(8,128)(2,1)}, u32[]{:S(2)}) copy-start(bf16[256,512]{1,0:T(8,128)(2,1)} %og_ref.1) | copy-start | bytes 786436
  67.6 4.4 %copy-start.4 = (f32[256,512]{1,0:T(8,128)}, f32[256,512]{1,0:T(8,128)S(1)}, u32[]{:S(2)}) copy-start(f32[256,512]{1,0:T(8,128)S(1)} %get-tuple-element.21) | copy-start | bytes 1572868
  67.6 3.8 %collective-permute-start.2 = (bf16[16,64,768]{2,1,0:T(8,128)(2,1)S(1)}, bf16[16,64,768]{2,1,0:T(8,128)(2,1)S(1)}, u32[]{:S(2)}, u32[]{:S(2)}) collective-permute-start(bf16[16,64,768]{2,1,0:T(8,128)(2,1)S(1)} %get-tuple-element.23), channel_id=1, source_target_pairs={{0,1},{1,0},{2,3},{3,2},{4,5},{5,4},{6,7},{7,6},{8,9},{9,8},{10,11... | collective-permute-start | bytes 4718600 | tf_op jit(solution)/shard_map/ppermute | solution.py:192
  68.4 5.1 %collective-permute-start.3 = (bf16[128,512]{1,0:T(8,128)(2,1)S(1)}, bf16[128,512]{1,0:T(8,128)(2,1)S(1)}, u32[]{:S(2)}, u32[]{:S(2)}) collective-permute-start(bf16[128,512]{1,0:T(8,128)(2,1)S(1)} %get-tuple-element.24), channel_id=1, source_target_pairs={{0,254},{2,0},{4,2},{6,4},{8,6},{10,8},{12,10},{14,12},{16,14},{18... | collective-permute-start | bytes 393224 | tf_op jit(solution)/shard_map/ppermute | solution.py:200
  124.2 27.8 %copy-start.5 = (f32[256,512]{1,0:T(8,128)S(1)}, f32[256,512]{1,0:T(8,128)}, u32[]{:S(2)}) copy-start(f32[256,512]{1,0:T(8,128)} %copy-done.4) | copy-start | bytes 1572868
  147.5 6.0 %collective-permute-start.4 = (bf16[128,8,256]{2,1,0:T(8,128)(2,1)S(1)}, bf16[128,8,256]{2,1,0:T(8,128)(2,1)S(1)}, u32[]{:S(2)}, u32[]{:S(2)}) collective-permute-start(bf16[128,8,256]{2,1,0:T(8,128)(2,1)S(1)} %all_to_all.17), channel_id=1, source_target_pairs={{0,1},{1,0},{2,3},{3,2},{4,5},{5,4},{6,7},{7,6},{8,9},{9,8},{10,11... | collective-permute-start | bytes 1572872 | tf_op jit(solution)/shard_map/ppermute | solution.py:192

commit v4 on v3

--- a/solution.py
+++ b/solution.py
@@ -17,6 +17,7 @@
 BF16 = jnp.bfloat16
 ALL = ("y", "x", "z", "c")
 CHIPS = ("y", "x", "z")
+PLANE = ("y", "x")
 
 
 def dot(a, b, contract=((1,), (0,))):
@@ -75,7 +76,6 @@
     first_hub = ROW_BLOCKS + 1
     low_core = core_ref[0] == 0
     weight_rows = D // hub_tiles
-    half = D * weight_rows // column_rows
 
     table[:LOCAL_ROWS] = feat_ref[...]
     table[LOCAL_ROWS : LOCAL_ROWS + TILE] = halo_ref[...]
@@ -118,23 +118,18 @@
         grads = acc[pl.ds(start, TILE)]
         low = jnp.concatenate([grads[at : at + OWN] for at in range(0, TILE, 2 * OWN)], 0)
         high = jnp.concatenate([grads[at + OWN : at + 2 * OWN] for at in range(0, TILE, 2 * OWN)], 0)
-        keep_ref[t, :, :D] = jnp.where(low_core, low, high).astype(BF16)
-        send_ref[t, :, :D] = jnp.where(low_core, high, low).astype(BF16)
+        keep_ref[t, :column_rows] = jnp.where(low_core, low, high).astype(BF16)
+        send_ref[t, :column_rows] = jnp.where(low_core, high, low).astype(BF16)
         return carry
 
     lax.fori_loop(0, hub_tiles, ship, 0)
 
     grad_self_w = dot(own, grad_pre, ((0,), (0,)))
     grad_neigh_w = dot(aggregate, grad_pre, ((0,), (0,)))
-    keep = jnp.where(low_core, grad_self_w, grad_neigh_w)
-    send = jnp.where(low_core, grad_neigh_w, grad_self_w)
-    for t in range(hub_tiles):
-        for value, ref in ((keep, keep_ref), (send, send_ref)):
-            pieces = []
-            for z in range(column_rows // OWN):
-                row = t * weight_rows + (z // 2) * OWN
-                pieces.append(value[row : row + OWN, (z % 2) * half : (z % 2 + 1) * half])
-            ref[t, :, D:] = jnp.concatenate(pieces, 0).astype(BF16)
+    keep = jnp.where(low_core, grad_self_w, grad_neigh_w).astype(BF16)
+    send = jnp.where(low_core, grad_neigh_w, grad_self_w).astype(BF16)
+    keep_ref[:, column_rows:] = keep.reshape(hub_tiles, weight_rows, D)
+    send_ref[:, column_rows:] = send.reshape(hub_tiles, weight_rows, D)
     base_ref[...] = dot(grad_pre, ws_ref[...], ((1,), (1,))) + acc[:LOCAL_ROWS]
     back_ref[...] = acc[LOCAL_ROWS : LOCAL_ROWS + TILE].astype(BF16)
 
@@ -166,7 +161,7 @@
 def layer(cols, core, feat, halo, mine, other, wide, flip, norm, pre, ws, wn, og):
     hub_tiles, column_rows, _ = mine.shape
     sources = (ROW_BLOCKS + 1 + hub_tiles) * TILE
-    parcel = jax.ShapeDtypeStruct((hub_tiles, column_rows, D + D * D // hub_tiles // column_rows), BF16)
+    parcel = jax.ShapeDtypeStruct((hub_tiles, column_rows + D // hub_tiles, D), BF16)
     return pl.pallas_call(
         layer_kernel,
         out_shape=(
@@ -200,12 +195,13 @@
     return lax.ppermute(value, CHIPS, pairs)
 
 
-def exchange(value):
-    return lax.all_to_all(value, CHIPS, 0, 0, tiled=True)
-
-
-def spread(value, count):
-    return exchange(jnp.broadcast_to(value[None], (count,) + value.shape))
+def exchange(value, axes):
+    return lax.all_to_all(value, axes, 0, 0, tiled=True)
+
+
+def spread(value, axes):
+    count = math.prod(lax.axis_size(axis) for axis in axes)
+    return exchange(jnp.broadcast_to(value[None], (count,) + value.shape), axes)
 
 
 def per_device(
@@ -226,8 +222,10 @@
     core = lax.axis_index("c").astype(jnp.int32)
     picks = halo_send[0]
     chosen = (picks[:, None] == jnp.arange(LOCAL_ROWS, dtype=jnp.int32)[None, :]).astype(BF16)
-    mine = spread(hub_feat, chips).reshape(planes, zs * OWN, D)
     halo = ring_shift(dot(chosen, features).astype(BF16), 1)
+    column = spread(hub_feat, ("z",)).reshape(zs * OWN, D)
+    column, halo = lax.optimization_barrier((column, halo))
+    mine = spread(column, PLANE)
     wide, flip, norm, pre = prepare(block_count, block_row, adjacency, features, w_self)
     other = swap_cores(mine)
     activations, base, back, keep, send = layer(
@@ -247,20 +245,22 @@
     )
     returned = ring_shift(back, -1)
     chip = (keep.astype(F32) + swap_cores(send).astype(F32)).astype(BF16)
-    chip, returned = lax.optimization_barrier((chip, returned))
-    total = jnp.sum(exchange(chip.reshape(chips, OWN, -1)).astype(F32), 0)
+    plane = jnp.sum(exchange(chip, PLANE).astype(F32), 0).astype(BF16)
+    plane, returned = lax.optimization_barrier((plane, returned))
+    column_rows = zs * OWN
+    hub_part = plane[:column_rows].reshape(zs, OWN, D)
+    weight_part = plane[column_rows:]
+    packed = jnp.concatenate(
+        [hub_part, jnp.broadcast_to(weight_part[None], (zs,) + weight_part.shape)], 1
+    )
+    total = jnp.sum(exchange(packed, ("z",)).astype(F32), 0)
     factor = 1.0 / math.sqrt(LOCAL_ROWS * 2 * chips)
-    weight_mine = spread((total[:, D:] * factor).astype(BF16), chips)
+    weight_mine = spread((total[OWN:] * factor).astype(BF16), PLANE).reshape(D, D)
     weight_other = swap_cores(weight_mine)
-
-    def unpack(value):
-        rows = value.reshape(chips // 2, 2, OWN, -1)
-        return jnp.transpose(rows, (0, 2, 1, 3)).reshape(D, D).astype(F32)
-
-    grad_w_self = unpack(jnp.where(core == 0, weight_mine, weight_other))
-    grad_w_neigh = unpack(jnp.where(core == 0, weight_other, weight_mine))
+    grad_w_self = jnp.where(core == 0, weight_mine, weight_other).astype(F32)
+    grad_w_neigh = jnp.where(core == 0, weight_other, weight_mine).astype(F32)
     grad_features = base + dot(chosen, returned, ((0,), (0,)))
-    return (activations, grad_features, total[:, :D], grad_w_self, grad_w_neigh)
+    return (activations, grad_features, total[:OWN], grad_w_self, grad_w_neigh)
 
 
 def solution(mesh):

time: 156 us -> 125 us (0.80)
  blocking collectives: 120 us -> 63.3 us
  waiting for transfers between devices: 11.9 us -> 25.4 us
  starting transfers between devices: 7.94 us -> 17.2 us
    all_to_all x3 -> x4, blocking collectives: 120 us -> 63.3 us  [exchange(): return lax.all_to_all(value, axes, 0, 0, tiled=True)]
    all_to_all x0 -> x1, waiting for transfers between devices: none -> 22 us  [exchange(): return lax.all_to_all(value, axes, 0, 0, tiled=True)]
    ppermute x2, waiting for transfers between devices: 8.86 us -> 0.01 us  [ring_shift(): return lax.ppermute(value, CHIPS, pairs)]
    ppermute x2, starting transfers between devices: 0.29 us -> 6.98 us  [ring_shift(): return lax.ppermute(value, CHIPS, pairs)]
    all_to_all x0 -> x1, starting transfers between devices: none -> 3.84 us  [exchange(): return lax.all_to_all(value, axes, 0, 0, tiled=True)]
  transfers between devices with their start and end apart: 5 -> 6, of which waited for: 3 -> 2; matrix products, arithmetic and copies ran while one was open for 2% -> 2% of each run, Pallas kernels for 1% -> 1%
where the time goes in v4:
time: 125 us; the launch traced here: 124 us
  blocking collectives  63.3 us (51%)
  waiting for transfers between devices  25.4 us (20%)
  starting transfers between devices  17.2 us (14%)
  Pallas kernels  6.63 us (5%)
  other arithmetic  4.36 us (3%)
  local copies, waits for them, and re-layouts  4.09 us (3%)
  matrix products  1.52 us (1%)
  between operations  1.51 us (1%)
    all_to_all x4, blocking collectives, exchange(): return lax.all_to_all(value, axes, 0, 0, tiled=True)  63.3 us
    all_to_all x1, waiting for transfers between devices, exchange(): return lax.all_to_all(value, axes, 0, 0, tiled=True)  22 us
    ppermute x2, starting transfers between devices, ring_shift(): return lax.ppermute(value, CHIPS, pairs)  6.98 us
    ppermute x3, starting transfers between devices, swap_cores(): return lax.ppermute(value, 'c', [(0, 1), (1, 0)])  6.4 us
    pallas_call x1, Pallas kernels, layer(): pl.pallas_call(layer_kernel, out_shape=(jax.ShapeDtypeStruct((LOCAL_ROWS,...  5.26 us
    all_to_all x1, starting transfers between devices, exchange(): return lax.all_to_all(value, axes, 0, 0, tiled=True)  3.84 us
    ppermute x3, waiting for transfers between devices, swap_cores(): return lax.ppermute(value, 'c', [(0, 1), (1, 0)])  3.41 us
    unnamed x24, local copies, waits for them, and re-layouts  2.62 us
  transfers between devices with their start and end apart: 6, of which 2 were waited for; matrix products, arithmetic and copies ran while one was open for 2% of the time, Pallas kernels for 1%

profile of v4, /device:TPU:1, one launch (start us, length us, event | category | flops | bytes accessed | tf_op | source)
XLA Modules:
  0.0 124.1 jit_solution(7474063710173555651)
XLA Ops:
  0.6 1.2 convolution_convert_fusion
  1.8 2.5 %collective-permute-start = (bf16[128,512]{1,0:T(8,128)(2,1)S(1)}, bf16[128,512]{1,0:T(8,128)(2,1)S(1)}, u32[]{:S(2)}, u32[]{:S(2)}) collective-permute-start(bf16[128,512]{1,0:T(8,128)(2,1)S(1)} %convolution_convert_fusion), channel_id=1, source_target_pairs={{0,2},{2,4},{4,6},{6,8},{8,10},{10,12},{12,14},{14,16},{16,18},{18... | collective-permute-start | bytes 393224 | tf_op jit(solution)/shard_map/ppermute | solution.py:195
  4.4 0.7 broadcast_in_dim.8
  5.1 14.3 %all_to_all.25 = bf16[8,8,512]{2,1,0:T(8,128)(2,1)S(1)} all-to-all(bf16[8,8,512]{2,1,0:T(8,128)(2,1)S(1)} %broadcast_in_dim.8), channel_id=1, replica_groups=mesh['y'=4,'x'=4,'z'=8,'c'=2] {'z'}, dimensions={0} | all-to-all | bytes 131072 | tf_op jit(solution)/shard_map/all_to_all | solution.py:199
  19.4 0.0 collective-permute-done.halo_ref
  19.4 0.1 broadcast_in_dim.9
  19.5 0.0 copy-start.3
  19.5 0.0 copy-start.8
  19.5 21.3 %all_to_all.26.mine_ref = bf16[16,64,512]{2,1,0:T(8,128)(2,1)S(1)} all-to-all(bf16[16,64,512]{2,1,0:T(8,128)(2,1)S(1)} %broadcast_in_dim.9), channel_id=1, replica_groups=mesh['y'=4,'x'=4,'z'=8,'c'=2] {'y','x'}, dimensions={0} | all-to-all | bytes 2097152 | tf_op jit(solution)/shard_map/all_to_all | solution.py:199
  40.8 3.6 %collective-permute-start.1 = (bf16[16,64,512]{2,1,0:T(8,128)(2,1)S(1)}, bf16[16,64,512]{2,1,0:T(8,128)(2,1)S(1)}, u32[]{:S(2)}, u32[]{:S(2)}) collective-permute-start(bf16[16,64,512]{2,1,0:T(8,128)(2,1)S(1)} %all_to_all.26.mine_ref), channel_id=1, source_target_pairs={{0,1},{1,0},{2,3},{3,2},{4,5},{5,4},{6,7},{7,6},{8,9},{9,8},{10,11... | collective-permute-start | bytes 3145736 | tf_op jit(solution)/shard_map/ppermute | solution.py:187
  45.1 0.0 copy-start.2
  45.1 1.1 copy-done.2
  46.2 1.4 %prepare.1 = (bf16[256,3072]{1,0:T(8,128)(2,1)S(1)}, bf16[3072,256]{1,0:T(8,128)(2,1)S(1)}, f32[256,128]{1,0:T(8,128)S(1)}, f32[256,512]{1,0:T(8,128)S(1)}) custom-call(s32[1]{0:T(128)S(6)} %copy.15.count_ref, s32[1,24]{1,0:T(1,128)S(1)} %copy-done.7, bf16[24,128,128]{2,1,0:T(8,128)(2,1)S(1)} %copy-done.2, bf16[256,512]{1,0:T(8,128)(2,1)S(1)} %copy-done, ...), custom_call_target="tpu_custom_call" | custom-call | flops 134217728 | bytes 5242880 | tf_op jit(solution)/shard_map/prepare/pallas_call | solution.py:143
  47.6 0.0 collective-permute-done.1.other_ref
  47.6 5.3 %layer.1 = (bf16[256,512]{1,0:T(8,128)(2,1)}, f32[256,512]{1,0:T(8,128)S(1)}, bf16[128,512]{1,0:T(8,128)(2,1)S(1)}, bf16[16,96,512]{2,1,0:T(8,128)(2,1)S(1)}, bf16[16,96,512]{2,1,0:T(8,128)(2,1)S(1)}) custom-call(s32[1,24]{1,0:T(1,128)S(1)} %copy-done.8, s32[1]{0:T(128)} %bitcast.core_ref, bf16[256,512]{1,0:T(8,128)(2,1)S(1)} %copy-done, ...), custom_call_target="tpu_custom_call" | custom-call | tf_op jit(solution)/shard_map/layer/pallas_call | solution.py:165
  52.9 0.8 copy-done.4
  53.7 0.7 copy-done.9
  54.4 3.4 %collective-permute-done.2 = bf16[16,96,512]{2,1,0:T(8,128)(2,1)S(1)} collective-permute-done((bf16[16,96,512]{2,1,0:T(8,128)(2,1)S(1)}, bf16[16,96,512]{2,1,0:T(8,128)(2,1)S(1)}, u32[]{:S(2)}, u32[]{:S(2)}) %collective-permute-start.2) | collective-permute-done | bytes 1572896 | tf_op jit(solution)/shard_map/ppermute | solution.py:187
  57.8 1.7 %add_convert_fusion = bf16[16,96,512]{2,1,0:T(8,128)(2,1)} fusion(bf16[16,96,512]{2,1,0:T(8,128)(2,1)S(1)} %collective-permute-done.2, bf16[16,96,512]{2,1,0:T(8,128)(2,1)S(1)} %get-tuple-element.26), kind=kLoop, calls=%fused_computation | loop fusion | flops 3145728 | bytes 4718592 | tf_op jit(solution)/shard_map/convert_element_type | solution.py:247
  59.5 3.8 %all-to-all-start.2 = ((bf16[16,96,512]{2,1,0:T(8,128)(2,1)}), bf16[16,96,512]{2,1,0:T(8,128)(2,1)S(1)}, u32[]{:S(2)}, u32[]{:S(2)}) async-start(bf16[16,96,512]{2,1,0:T(8,128)(2,1)} %add_convert_fusion), calls=%async_computation.2 | async-start | bytes 3145728 | tf_op jit(solution)/shard_map/all_to_all | solution.py:199
  63.3 4.4 %collective-permute-start.3 = (bf16[128,512]{1,0:T(8,128)(2,1)S(1)}, bf16[128,512]{1,0:T(8,128)(2,1)S(1)}, u32[]{:S(2)}, u32[]{:S(2)}) collective-permute-start(bf16[128,512]{1,0:T(8,128)(2,1)S(1)} %copy-done.10), channel_id=1, source_target_pairs={{0,254},{2,0},{4,2},{6,4},{8,6},{10,8},{12,10},{14,12},{16,14},{18... | collective-permute-start | bytes 393224 | tf_op jit(solution)/shard_map/ppermute | solution.py:195
  67.7 22.0 %all-to-all-done.2 = bf16[16,96,512]{2,1,0:T(8,128)(2,1)S(1)} async-done(((bf16[16,96,512]{2,1,0:T(8,128)(2,1)}), bf16[16,96,512]{2,1,0:T(8,128)(2,1)S(1)}, u32[]{:S(2)}, u32[]{:S(2)}) %all-to-all-start.2) | async-done | bytes 1572896 | tf_op jit(solution)/shard_map/all_to_all | solution.py:199
  89.7 0.2 reduce_sum.21
  90.0 0.0 copy-start.11
  90.1 0.0 copy-start.5
  90.1 14.2 %all_to_all.27 = bf16[8,40,512]{2,1,0:T(8,128)(2,1)S(1)} all-to-all(bf16[8,40,512]{2,1,0:T(8,128)(2,1)S(1)} %pad_maximum_fusion), channel_id=1, replica_groups=mesh['y'=4,'x'=4,'z'=8,'c'=2] {'z'}, dimensions={0} | all-to-all | bytes 655360 | tf_op jit(solution)/shard_map/all_to_all | solution.py:199
  104.4 13.5 %all_to_all.28 = bf16[16,32,512]{2,1,0:T(8,128)(2,1)S(1)} all-to-all(bf16[16,32,512]{2,1,0:T(8,128)(2,1)S(1)} %broadcast_in_dim.11), channel_id=1, replica_groups=mesh['y'=4,'x'=4,'z'=8,'c'=2] {'y','x'}, dimensions={0} | all-to-all | bytes 1048576 | tf_op jit(solution)/shard_map/all_to_all | solution.py:199
  117.9 2.8 %collective-permute-start.4 = (bf16[512,512]{1,0:T(8,128)(2,1)S(1)}, bf16[512,512]{1,0:T(8,128)(2,1)S(1)}, u32[]{:S(2)}, u32[]{:S(2)}) collective-permute-start(bf16[512,512]{1,0:T(8,128)(2,1)S(1)} %bitcast.10), channel_id=1, source_target_pairs={{0,1},{1,0},{2,3},{3,2},{4,5},{5,4},{6,7},{7,6},{8,9},{9,8},{10,11... | collective-permute-start | bytes 1572872 | tf_op jit(solution)/shard_map/ppermute | solution.py:187
  120.7 0.3 fusion
  121.1 0.9 add.7
  122.0 0.6 slice.16
  122.6 1.5 %select_convert_fusion = (f32[512,512]{1,0:T(8,128)}, f32[512,512]{1,0:T(8,128)}) fusion(bf16[512,512]{1,0:T(8,128)(2,1)S(1)} %collective-permute-done.4, pred[]{:T(512)S(6)} %eq.23, bf16[16,32,512]{2,1,0:T(8,128)(2,1)S(1)} %all_to_all.28), kind=kLoop, calls=%fused_computation.3 | loop fusion | flops 1048576 | bytes 3145729 | tf_op jit(solution)/shard_map/convert_element_type | solution.py:261
  (26 shorter events, 0.2 us)
Async XLA Ops:
  1.8 17.5 %collective-permute-start = (bf16[128,512]{1,0:T(8,128)(2,1)S(1)}, bf16[128,512]{1,0:T(8,128)(2,1)S(1)}, u32[]{:S(2)}, u32[]{:S(2)}) collective-permute-start(bf16[128,512]{1,0:T(8,128)(2,1)S(1)} %convolution_convert_fusion), channel_id=1, source_target_pairs={{0,2},{2,4},{4,6},{6,8},{8,10},{10,12},{12,14},{14,16},{16,18},{18... | collective-permute-start | bytes 393224 | tf_op jit(solution)/shard_map/ppermute | solution.py:195
  19.4 25.7 %copy-start = (bf16[256,512]{1,0:T(8,128)(2,1)S(1)}, bf16[256,512]{1,0:T(8,128)(2,1)}, u32[]{:S(2)}) copy-start(bf16[256,512]{1,0:T(8,128)(2,1)} %feat_ref.3) | copy-start | bytes 786436
  19.4 25.7 %copy-start.1 = (bf16[512,512]{1,0:T(8,128)(2,1)S(1)}, bf16[512,512]{1,0:T(8,128)(2,1)}, u32[]{:S(2)}) copy-start(bf16[512,512]{1,0:T(8,128)(2,1)} %ws_ref.3) | copy-start | bytes 1572868
  19.4 25.7 %copy-start.7 = (s32[1,24]{1,0:T(1,128)S(1)}, s32[1,24]{1,0:T(1,128)}, u32[]{:S(2)}) copy-start(s32[1,24]{1,0:T(1,128)} %row_ref.1) | copy-start | bytes 292
  19.5 28.1 %copy-start.3 = (bf16[512,512]{1,0:T(8,128)(2,1)S(1)}, bf16[512,512]{1,0:T(8,128)(2,1)}, u32[]{:S(2)}) copy-start(bf16[512,512]{1,0:T(8,128)(2,1)} %wn_ref.1) | copy-start | bytes 1572868
  19.5 28.1 %copy-start.8 = (s32[1,24]{1,0:T(1,128)S(1)}, s32[1,24]{1,0:T(1,128)}, u32[]{:S(2)}) copy-start(s32[1,24]{1,0:T(1,128)} %col_ref.1) | copy-start | bytes 292
  40.8 6.8 %collective-permute-start.1 = (bf16[16,64,512]{2,1,0:T(8,128)(2,1)S(1)}, bf16[16,64,512]{2,1,0:T(8,128)(2,1)S(1)}, u32[]{:S(2)}, u32[]{:S(2)}) collective-permute-start(bf16[16,64,512]{2,1,0:T(8,128)(2,1)S(1)} %all_to_all.26.mine_ref), channel_id=1, source_target_pairs={{0,1},{1,0},{2,3},{3,2},{4,5},{5,4},{6,7},{7,6},{8,9},{9,8},{10,11... | collective-permute-start | bytes 3145736 | tf_op jit(solution)/shard_map/ppermute | solution.py:187
  45.1 1.1 copy-start.2
  46.2 1.4 %copy-start.6 = (bf16[256,512]{1,0:T(8,128)(2,1)S(1)}, bf16[256,512]{1,0:T(8,128)(2,1)}, u32[]{:S(2)}) copy-start(bf16[256,512]{1,0:T(8,128)(2,1)} %og_ref.1) | copy-start | bytes 786436
  52.9 0.8 copy-start.4
  53.7 0.7 copy-start.9
  54.3 3.4 %collective-permute-start.2 = (bf16[16,96,512]{2,1,0:T(8,128)(2,1)S(1)}, bf16[16,96,512]{2,1,0:T(8,128)(2,1)S(1)}, u32[]{:S(2)}, u32[]{:S(2)}) collective-permute-start(bf16[16,96,512]{2,1,0:T(8,128)(2,1)S(1)} %get-tuple-element.27), channel_id=1, source_target_pairs={{0,1},{1,0},{2,3},{3,2},{4,5},{5,4},{6,7},{7,6},{8,9},{9,8},{10,11... | collective-permute-start | bytes 4718600 | tf_op jit(solution)/shard_map/ppermute | solution.py:187
  59.4 3.9 %copy-start.10 = (bf16[128,512]{1,0:T(8,128)(2,1)S(1)}, bf16[128,512]{1,0:T(8,128)(2,1)}, u32[]{:S(2)}) copy-start(bf16[128,512]{1,0:T(8,128)(2,1)} %copy-done.9) | copy-start | bytes 393220
  59.5 30.3 %all-to-all-start.2 = ((bf16[16,96,512]{2,1,0:T(8,128)(2,1)}), bf16[16,96,512]{2,1,0:T(8,128)(2,1)S(1)}, u32[]{:S(2)}, u32[]{:S(2)}) async-start(bf16[16,96,512]{2,1,0:T(8,128)(2,1)} %add_convert_fusion), calls=%async_computation.2 | async-start | bytes 3145728 | tf_op jit(solution)/shard_map/all_to_all | solution.py:199
  63.3 26.6 %collective-permute-start.3 = (bf16[128,512]{1,0:T(8,128)(2,1)S(1)}, bf16[128,512]{1,0:T(8,128)(2,1)S(1)}, u32[]{:S(2)}, u32[]{:S(2)}) collective-permute-start(bf16[128,512]{1,0:T(8,128)(2,1)S(1)} %copy-done.10), channel_id=1, source_target_pairs={{0,254},{2,0},{4,2},{6,4},{8,6},{10,8},{12,10},{14,12},{16,14},{18... | collective-permute-start | bytes 393224 | tf_op jit(solution)/shard_map/ppermute | solution.py:195
  90.0 30.7 %copy-start.11 = (s32[1,128]{1,0:T(1,128)S(1)}, s32[1,128]{1,0:T(1,128)}, u32[]{:S(2)}) copy-start(s32[1,128]{1,0:T(1,128)} %param.16) | copy-start | bytes 1540
  90.1 31.0 %copy-start.5 = (f32[256,512]{1,0:T(8,128)S(1)}, f32[256,512]{1,0:T(8,128)}, u32[]{:S(2)}) copy-start(f32[256,512]{1,0:T(8,128)} %copy-done.4) | copy-start | bytes 1572868
  117.9 4.7 %collective-permute-start.4 = (bf16[512,512]{1,0:T(8,128)(2,1)S(1)}, bf16[512,512]{1,0:T(8,128)(2,1)S(1)}, u32[]{:S(2)}, u32[]{:S(2)}) collective-permute-start(bf16[512,512]{1,0:T(8,128)(2,1)S(1)} %bitcast.10), channel_id=1, source_target_pairs={{0,1},{1,0},{2,3},{3,2},{4,5},{5,4},{6,7},{7,6},{8,9},{9,8},{10,11... | collective-permute-start | bytes 1572872 | tf_op jit(solution)/shard_map/ppermute | solution.py:187

commit v5 on v4

--- a/solution.py
+++ b/solution.py
@@ -48,7 +48,7 @@
     pre_ref[...] = dot(feat_ref[...], ws_ref[...])
 
 
-def layer_kernel(
+def forward_kernel(
     col_ref,
     core_ref,
     feat_ref,
@@ -59,14 +59,13 @@
     flip_ref,
     norm_ref,
     pre_ref,
-    ws_ref,
     wn_ref,
     og_ref,
     act_ref,
-    base_ref,
+    agg_ref,
+    grad_pre_ref,
+    grad_agg_ref,
     back_ref,
-    keep_ref,
-    send_ref,
     table,
     gathered,
     acc,
@@ -75,7 +74,6 @@
     hub_tiles, column_rows, _ = mine_ref.shape
     first_hub = ROW_BLOCKS + 1
     low_core = core_ref[0] == 0
-    weight_rows = D // hub_tiles
 
     table[:LOCAL_ROWS] = feat_ref[...]
     table[LOCAL_ROWS : LOCAL_ROWS + TILE] = halo_ref[...]
@@ -101,17 +99,50 @@
     norm = jnp.concatenate([norm_ref[...]] * (D // TILE), 1)
     summed = dot(wide_ref[...], gathered[...])
     aggregate = (summed * norm).astype(BF16)
-    own = feat_ref[...]
+    agg_ref[...] = aggregate
     preact = pre_ref[...] + dot(aggregate, wn_ref[...])
     gate = jax.nn.sigmoid(preact)
     act_ref[...] = (preact * gate).astype(BF16)
     grad_pre = (og_ref[...].astype(F32) * gate * (1.0 + preact * (1.0 - gate))).astype(BF16)
+    grad_pre_ref[...] = grad_pre
     grad_agg = (dot(grad_pre, wn_ref[...], ((1,), (1,))) * norm).astype(BF16)
+    grad_agg_ref[...] = grad_agg
+
+    acc[...] = jnp.zeros_like(acc)
+    for s in range(slots):
+
+        @pl.when(col_ref[0, s] == ROW_BLOCKS)
+        def _(s=s):
+            acc[...] += dot(flip_ref[s * TILE : (s + 1) * TILE], grad_agg_ref[...])
+
+    back_ref[...] = acc[...].astype(BF16)
+
+
+def backward_kernel(
+    col_ref,
+    core_ref,
+    feat_ref,
+    flip_ref,
+    agg_ref,
+    grad_pre_ref,
+    grad_agg_ref,
+    ws_ref,
+    base_ref,
+    keep_ref,
+    send_ref,
+    acc,
+):
+    slots = flip_ref.shape[0] // TILE
+    hub_tiles, parcel_rows, _ = keep_ref.shape
+    weight_rows = D // hub_tiles
+    column_rows = parcel_rows - weight_rows
+    first_hub = ROW_BLOCKS + 1
+    low_core = core_ref[0] == 0
 
     acc[...] = jnp.zeros_like(acc)
     for s in range(slots):
         into = pl.ds(pl.multiple_of(col_ref[0, s] * TILE, TILE), TILE)
-        acc[into] += dot(flip_ref[s * TILE : (s + 1) * TILE], grad_agg)
+        acc[into] += dot(flip_ref[s * TILE : (s + 1) * TILE], grad_agg_ref[...])
 
     def ship(t, carry):
         start = pl.multiple_of((first_hub + t) * TILE, TILE)
@@ -124,14 +155,14 @@
 
     lax.fori_loop(0, hub_tiles, ship, 0)
 
-    grad_self_w = dot(own, grad_pre, ((0,), (0,)))
-    grad_neigh_w = dot(aggregate, grad_pre, ((0,), (0,)))
+    grad_pre = grad_pre_ref[...]
+    grad_self_w = dot(feat_ref[...], grad_pre, ((0,), (0,)))
+    grad_neigh_w = dot(agg_ref[...], grad_pre, ((0,), (0,)))
     keep = jnp.where(low_core, grad_self_w, grad_neigh_w).astype(BF16)
     send = jnp.where(low_core, grad_neigh_w, grad_self_w).astype(BF16)
     keep_ref[:, column_rows:] = keep.reshape(hub_tiles, weight_rows, D)
     send_ref[:, column_rows:] = send.reshape(hub_tiles, weight_rows, D)
     base_ref[...] = dot(grad_pre, ws_ref[...], ((1,), (1,))) + acc[:LOCAL_ROWS]
-    back_ref[...] = acc[LOCAL_ROWS : LOCAL_ROWS + TILE].astype(BF16)
 
 
 SMEM = pl.BlockSpec(memory_space=pltpu.SMEM)
@@ -158,29 +189,37 @@
     )(count, rows, adj, feat, ws)
 
 
-def layer(cols, core, feat, halo, mine, other, wide, flip, norm, pre, ws, wn, og):
-    hub_tiles, column_rows, _ = mine.shape
+def forward(cols, core, feat, halo, mine, other, wide, flip, norm, pre, wn, og):
+    hub_tiles = mine.shape[0]
     sources = (ROW_BLOCKS + 1 + hub_tiles) * TILE
-    parcel = jax.ShapeDtypeStruct((hub_tiles, column_rows + D // hub_tiles, D), BF16)
+    local = jax.ShapeDtypeStruct((LOCAL_ROWS, D), BF16)
     return pl.pallas_call(
-        layer_kernel,
-        out_shape=(
-            jax.ShapeDtypeStruct((LOCAL_ROWS, D), BF16),
-            jax.ShapeDtypeStruct((LOCAL_ROWS, D), F32),
-            jax.ShapeDtypeStruct((TILE, D), BF16),
-            parcel,
-            parcel,
-        ),
-        in_specs=[SMEM] * 2 + [VMEM] * 11,
+        forward_kernel,
+        out_shape=(local, local, local, local, jax.ShapeDtypeStruct((TILE, D), BF16)),
+        in_specs=[SMEM] * 2 + [VMEM] * 10,
         out_specs=(VMEM,) * 5,
         scratch_shapes=[
             pltpu.VMEM((sources, D), BF16),
             pltpu.VMEM((wide.shape[1], D), BF16),
-            pltpu.VMEM((sources, D), F32),
+            pltpu.VMEM((TILE, D), F32),
         ],
-        compiler_params=pltpu.CompilerParams(vmem_limit_bytes=32 * 1024 * 1024),
-        name="layer",
-    )(cols, core, feat, halo, mine, other, wide, flip, norm, pre, ws, wn, og)
+        compiler_params=pltpu.CompilerParams(vmem_limit_bytes=16 * 1024 * 1024),
+        name="forward",
+    )(cols, core, feat, halo, mine, other, wide, flip, norm, pre, wn, og)
+
+
+def backward(cols, core, feat, flip, agg, grad_pre, grad_agg, ws, hub_tiles, column_rows):
+    sources = (ROW_BLOCKS + 1 + hub_tiles) * TILE
+    parcel = jax.ShapeDtypeStruct((hub_tiles, column_rows + D // hub_tiles, D), BF16)
+    return pl.pallas_call(
+        backward_kernel,
+        out_shape=(jax.ShapeDtypeStruct((LOCAL_ROWS, D), F32), parcel, parcel),
+        in_specs=[SMEM] * 2 + [VMEM] * 6,
+        out_specs=(VMEM,) * 3,
+        scratch_shapes=[pltpu.VMEM((sources, D), F32)],
+        compiler_params=pltpu.CompilerParams(vmem_limit_bytes=16 * 1024 * 1024),
+        name="backward",
+    )(cols, core, feat, flip, agg, grad_pre, grad_agg, ws)
 
 
 def swap_cores(value):
@@ -228,9 +267,10 @@
     mine = spread(column, PLANE)
     wide, flip, norm, pre = prepare(block_count, block_row, adjacency, features, w_self)
     other = swap_cores(mine)
-    activations, base, back, keep, send = layer(
+    scalar = core.reshape(1)
+    activations, aggregate, grad_pre, grad_agg, back = forward(
         block_col,
-        core.reshape(1),
+        scalar,
         features,
         halo,
         mine,
@@ -239,14 +279,24 @@
         flip,
         norm,
         pre,
-        w_self,
         w_neigh,
         out_grad,
     )
     returned = ring_shift(back, -1)
+    base, keep, send = backward(
+        block_col,
+        scalar,
+        features,
+        flip,
+        aggregate,
+        grad_pre,
+        grad_agg,
+        w_self,
+        planes,
+        zs * OWN,
+    )
     chip = (keep.astype(F32) + swap_cores(send).astype(F32)).astype(BF16)
     plane = jnp.sum(exchange(chip, PLANE).astype(F32), 0).astype(BF16)
-    plane, returned = lax.optimization_barrier((plane, returned))
     column_rows = zs * OWN
     hub_part = plane[:column_rows].reshape(zs, OWN, D)
     weight_part = plane[column_rows:]
@@ -256,6 +306,7 @@
     total = jnp.sum(exchange(packed, ("z",)).astype(F32), 0)
     factor = 1.0 / math.sqrt(LOCAL_ROWS * 2 * chips)
     weight_mine = spread((total[OWN:] * factor).astype(BF16), PLANE).reshape(D, D)
+    weight_mine, returned = lax.optimization_barrier((weight_mine, returned))
     weight_other = swap_cores(weight_mine)
     grad_w_self = jnp.where(core == 0, weight_mine, weight_other).astype(F32)
     grad_w_neigh = jnp.where(core == 0, weight_other, weight_mine).astype(F32)

time: 125 us -> 120 us (0.960)
  waiting for transfers between devices: 25.4 us -> 8.63 us
  blocking collectives: 63.3 us -> 74.6 us
  Pallas kernels: 6.63 us -> 8.04 us
    all_to_all x1, waiting for transfers between devices: 22 us -> 3.64 us  [exchange(): return lax.all_to_all(value, axes, 0, 0, tiled=True)]
    all_to_all x4, blocking collectives: 63.3 us -> 74.6 us  [exchange(): return lax.all_to_all(value, axes, 0, 0, tiled=True)]
    ppermute x2, waiting for transfers between devices: 0.01 us -> 1.95 us  [ring_shift(): return lax.ppermute(value, CHIPS, pairs)]
    unnamed x24 -> x20, local copies, waits for them, and re-layouts: 2.62 us -> 1.17 us
    pallas_call x1 -> x2, Pallas kernels: 5.26 us -> 6.66 us  [the longest x1 3.81 us: forward(): pl.pallas_call(forward_kernel, out_shape=(local, local, local, local, jax...]
  transfers between devices with their start and end apart: 6 -> 6, of which waited for: 2 -> 3; matrix products, arithmetic and copies ran while one was open for 2% -> 2% of each run, Pallas kernels for 1% -> 1%
where the time goes in v5:
time: 120 us; the launch traced here: 119 us
  blocking collectives  74.6 us (62%)
  starting transfers between devices  18.3 us (15%)
  waiting for transfers between devices  8.63 us (7%)
  Pallas kernels  8.04 us (7%)
  local copies, waits for them, and re-layouts  3.45 us (3%)
  other arithmetic  3.14 us (3%)
  matrix products  1.52 us (1%)
  between operations  1.51 us (1%)
    all_to_all x4, blocking collectives, exchange(): return lax.all_to_all(value, axes, 0, 0, tiled=True)  74.6 us
    ppermute x3, starting transfers between devices, swap_cores(): return lax.ppermute(value, 'c', [(0, 1), (1, 0)])  7.29 us
    ppermute x2, starting transfers between devices, ring_shift(): return lax.ppermute(value, CHIPS, pairs)  6.39 us
    all_to_all x1, starting transfers between devices, exchange(): return lax.all_to_all(value, axes, 0, 0, tiled=True)  4.61 us
    pallas_call x1, Pallas kernels, forward(): pl.pallas_call(forward_kernel, out_shape=(local, local, local, local, jax...  3.81 us
    all_to_all x1, waiting for transfers between devices, exchange(): return lax.all_to_all(value, axes, 0, 0, tiled=True)  3.64 us
    ppermute x3, waiting for transfers between devices, swap_cores(): return lax.ppermute(value, 'c', [(0, 1), (1, 0)])  3.04 us
    pallas_call x1, Pallas kernels, backward(): pl.pallas_call(backward_kernel, out_shape=(jax.ShapeDtypeStruct((LOCAL_RO...  2.85 us
  transfers between devices with their start and end apart: 6, of which 3 were waited for; matrix products, arithmetic and copies ran while one was open for 2% of the time, Pallas kernels for 1%

profile of v5, /device:TPU:1, one launch (start us, length us, event | category | flops | bytes accessed | tf_op | source)
XLA Modules:
  0.0 119.1 jit_solution(7420187103500505283)
XLA Ops:
  0.6 1.2 convolution_convert_fusion
  1.8 2.5 %collective-permute-start = (bf16[128,512]{1,0:T(8,128)(2,1)S(1)}, bf16[128,512]{1,0:T(8,128)(2,1)S(1)}, u32[]{:S(2)}, u32[]{:S(2)}) collective-permute-start(bf16[128,512]{1,0:T(8,128)(2,1)S(1)} %convolution_convert_fusion), channel_id=1, source_target_pairs={{0,2},{2,4},{4,6},{6,8},{8,10},{10,12},{12,14},{14,16},{16,18},{18... | collective-permute-start | bytes 393224 | tf_op jit(solution)/shard_map/ppermute | solution.py:234
  4.4 0.7 broadcast_in_dim.8
  5.1 14.3 %all_to_all.25 = bf16[8,8,512]{2,1,0:T(8,128)(2,1)S(1)} all-to-all(bf16[8,8,512]{2,1,0:T(8,128)(2,1)S(1)} %broadcast_in_dim.8), channel_id=1, replica_groups=mesh['y'=4,'x'=4,'z'=8,'c'=2] {'z'}, dimensions={0} | all-to-all | bytes 131072 | tf_op jit(solution)/shard_map/all_to_all | solution.py:238
  19.4 0.1 broadcast_in_dim.9
  19.5 0.0 copy-start.3
  19.5 0.0 copy-start.5
  19.5 21.3 %all_to_all.26.mine_ref = bf16[16,64,512]{2,1,0:T(8,128)(2,1)S(1)} all-to-all(bf16[16,64,512]{2,1,0:T(8,128)(2,1)S(1)} %broadcast_in_dim.9), channel_id=1, replica_groups=mesh['y'=4,'x'=4,'z'=8,'c'=2] {'y','x'}, dimensions={0} | all-to-all | bytes 2097152 | tf_op jit(solution)/shard_map/all_to_all | solution.py:238
  40.8 3.6 %collective-permute-start.1 = (bf16[16,64,512]{2,1,0:T(8,128)(2,1)S(1)}, bf16[16,64,512]{2,1,0:T(8,128)(2,1)S(1)}, u32[]{:S(2)}, u32[]{:S(2)}) collective-permute-start(bf16[16,64,512]{2,1,0:T(8,128)(2,1)S(1)} %all_to_all.26.mine_ref), channel_id=1, source_target_pairs={{0,1},{1,0},{2,3},{3,2},{4,5},{5,4},{6,7},{7,6},{8,9},{9,8},{10,11... | collective-permute-start | bytes 3145736 | tf_op jit(solution)/shard_map/ppermute | solution.py:226
  45.1 0.0 copy-start.2
  45.1 1.1 copy-done.2
  46.2 1.4 %prepare.1 = (bf16[256,3072]{1,0:T(8,128)(2,1)S(1)}, bf16[3072,256]{1,0:T(8,128)(2,1)S(1)}, f32[256,128]{1,0:T(8,128)S(1)}, f32[256,512]{1,0:T(8,128)S(1)}) custom-call(s32[1]{0:T(128)S(6)} %copy.15.count_ref, s32[1,24]{1,0:T(1,128)S(1)} %copy-done.6, bf16[24,128,128]{2,1,0:T(8,128)(2,1)S(1)} %copy-done.2, bf16[256,512]{1,0:T(8,128)(2,1)S(1)} %copy-done, ...), custom_call_target="tpu_custom_call" | custom-call | flops 134217728 | bytes 5242880 | tf_op jit(solution)/shard_map/prepare/pallas_call | solution.py:174
  47.6 3.8 %forward.1 = (bf16[256,512]{1,0:T(8,128)(2,1)}, bf16[256,512]{1,0:T(8,128)(2,1)S(1)}, bf16[256,512]{1,0:T(8,128)(2,1)S(1)}, bf16[256,512]{1,0:T(8,128)(2,1)S(1)}, bf16[128,512]{1,0:T(8,128)(2,1)S(1)}) custom-call(s32[1,24]{1,0:T(1,128)S(1)} %copy-done.5, s32[1]{0:T(128)} %bitcast.core_ref, bf16[256,512]{1,0:T(8,128)(2,1)S(1)} %copy-done, ...), custom_call_target="tpu_custom_call" | custom-call | tf_op jit(solution)/shard_map/forward/pallas_call | solution.py:196
  51.4 2.9 %backward.1 = (f32[256,512]{1,0:T(8,128)S(1)}, bf16[16,96,512]{2,1,0:T(8,128)(2,1)S(1)}, bf16[16,96,512]{2,1,0:T(8,128)(2,1)S(1)}) custom-call(s32[1,24]{1,0:T(1,128)S(1)} %copy-done.5, s32[1]{0:T(128)} %bitcast.core_ref, bf16[256,512]{1,0:T(8,128)(2,1)S(1)} %copy-done, bf16[3072,256]{1,0:T(8,128)(2,1)S(1)} %get-tuple-element.24.flip_ref, ...), custom_call_target="tpu_custom_call" | custom-call | tf_op jit(solution)/shard_map/backward/pallas_call | solution.py:214
  54.3 0.6 collective-permute-start.2
  54.9 3.0 %collective-permute-done.2 = bf16[16,96,512]{2,1,0:T(8,128)(2,1)S(1)} collective-permute-done((bf16[16,96,512]{2,1,0:T(8,128)(2,1)S(1)}, bf16[16,96,512]{2,1,0:T(8,128)(2,1)S(1)}, u32[]{:S(2)}, u32[]{:S(2)}) %collective-permute-start.2) | collective-permute-done | bytes 1572896 | tf_op jit(solution)/shard_map/ppermute | solution.py:226
  58.0 0.5 add_convert_fusion
  58.5 25.5 %all_to_all.27 = bf16[16,96,512]{2,1,0:T(8,128)(2,1)S(1)} all-to-all(bf16[16,96,512]{2,1,0:T(8,128)(2,1)S(1)} %add_convert_fusion), channel_id=1, replica_groups=mesh['y'=4,'x'=4,'z'=8,'c'=2] {'y','x'}, dimensions={0} | all-to-all | bytes 3145728 | tf_op jit(solution)/shard_map/all_to_all | solution.py:238
  84.0 0.2 reduce_sum.21
  84.3 0.0 copy-start.8
  84.3 0.0 copy-start.9
  84.3 13.5 %all_to_all.28 = bf16[8,40,512]{2,1,0:T(8,128)(2,1)S(1)} all-to-all(bf16[8,40,512]{2,1,0:T(8,128)(2,1)S(1)} %pad_maximum_fusion), channel_id=1, replica_groups=mesh['y'=4,'x'=4,'z'=8,'c'=2] {'z'}, dimensions={0} | all-to-all | bytes 655360 | tf_op jit(solution)/shard_map/all_to_all | solution.py:238
  97.9 0.8 broadcast_in_dim.11
  98.7 4.6 %all-to-all-start.4 = ((bf16[16,32,512]{2,1,0:T(8,128)(2,1)}), bf16[16,32,512]{2,1,0:T(8,128)(2,1)S(1)}, u32[]{:S(2)}, u32[]{:S(2)}) async-start(bf16[16,32,512]{2,1,0:T(8,128)(2,1)} %broadcast_in_dim.11), calls=%async_computation.4 | async-start | bytes 1048576 | tf_op jit(solution)/shard_map/all_to_all | solution.py:238
  103.3 3.8 %collective-permute-start.3 = (bf16[128,512]{1,0:T(8,128)(2,1)S(1)}, bf16[128,512]{1,0:T(8,128)(2,1)S(1)}, u32[]{:S(2)}, u32[]{:S(2)}) collective-permute-start(bf16[128,512]{1,0:T(8,128)(2,1)S(1)} %copy-done.8), channel_id=1, source_target_pairs={{0,254},{2,0},{4,2},{6,4},{8,6},{10,8},{12,10},{14,12},{16,14},{18... | collective-permute-start | bytes 393224 | tf_op jit(solution)/shard_map/ppermute | solution.py:234
  107.2 1.9 %collective-permute-done.3 = bf16[128,512]{1,0:T(8,128)(2,1)S(1)} collective-permute-done((bf16[128,512]{1,0:T(8,128)(2,1)S(1)}, bf16[128,512]{1,0:T(8,128)(2,1)S(1)}, u32[]{:S(2)}, u32[]{:S(2)}) %collective-permute-start.3) | collective-permute-done | bytes 131104 | tf_op jit(solution)/shard_map/ppermute | solution.py:234
  109.1 3.6 %all-to-all-done.4 = bf16[16,32,512]{2,1,0:T(8,128)(2,1)S(1)} async-done(((bf16[16,32,512]{2,1,0:T(8,128)(2,1)}), bf16[16,32,512]{2,1,0:T(8,128)(2,1)S(1)}, u32[]{:S(2)}, u32[]{:S(2)}) %all-to-all-start.4) | async-done | bytes 524320 | tf_op jit(solution)/shard_map/all_to_all | solution.py:238
  112.8 3.1 %collective-permute-start.4 = (bf16[512,512]{1,0:T(8,128)(2,1)S(1)}, bf16[512,512]{1,0:T(8,128)(2,1)S(1)}, u32[]{:S(2)}, u32[]{:S(2)}) collective-permute-start(bf16[512,512]{1,0:T(8,128)(2,1)S(1)} %bitcast.8), channel_id=1, source_target_pairs={{0,1},{1,0},{2,3},{3,2},{4,5},{5,4},{6,7},{7,6},{8,9},{9,8},{10,11... | collective-permute-start | bytes 1572872 | tf_op jit(solution)/shard_map/ppermute | solution.py:226
  115.9 0.6 slice.19
  116.5 0.3 fusion
  116.8 0.9 add.7
  117.7 1.5 %select_convert_fusion = (f32[512,512]{1,0:T(8,128)}, f32[512,512]{1,0:T(8,128)}) fusion(bf16[512,512]{1,0:T(8,128)(2,1)S(1)} %collective-permute-done.4, bf16[512,512]{1,0:T(8,128)(2,1)S(1)} %bitcast.9, pred[]{:T(512)S(6)} %eq.23), kind=kLoop, calls=%fused_computation.3 | loop fusion | flops 1048576 | bytes 3145729 | tf_op jit(solution)/shard_map/convert_element_type | solution.py:312
  (23 shorter events, 0.1 us)
Async XLA Ops:
  1.8 17.5 %collective-permute-start = (bf16[128,512]{1,0:T(8,128)(2,1)S(1)}, bf16[128,512]{1,0:T(8,128)(2,1)S(1)}, u32[]{:S(2)}, u32[]{:S(2)}) collective-permute-start(bf16[128,512]{1,0:T(8,128)(2,1)S(1)} %convolution_convert_fusion), channel_id=1, source_target_pairs={{0,2},{2,4},{4,6},{6,8},{8,10},{10,12},{12,14},{14,16},{16,18},{18... | collective-permute-start | bytes 393224 | tf_op jit(solution)/shard_map/ppermute | solution.py:234
  19.4 25.7 %copy-start = (bf16[256,512]{1,0:T(8,128)(2,1)S(1)}, bf16[256,512]{1,0:T(8,128)(2,1)}, u32[]{:S(2)}) copy-start(bf16[256,512]{1,0:T(8,128)(2,1)} %feat_ref.5) | copy-start | bytes 786436
  19.4 25.7 %copy-start.1 = (bf16[512,512]{1,0:T(8,128)(2,1)S(1)}, bf16[512,512]{1,0:T(8,128)(2,1)}, u32[]{:S(2)}) copy-start(bf16[512,512]{1,0:T(8,128)(2,1)} %ws_ref.3) | copy-start | bytes 1572868
  19.4 25.7 %copy-start.6 = (s32[1,24]{1,0:T(1,128)S(1)}, s32[1,24]{1,0:T(1,128)}, u32[]{:S(2)}) copy-start(s32[1,24]{1,0:T(1,128)} %row_ref.1) | copy-start | bytes 292
  19.5 28.1 %copy-start.3 = (bf16[512,512]{1,0:T(8,128)(2,1)S(1)}, bf16[512,512]{1,0:T(8,128)(2,1)}, u32[]{:S(2)}) copy-start(bf16[512,512]{1,0:T(8,128)(2,1)} %wn_ref.1) | copy-start | bytes 1572868
  19.5 28.1 %copy-start.5 = (s32[1,24]{1,0:T(1,128)S(1)}, s32[1,24]{1,0:T(1,128)}, u32[]{:S(2)}) copy-start(s32[1,24]{1,0:T(1,128)} %col_ref.3) | copy-start | bytes 292
  40.8 6.8 %collective-permute-start.1 = (bf16[16,64,512]{2,1,0:T(8,128)(2,1)S(1)}, bf16[16,64,512]{2,1,0:T(8,128)(2,1)S(1)}, u32[]{:S(2)}, u32[]{:S(2)}) collective-permute-start(bf16[16,64,512]{2,1,0:T(8,128)(2,1)S(1)} %all_to_all.26.mine_ref), channel_id=1, source_target_pairs={{0,1},{1,0},{2,3},{3,2},{4,5},{5,4},{6,7},{7,6},{8,9},{9,8},{10,11... | collective-permute-start | bytes 3145736 | tf_op jit(solution)/shard_map/ppermute | solution.py:226
  45.1 1.1 copy-start.2
  46.2 1.4 %copy-start.4 = (bf16[256,512]{1,0:T(8,128)(2,1)S(1)}, bf16[256,512]{1,0:T(8,128)(2,1)}, u32[]{:S(2)}) copy-start(bf16[256,512]{1,0:T(8,128)(2,1)} %og_ref.1) | copy-start | bytes 786436
  51.4 2.9 %copy-start.7 = (bf16[128,512]{1,0:T(8,128)(2,1)}, bf16[128,512]{1,0:T(8,128)(2,1)S(1)}, u32[]{:S(2)}) copy-start(bf16[128,512]{1,0:T(8,128)(2,1)S(1)} %get-tuple-element.34) | copy-start | bytes 393220
  54.3 3.6 %collective-permute-start.2 = (bf16[16,96,512]{2,1,0:T(8,128)(2,1)S(1)}, bf16[16,96,512]{2,1,0:T(8,128)(2,1)S(1)}, u32[]{:S(2)}, u32[]{:S(2)}) collective-permute-start(bf16[16,96,512]{2,1,0:T(8,128)(2,1)S(1)} %get-tuple-element.33), channel_id=1, source_target_pairs={{0,1},{1,0},{2,3},{3,2},{4,5},{5,4},{6,7},{7,6},{8,9},{9,8},{10,11... | collective-permute-start | bytes 4718600 | tf_op jit(solution)/shard_map/ppermute | solution.py:226
  84.3 19.1 %copy-start.8 = (bf16[128,512]{1,0:T(8,128)(2,1)S(1)}, bf16[128,512]{1,0:T(8,128)(2,1)}, u32[]{:S(2)}) copy-start(bf16[128,512]{1,0:T(8,128)(2,1)} %copy-done.7) | copy-start | bytes 393220
  84.3 32.2 %copy-start.9 = (s32[1,128]{1,0:T(1,128)S(1)}, s32[1,128]{1,0:T(1,128)}, u32[]{:S(2)}) copy-start(s32[1,128]{1,0:T(1,128)} %param.16) | copy-start | bytes 1540
  98.7 14.1 %all-to-all-start.4 = ((bf16[16,32,512]{2,1,0:T(8,128)(2,1)}), bf16[16,32,512]{2,1,0:T(8,128)(2,1)S(1)}, u32[]{:S(2)}, u32[]{:S(2)}) async-start(bf16[16,32,512]{2,1,0:T(8,128)(2,1)} %broadcast_in_dim.11), calls=%async_computation.4 | async-start | bytes 1048576 | tf_op jit(solution)/shard_map/all_to_all | solution.py:238
  103.3 5.8 %collective-permute-start.3 = (bf16[128,512]{1,0:T(8,128)(2,1)S(1)}, bf16[128,512]{1,0:T(8,128)(2,1)S(1)}, u32[]{:S(2)}, u32[]{:S(2)}) collective-permute-start(bf16[128,512]{1,0:T(8,128)(2,1)S(1)} %copy-done.8), channel_id=1, source_target_pairs={{0,254},{2,0},{4,2},{6,4},{8,6},{10,8},{12,10},{14,12},{16,14},{18... | collective-permute-start | bytes 393224 | tf_op jit(solution)/shard_map/ppermute | solution.py:234
  112.8 4.9 %collective-permute-start.4 = (bf16[512,512]{1,0:T(8,128)(2,1)S(1)}, bf16[512,512]{1,0:T(8,128)(2,1)S(1)}, u32[]{:S(2)}, u32[]{:S(2)}) collective-permute-start(bf16[512,512]{1,0:T(8,128)(2,1)S(1)} %bitcast.8), channel_id=1, source_target_pairs={{0,1},{1,0},{2,3},{3,2},{4,5},{5,4},{6,7},{7,6},{8,9},{9,8},{10,11... | collective-permute-start | bytes 1572872 | tf_op jit(solution)/shard_map/ppermute | solution.py:226

commit v6 on v4

--- a/solution.py
+++ b/solution.py
@@ -18,6 +18,8 @@
 ALL = ("y", "x", "z", "c")
 CHIPS = ("y", "x", "z")
 PLANE = ("y", "x")
+SIDE = 4
+ZS = 8
 
 
 def dot(a, b, contract=((1,), (0,))):
@@ -50,7 +52,7 @@
 
 def layer_kernel(
     col_ref,
-    core_ref,
+    spot_ref,
     feat_ref,
     halo_ref,
     mine_ref,
@@ -74,15 +76,25 @@
     slots = flip_ref.shape[0] // TILE
     hub_tiles, column_rows, _ = mine_ref.shape
     first_hub = ROW_BLOCKS + 1
-    low_core = core_ref[0] == 0
+    low_core = spot_ref[0] == 0
+    y, x = spot_ref[1], spot_ref[2]
+
+    def order(tile, sign):
+        down = (tile // SIDE - y) * sign & (SIDE - 1)
+        along = (tile % SIDE - x) * sign & (SIDE - 1)
+        down_first, along_first = down * SIDE + along, along * SIDE + down
+        mine = jnp.where(low_core, down_first, along_first)
+        return mine, jnp.where(low_core, along_first, down_first)
+
     weight_rows = D // hub_tiles
 
     table[:LOCAL_ROWS] = feat_ref[...]
     table[LOCAL_ROWS : LOCAL_ROWS + TILE] = halo_ref[...]
 
     def fill(t, carry):
-        here = mine_ref[t].astype(F32)
-        there = other_ref[t].astype(F32)
+        here_at, there_at = order(t, -1)
+        here = mine_ref[here_at].astype(F32)
+        there = other_ref[there_at].astype(F32)
         low = jnp.where(low_core, here, there)
         high = jnp.where(low_core, there, here)
         pieces = []
@@ -118,8 +130,9 @@
         grads = acc[pl.ds(start, TILE)]
         low = jnp.concatenate([grads[at : at + OWN] for at in range(0, TILE, 2 * OWN)], 0)
         high = jnp.concatenate([grads[at + OWN : at + 2 * OWN] for at in range(0, TILE, 2 * OWN)], 0)
-        keep_ref[t, :column_rows] = jnp.where(low_core, low, high).astype(BF16)
-        send_ref[t, :column_rows] = jnp.where(low_core, high, low).astype(BF16)
+        keep_at, send_at = order(t, 1)
+        keep_ref[keep_at, :column_rows] = jnp.where(low_core, low, high).astype(BF16)
+        send_ref[send_at, :column_rows] = jnp.where(low_core, high, low).astype(BF16)
         return carry
 
     lax.fori_loop(0, hub_tiles, ship, 0)
@@ -128,8 +141,10 @@
     grad_neigh_w = dot(aggregate, grad_pre, ((0,), (0,)))
     keep = jnp.where(low_core, grad_self_w, grad_neigh_w).astype(BF16)
     send = jnp.where(low_core, grad_neigh_w, grad_self_w).astype(BF16)
-    keep_ref[:, column_rows:] = keep.reshape(hub_tiles, weight_rows, D)
-    send_ref[:, column_rows:] = send.reshape(hub_tiles, weight_rows, D)
+    for t in range(hub_tiles):
+        keep_at, send_at = order(t, 1)
+        keep_ref[keep_at, column_rows:] = keep[t * weight_rows : (t + 1) * weight_rows]
+        send_ref[send_at, column_rows:] = send[t * weight_rows : (t + 1) * weight_rows]
     base_ref[...] = dot(grad_pre, ws_ref[...], ((1,), (1,))) + acc[:LOCAL_ROWS]
     back_ref[...] = acc[LOCAL_ROWS : LOCAL_ROWS + TILE].astype(BF16)
 
@@ -178,7 +193,7 @@
             pltpu.VMEM((wide.shape[1], D), BF16),
             pltpu.VMEM((sources, D), F32),
         ],
-        compiler_params=pltpu.CompilerParams(vmem_limit_bytes=32 * 1024 * 1024),
+        compiler_params=pltpu.CompilerParams(vmem_limit_bytes=16 * 1024 * 1024),
         name="layer",
     )(cols, core, feat, halo, mine, other, wide, flip, norm, pre, ws, wn, og)
 
@@ -193,6 +208,34 @@
         count *= lax.axis_size(axis)
     pairs = [(source, (source + steps) % count) for source in range(count)]
     return lax.ppermute(value, CHIPS, pairs)
+
+
+def place(y, x, z, c):
+    return ((y % SIDE * SIDE + x % SIDE) * ZS + z) * 2 + c
+
+
+def hop(value, first, steps):
+    pairs = []
+    for y in range(SIDE):
+        for x in range(SIDE):
+            for c in (0, 1):
+                down = steps if (c == 0) == first else 0
+                for z in range(ZS):
+                    pairs.append((place(y, x, z, c), place(y + down, x + steps - down, z, c)))
+    return lax.ppermute(value, ALL, pairs)
+
+
+def add_along(parts, first):
+    came = [hop(parts[k], first, k) for k in (2, 1, 3)]
+    total = parts[0].astype(F32)
+    for part in came:
+        total += part.astype(F32)
+    return total.astype(BF16)
+
+
+def collect(value, first):
+    far, near, back = (hop(value, first, k) for k in (2, 1, 3))
+    return jnp.concatenate([value, near, far, back], 0)
 
 
 def exchange(value, axes):
@@ -224,13 +267,13 @@
     chosen = (picks[:, None] == jnp.arange(LOCAL_ROWS, dtype=jnp.int32)[None, :]).astype(BF16)
     halo = ring_shift(dot(chosen, features).astype(BF16), 1)
     column = spread(hub_feat, ("z",)).reshape(zs * OWN, D)
-    column, halo = lax.optimization_barrier((column, halo))
-    mine = spread(column, PLANE)
+    mine = collect(collect(column, False), True).reshape(planes, zs * OWN, D)
+    mine, halo = lax.optimization_barrier((mine, halo))
     wide, flip, norm, pre = prepare(block_count, block_row, adjacency, features, w_self)
     other = swap_cores(mine)
     activations, base, back, keep, send = layer(
         block_col,
-        core.reshape(1),
+        jnp.stack([core, lax.axis_index("y"), lax.axis_index("x")]).astype(jnp.int32),
         features,
         halo,
         mine,
@@ -245,8 +288,8 @@
     )
     returned = ring_shift(back, -1)
     chip = (keep.astype(F32) + swap_cores(send).astype(F32)).astype(BF16)
-    plane = jnp.sum(exchange(chip, PLANE).astype(F32), 0).astype(BF16)
-    plane, returned = lax.optimization_barrier((plane, returned))
+    lines = add_along(chip.reshape(SIDE, SIDE, -1, D), True)
+    plane = add_along(lines, False)
     column_rows = zs * OWN
     hub_part = plane[:column_rows].reshape(zs, OWN, D)
     weight_part = plane[column_rows:]
@@ -256,6 +299,7 @@
     total = jnp.sum(exchange(packed, ("z",)).astype(F32), 0)
     factor = 1.0 / math.sqrt(LOCAL_ROWS * 2 * chips)
     weight_mine = spread((total[OWN:] * factor).astype(BF16), PLANE).reshape(D, D)
+    weight_mine, returned = lax.optimization_barrier((weight_mine, returned))
     weight_other = swap_cores(weight_mine)
     grad_w_self = jnp.where(core == 0, weight_mine, weight_other).astype(F32)
     grad_w_neigh = jnp.where(core == 0, weight_other, weight_mine).astype(F32)

time: 125 us -> 111 us (0.89)
  blocking collectives: 63.3 us -> 12.4 us
  starting transfers between devices: 17.2 us -> 39.9 us
  waiting for transfers between devices: 25.4 us -> 40.5 us
    all_to_all x4 -> x1, blocking collectives: 63.3 us -> 12.4 us  [exchange(): return lax.all_to_all(value, axes, 0, 0, tiled=True)]
    ppermute x0 -> x12, waiting for transfers between devices: none -> 28.1 us  [hop(): return lax.ppermute(value, ALL, pairs)]
    all_to_all x1 -> x2, waiting for transfers between devices: 22 us -> 7.04 us  [exchange(): return lax.all_to_all(value, axes, 0, 0, tiled=True)]
    ppermute x0 -> x12, starting transfers between devices: none -> 11.6 us  [hop(): return lax.ppermute(value, ALL, pairs)]
    all_to_all x1 -> x2, starting transfers between devices: 3.84 us -> 13.2 us  [exchange(): return lax.all_to_all(value, axes, 0, 0, tiled=True)]
    ppermute x3, starting transfers between devices: 6.4 us -> 9.31 us  [swap_cores(): return lax.ppermute(value, 'c', [(0, 1), (1, 0)])]
    ppermute x2, waiting for transfers between devices: 0.01 us -> 1.95 us  [ring_shift(): return lax.ppermute(value, CHIPS, pairs)]
    unnamed x24 -> x30, local copies, waits for them, and re-layouts: 2.62 us -> 1.24 us
  transfers between devices with their start and end apart: 6 -> 19, of which waited for: 2 -> 13; matrix products, arithmetic and copies ran while one was open for 2% -> 3% of each run, Pallas kernels for 1% -> 1%
where the time goes in v6:
time: 111 us
  waiting for transfers between devices  40.5 us (36%)
  starting transfers between devices  39.9 us (36%)
  blocking collectives  12.4 us (11%)
  Pallas kernels  6.89 us (6%)
  local copies, waits for them, and re-layouts  4.2 us (4%)
  other arithmetic  3.27 us (3%)
  matrix products  2.18 us (2%)
  between operations  1.58 us (1%)
    ppermute x12, waiting for transfers between devices, hop(): return lax.ppermute(value, ALL, pairs)  28.1 us
    all_to_all x2, starting transfers between devices, exchange(): return lax.all_to_all(value, axes, 0, 0, tiled=True)  13.2 us
    all_to_all x1, blocking collectives, exchange(): return lax.all_to_all(value, axes, 0, 0, tiled=True)  12.4 us
    ppermute x12, starting transfers between devices, hop(): return lax.ppermute(value, ALL, pairs)  11.6 us
    ppermute x3, starting transfers between devices, swap_cores(): return lax.ppermute(value, 'c', [(0, 1), (1, 0)])  9.31 us
    all_to_all x2, waiting for transfers between devices, exchange(): return lax.all_to_all(value, axes, 0, 0, tiled=True)  7.04 us
    ppermute x2, starting transfers between devices, ring_shift(): return lax.ppermute(value, CHIPS, pairs)  5.76 us
    pallas_call x1, Pallas kernels, layer(): pl.pallas_call(layer_kernel, out_shape=(jax.ShapeDtypeStruct((LOCAL_ROWS,...  5.52 us
  transfers between devices with their start and end apart: 19, of which 13 were waited for; matrix products, arithmetic and copies ran while one was open for 3% of the time, Pallas kernels for 1%

profile of v6, /device:TPU:1, one launch (start us, length us, event | category | flops | bytes accessed | tf_op | source)
XLA Modules:
  0.0 110.8 jit_solution(2211084489547776975)
XLA Ops:
  0.6 1.3 %broadcast_in_dim.6 = bf16[8,8,512]{2,1,0:T(8,128)(2,1)} broadcast(bf16[8,512]{1,0:T(8,128)(2,1)} %param.11), dimensions={1,2} | broadcast | bytes 73728 | tf_op jit(solution)/shard_map/broadcast_in_dim | solution.py:247
  2.0 9.1 %all-to-all-start = ((bf16[8,8,512]{2,1,0:T(8,128)(2,1)}), bf16[8,8,512]{2,1,0:T(8,128)(2,1)S(1)}, u32[]{:S(2)}, u32[]{:S(2)}) async-start(bf16[8,8,512]{2,1,0:T(8,128)(2,1)} %broadcast_in_dim.6), calls=%async_computation | async-start | bytes 131072 | tf_op jit(solution)/shard_map/all_to_all | solution.py:242
  11.1 1.8 %convolution_convert_fusion = bf16[128,512]{1,0:T(8,128)(2,1)} fusion(bf16[256,512]{1,0:T(8,128)(2,1)} %feat_ref.3, s32[128]{0:T(128)} %bitcast.31), kind=kOutput, calls=%fused_computation.1 | convolution fusion | flops 33652736 | bytes 393728 | tf_op jit(solution)/shard_map/dot_general | solution.py:26
  13.0 1.5 %collective-permute-start.6 = (bf16[128,512]{1,0:T(8,128)(2,1)}, bf16[128,512]{1,0:T(8,128)(2,1)S(1)}, u32[]{:S(2)}, u32[]{:S(2)}) collective-permute-start(bf16[128,512]{1,0:T(8,128)(2,1)} %convolution_convert_fusion), channel_id=1, source_target_pairs={{0,2},{2,4},{4,6},{6,8},{8,10},{10,12},{12,14},{14,16},{16,18},{18... | collective-permute-start | bytes 393224 | tf_op jit(solution)/shard_map/ppermute | solution.py:210
  14.4 4.0 %all-to-all-done = bf16[8,8,512]{2,1,0:T(8,128)(2,1)S(1)} async-done(((bf16[8,8,512]{2,1,0:T(8,128)(2,1)}), bf16[8,8,512]{2,1,0:T(8,128)(2,1)S(1)}, u32[]{:S(2)}, u32[]{:S(2)}) %all-to-all-start) | async-done | bytes 65568 | tf_op jit(solution)/shard_map/all_to_all | solution.py:242
  18.5 2.7 %collective-permute-start.2 = (bf16[64,512]{1,0:T(8,128)(2,1)S(1)}, bf16[64,512]{1,0:T(8,128)(2,1)S(1)}, u32[]{:S(2)}, u32[]{:S(2)}) collective-permute-start(bf16[64,512]{1,0:T(8,128)(2,1)S(1)} %bitcast.27), channel_id=1, source_target_pairs={{0,48},{2,50},{4,52},{6,54},{8,56},{10,58},{12,60},{14,62},{1,193}... | collective-permute-start | bytes 196616 | tf_op jit(solution)/shard_map/ppermute | solution.py:225
  21.5 0.7 collective-permute-start
  22.5 3.7 %collective-permute-done.1 = bf16[64,512]{1,0:T(8,128)(2,1)S(1)} collective-permute-done((bf16[64,512]{1,0:T(8,128)(2,1)S(1)}, bf16[64,512]{1,0:T(8,128)(2,1)S(1)}, u32[]{:S(2)}, u32[]{:S(2)}) %collective-permute-start.1) | collective-permute-done | bytes 65568 | tf_op jit(solution)/shard_map/ppermute | solution.py:225
  26.6 2.7 %collective-permute-start.5 = (bf16[256,512]{1,0:T(8,128)(2,1)S(1)}, bf16[256,512]{1,0:T(8,128)(2,1)S(1)}, u32[]{:S(2)}, u32[]{:S(2)}) collective-permute-start(bf16[256,512]{1,0:T(8,128)(2,1)S(1)} %pad_maximum_fusion.1), channel_id=1, source_target_pairs={{0,192},{2,194},{4,196},{6,198},{8,200},{10,202},{12,204},{14,206}... | collective-permute-start | bytes 786440 | tf_op jit(solution)/shard_map/ppermute | solution.py:225
  30.3 8.9 %collective-permute-done.3 = bf16[256,512]{1,0:T(8,128)(2,1)S(1)} collective-permute-done((bf16[256,512]{1,0:T(8,128)(2,1)S(1)}, bf16[256,512]{1,0:T(8,128)(2,1)S(1)}, u32[]{:S(2)}, u32[]{:S(2)}) %collective-permute-start.3) | collective-permute-done | bytes 262176 | tf_op jit(solution)/shard_map/ppermute | solution.py:225
  39.3 4.5 %collective-permute-start.7 = (bf16[16,64,512]{2,1,0:T(8,128)(2,1)S(1)}, bf16[16,64,512]{2,1,0:T(8,128)(2,1)S(1)}, u32[]{:S(2)}, u32[]{:S(2)}) collective-permute-start(bf16[16,64,512]{2,1,0:T(8,128)(2,1)S(1)} %bitcast.23), channel_id=1, source_target_pairs={{0,1},{1,0},{2,3},{3,2},{4,5},{5,4},{6,7},{7,6},{8,9},{9,8},{10,11... | collective-permute-start | bytes 3145736 | tf_op jit(solution)/shard_map/ppermute | solution.py:202
  44.5 1.1 %copy-done.2 = bf16[24,128,128]{2,1,0:T(8,128)(2,1)S(1)} copy-done((bf16[24,128,128]{2,1,0:T(8,128)(2,1)S(1)}, bf16[24,128,128]{2,1,0:T(8,128)(2,1)}, u32[]{:S(2)}) %copy-start.2) | copy-done | bytes 786456
  45.6 1.4 %prepare.1 = (bf16[256,3072]{1,0:T(8,128)(2,1)S(1)}, bf16[3072,256]{1,0:T(8,128)(2,1)S(1)}, f32[256,128]{1,0:T(8,128)S(1)}, f32[256,512]{1,0:T(8,128)S(1)}) custom-call(s32[1]{0:T(128)S(6)} %copy.21.count_ref, s32[1,24]{1,0:T(1,128)S(1)} %copy-done.7, bf16[24,128,128]{2,1,0:T(8,128)(2,1)S(1)} %copy-done.2, bf16[256,512]{1,0:T(8,128)(2,1)S(1)} %copy-done, ...), custom_call_target="tpu_custom_call" | custom-call | flops 134217728 | bytes 5242880 | tf_op jit(solution)/shard_map/prepare/pallas_call | solution.py:158
  47.1 5.5 %layer.1 = (bf16[256,512]{1,0:T(8,128)(2,1)}, f32[256,512]{1,0:T(8,128)S(1)}, bf16[128,512]{1,0:T(8,128)(2,1)S(1)}, bf16[16,96,512]{2,1,0:T(8,128)(2,1)S(1)}, bf16[16,96,512]{2,1,0:T(8,128)(2,1)S(1)}) custom-call(s32[1,24]{1,0:T(1,128)S(1)} %copy-done.8, s32[3]{0:T(128)S(1)} %pad_add_fusion.spot_ref, bf16[256,512]{1,0:T(8,128)(2,1)S(1)} %copy-done, ...), custom_call_target="tpu_custom_call" | custom-call | tf_op jit(solution)/shard_map/layer/pallas_call | solution.py:180
  52.6 3.4 %collective-permute-done.8 = bf16[16,96,512]{2,1,0:T(8,128)(2,1)S(1)} collective-permute-done((bf16[16,96,512]{2,1,0:T(8,128)(2,1)S(1)}, bf16[16,96,512]{2,1,0:T(8,128)(2,1)S(1)}, u32[]{:S(2)}, u32[]{:S(2)}) %collective-permute-start.8) | collective-permute-done | bytes 1572896 | tf_op jit(solution)/shard_map/ppermute | solution.py:202
  56.7 1.1 %collective-permute-start.9 = (bf16[4,96,512]{2,1,0:T(8,128)(2,1)S(1)}, bf16[4,96,512]{2,1,0:T(8,128)(2,1)S(1)}, u32[]{:S(2)}, u32[]{:S(2)}) collective-permute-start(bf16[4,96,512]{2,1,0:T(8,128)(2,1)S(1)} %get-tuple-element.31), channel_id=1, source_target_pairs={{0,128},{2,130},{4,132},{6,134},{8,136},{10,138},{12,140},{14,142}... | collective-permute-start | bytes 1179656 | tf_op jit(solution)/shard_map/ppermute | solution.py:225
  58.3 0.9 collective-permute-start.10
  59.3 6.0 %collective-permute-done.9 = bf16[4,96,512]{2,1,0:T(8,128)(2,1)S(1)} collective-permute-done((bf16[4,96,512]{2,1,0:T(8,128)(2,1)S(1)}, bf16[4,96,512]{2,1,0:T(8,128)(2,1)S(1)}, u32[]{:S(2)}, u32[]{:S(2)}) %collective-permute-start.9) | collective-permute-done | bytes 393248 | tf_op jit(solution)/shard_map/ppermute | solution.py:225
  65.2 2.1 %collective-permute-done.11 = bf16[4,96,512]{2,1,0:T(8,128)(2,1)S(1)} collective-permute-done((bf16[4,96,512]{2,1,0:T(8,128)(2,1)S(1)}, bf16[4,96,512]{2,1,0:T(8,128)(2,1)S(1)}, u32[]{:S(2)}, u32[]{:S(2)}) %collective-permute-start.11) | collective-permute-done | bytes 393248 | tf_op jit(solution)/shard_map/ppermute | solution.py:225
  67.3 2.1 %collective-permute-done.10 = bf16[4,96,512]{2,1,0:T(8,128)(2,1)S(1)} collective-permute-done((bf16[4,96,512]{2,1,0:T(8,128)(2,1)S(1)}, bf16[4,96,512]{2,1,0:T(8,128)(2,1)S(1)}, u32[]{:S(2)}, u32[]{:S(2)}) %collective-permute-start.10) | collective-permute-done | bytes 393248 | tf_op jit(solution)/shard_map/ppermute | solution.py:225
  69.8 0.9 collective-permute-start.14
  71.3 3.5 %collective-permute-done.12 = bf16[96,512]{1,0:T(8,128)(2,1)S(1)} collective-permute-done((bf16[96,512]{1,0:T(8,128)(2,1)S(1)}, bf16[96,512]{1,0:T(8,128)(2,1)S(1)}, u32[]{:S(2)}, u32[]{:S(2)}) %collective-permute-start.12) | collective-permute-done | bytes 98336 | tf_op jit(solution)/shard_map/ppermute | solution.py:225
  74.7 1.3 %collective-permute-done.13 = bf16[96,512]{1,0:T(8,128)(2,1)S(1)} collective-permute-done((bf16[96,512]{1,0:T(8,128)(2,1)S(1)}, bf16[96,512]{1,0:T(8,128)(2,1)S(1)}, u32[]{:S(2)}, u32[]{:S(2)}) %collective-permute-start.13) | collective-permute-done | bytes 98336 | tf_op jit(solution)/shard_map/ppermute | solution.py:225
  76.2 12.4 %all_to_all.15 = bf16[8,40,512]{2,1,0:T(8,128)(2,1)S(1)} all-to-all(bf16[8,40,512]{2,1,0:T(8,128)(2,1)S(1)} %pad_maximum_fusion), channel_id=1, replica_groups=mesh['y'=4,'x'=4,'z'=8,'c'=2] {'z'}, dimensions={0} | all-to-all | bytes 655360 | tf_op jit(solution)/shard_map/all_to_all | solution.py:242
  88.6 0.8 broadcast_in_dim.8
  89.5 4.0 %all-to-all-start.2 = ((bf16[16,32,512]{2,1,0:T(8,128)(2,1)}), bf16[16,32,512]{2,1,0:T(8,128)(2,1)S(1)}, u32[]{:S(2)}, u32[]{:S(2)}) async-start(bf16[16,32,512]{2,1,0:T(8,128)(2,1)} %broadcast_in_dim.8), calls=%async_computation.2 | async-start | bytes 1048576 | tf_op jit(solution)/shard_map/all_to_all | solution.py:242
  93.5 4.3 %collective-permute-start.15 = (bf16[128,512]{1,0:T(8,128)(2,1)S(1)}, bf16[128,512]{1,0:T(8,128)(2,1)S(1)}, u32[]{:S(2)}, u32[]{:S(2)}) collective-permute-start(bf16[128,512]{1,0:T(8,128)(2,1)S(1)} %copy-done.10), channel_id=1, source_target_pairs={{0,254},{2,0},{4,2},{6,4},{8,6},{10,8},{12,10},{14,12},{16,14},{18... | collective-permute-start | bytes 393224 | tf_op jit(solution)/shard_map/ppermute | solution.py:210
  97.8 1.9 %collective-permute-done.15 = bf16[128,512]{1,0:T(8,128)(2,1)S(1)} collective-permute-done((bf16[128,512]{1,0:T(8,128)(2,1)S(1)}, bf16[128,512]{1,0:T(8,128)(2,1)S(1)}, u32[]{:S(2)}, u32[]{:S(2)}) %collective-permute-start.15) | collective-permute-done | bytes 131104 | tf_op jit(solution)/shard_map/ppermute | solution.py:210
  99.8 3.0 %all-to-all-done.2 = bf16[16,32,512]{2,1,0:T(8,128)(2,1)S(1)} async-done(((bf16[16,32,512]{2,1,0:T(8,128)(2,1)}), bf16[16,32,512]{2,1,0:T(8,128)(2,1)S(1)}, u32[]{:S(2)}, u32[]{:S(2)}) %all-to-all-start.2) | async-done | bytes 524320 | tf_op jit(solution)/shard_map/all_to_all | solution.py:242
  102.8 4.8 %collective-permute-start.16 = (bf16[512,512]{1,0:T(8,128)(2,1)S(1)}, bf16[512,512]{1,0:T(8,128)(2,1)S(1)}, u32[]{:S(2)}, u32[]{:S(2)}) collective-permute-start(bf16[512,512]{1,0:T(8,128)(2,1)S(1)} %bitcast.25), channel_id=1, source_target_pairs={{0,1},{1,0},{2,3},{3,2},{4,5},{5,4},{6,7},{7,6},{8,9},{9,8},{10,11... | collective-permute-start | bytes 1572872 | tf_op jit(solution)/shard_map/ppermute | solution.py:202
  108.5 0.9 add.31
  109.4 1.5 %select_convert_fusion = (f32[512,512]{1,0:T(8,128)}, f32[512,512]{1,0:T(8,128)}) fusion(bf16[512,512]{1,0:T(8,128)(2,1)S(1)} %collective-permute-done.16, bf16[512,512]{1,0:T(8,128)(2,1)S(1)} %bitcast.26, pred[]{:T(512)S(6)} %eq.23), kind=kLoop, calls=%fused_computation.4 | loop fusion | flops 1048576 | bytes 3145729 | tf_op jit(solution)/shard_map/convert_element_type | solution.py:305
  (60 shorter events, 5.4 us)
Async XLA Ops:
  2.0 42.5 %copy-start = (bf16[256,512]{1,0:T(8,128)(2,1)S(1)}, bf16[256,512]{1,0:T(8,128)(2,1)}, u32[]{:S(2)}) copy-start(bf16[256,512]{1,0:T(8,128)(2,1)} %feat_ref.3) | copy-start | bytes 786436
  2.0 42.5 %copy-start.1 = (bf16[512,512]{1,0:T(8,128)(2,1)S(1)}, bf16[512,512]{1,0:T(8,128)(2,1)}, u32[]{:S(2)}) copy-start(bf16[512,512]{1,0:T(8,128)(2,1)} %ws_ref.3) | copy-start | bytes 1572868
  2.0 42.5 %copy-start.7 = (s32[1,24]{1,0:T(1,128)S(1)}, s32[1,24]{1,0:T(1,128)}, u32[]{:S(2)}) copy-start(s32[1,24]{1,0:T(1,128)} %row_ref.1) | copy-start | bytes 292
  2.0 16.5 %all-to-all-start = ((bf16[8,8,512]{2,1,0:T(8,128)(2,1)}), bf16[8,8,512]{2,1,0:T(8,128)(2,1)S(1)}, u32[]{:S(2)}, u32[]{:S(2)}) async-start(bf16[8,8,512]{2,1,0:T(8,128)(2,1)} %broadcast_in_dim.6), calls=%async_computation | async-start | bytes 131072 | tf_op jit(solution)/shard_map/all_to_all | solution.py:242
  13.0 26.3 %collective-permute-start.6 = (bf16[128,512]{1,0:T(8,128)(2,1)}, bf16[128,512]{1,0:T(8,128)(2,1)S(1)}, u32[]{:S(2)}, u32[]{:S(2)}) collective-permute-start(bf16[128,512]{1,0:T(8,128)(2,1)} %convolution_convert_fusion), channel_id=1, source_target_pairs={{0,2},{2,4},{4,6},{6,8},{8,10},{10,12},{12,14},{14,16},{16,18},{18... | collective-permute-start | bytes 393224 | tf_op jit(solution)/shard_map/ppermute | solution.py:210
  18.5 4.1 %collective-permute-start.2 = (bf16[64,512]{1,0:T(8,128)(2,1)S(1)}, bf16[64,512]{1,0:T(8,128)(2,1)S(1)}, u32[]{:S(2)}, u32[]{:S(2)}) collective-permute-start(bf16[64,512]{1,0:T(8,128)(2,1)S(1)} %bitcast.27), channel_id=1, source_target_pairs={{0,48},{2,50},{4,52},{6,54},{8,56},{10,58},{12,60},{14,62},{1,193}... | collective-permute-start | bytes 196616 | tf_op jit(solution)/shard_map/ppermute | solution.py:225
  21.2 5.0 %collective-permute-start.1 = (bf16[64,512]{1,0:T(8,128)(2,1)S(1)}, bf16[64,512]{1,0:T(8,128)(2,1)S(1)}, u32[]{:S(2)}, u32[]{:S(2)}) collective-permute-start(bf16[64,512]{1,0:T(8,128)(2,1)S(1)} %bitcast.28), channel_id=1, source_target_pairs={{0,32},{2,34},{4,36},{6,38},{8,40},{10,42},{12,44},{14,46},{1,129}... | collective-permute-start | bytes 196616 | tf_op jit(solution)/shard_map/ppermute | solution.py:225
  21.5 5.0 %collective-permute-start = (bf16[64,512]{1,0:T(8,128)(2,1)S(1)}, bf16[64,512]{1,0:T(8,128)(2,1)S(1)}, u32[]{:S(2)}, u32[]{:S(2)}) collective-permute-start(bf16[64,512]{1,0:T(8,128)(2,1)S(1)} %bitcast.29), channel_id=1, source_target_pairs={{0,16},{2,18},{4,20},{6,22},{8,24},{10,26},{12,28},{14,30},{1,65},... | collective-permute-start | bytes 196616 | tf_op jit(solution)/shard_map/ppermute | solution.py:225
  26.6 12.6 %collective-permute-start.5 = (bf16[256,512]{1,0:T(8,128)(2,1)S(1)}, bf16[256,512]{1,0:T(8,128)(2,1)S(1)}, u32[]{:S(2)}, u32[]{:S(2)}) collective-permute-start(bf16[256,512]{1,0:T(8,128)(2,1)S(1)} %pad_maximum_fusion.1), channel_id=1, source_target_pairs={{0,192},{2,194},{4,196},{6,198},{8,200},{10,202},{12,204},{14,206}... | collective-permute-start | bytes 786440 | tf_op jit(solution)/shard_map/ppermute | solution.py:225
  29.3 9.8 %collective-permute-start.4 = (bf16[256,512]{1,0:T(8,128)(2,1)S(1)}, bf16[256,512]{1,0:T(8,128)(2,1)S(1)}, u32[]{:S(2)}, u32[]{:S(2)}) collective-permute-start(bf16[256,512]{1,0:T(8,128)(2,1)S(1)} %pad_maximum_fusion.1), channel_id=1, source_target_pairs={{0,128},{2,130},{4,132},{6,134},{8,136},{10,138},{12,140},{14,142}... | collective-permute-start | bytes 786440 | tf_op jit(solution)/shard_map/ppermute | solution.py:225
  29.6 9.5 %collective-permute-start.3 = (bf16[256,512]{1,0:T(8,128)(2,1)S(1)}, bf16[256,512]{1,0:T(8,128)(2,1)S(1)}, u32[]{:S(2)}, u32[]{:S(2)}) collective-permute-start(bf16[256,512]{1,0:T(8,128)(2,1)S(1)} %pad_maximum_fusion.1), channel_id=1, source_target_pairs={{0,64},{2,66},{4,68},{6,70},{8,72},{10,74},{12,76},{14,78},{1,17},... | collective-permute-start | bytes 786440 | tf_op jit(solution)/shard_map/ppermute | solution.py:225
  30.2 16.8 %copy-start.3 = (bf16[512,512]{1,0:T(8,128)(2,1)S(1)}, bf16[512,512]{1,0:T(8,128)(2,1)}, u32[]{:S(2)}) copy-start(bf16[512,512]{1,0:T(8,128)(2,1)} %wn_ref.1) | copy-start | bytes 1572868
  30.3 16.8 %copy-start.8 = (s32[1,24]{1,0:T(1,128)S(1)}, s32[1,24]{1,0:T(1,128)}, u32[]{:S(2)}) copy-start(s32[1,24]{1,0:T(1,128)} %col_ref.1) | copy-start | bytes 292
  39.3 7.8 %collective-permute-start.7 = (bf16[16,64,512]{2,1,0:T(8,128)(2,1)S(1)}, bf16[16,64,512]{2,1,0:T(8,128)(2,1)S(1)}, u32[]{:S(2)}, u32[]{:S(2)}) collective-permute-start(bf16[16,64,512]{2,1,0:T(8,128)(2,1)S(1)} %bitcast.23), channel_id=1, source_target_pairs={{0,1},{1,0},{2,3},{3,2},{4,5},{5,4},{6,7},{7,6},{8,9},{9,8},{10,11... | collective-permute-start | bytes 3145736 | tf_op jit(solution)/shard_map/ppermute | solution.py:202
  44.5 1.1 %copy-start.2 = (bf16[24,128,128]{2,1,0:T(8,128)(2,1)S(1)}, bf16[24,128,128]{2,1,0:T(8,128)(2,1)}, u32[]{:S(2)}) copy-start(bf16[24,128,128]{2,1,0:T(8,128)(2,1)} %adj_ref.1) | copy-start | bytes 2359300
  45.6 1.5 %copy-start.6 = (bf16[256,512]{1,0:T(8,128)(2,1)S(1)}, bf16[256,512]{1,0:T(8,128)(2,1)}, u32[]{:S(2)}) copy-start(bf16[256,512]{1,0:T(8,128)(2,1)} %og_ref.1) | copy-start | bytes 786436
  52.6 3.9 %copy-start.4 = (f32[256,512]{1,0:T(8,128)}, f32[256,512]{1,0:T(8,128)S(1)}, u32[]{:S(2)}) copy-start(f32[256,512]{1,0:T(8,128)S(1)} %get-tuple-element.25) | copy-start | bytes 1572868
  52.6 3.9 %copy-start.9 = (bf16[128,512]{1,0:T(8,128)(2,1)}, bf16[128,512]{1,0:T(8,128)(2,1)S(1)}, u32[]{:S(2)}) copy-start(bf16[128,512]{1,0:T(8,128)(2,1)S(1)} %get-tuple-element.28) | copy-start | bytes 393220
  52.6 3.4 %collective-permute-start.8 = (bf16[16,96,512]{2,1,0:T(8,128)(2,1)S(1)}, bf16[16,96,512]{2,1,0:T(8,128)(2,1)S(1)}, u32[]{:S(2)}, u32[]{:S(2)}) collective-permute-start(bf16[16,96,512]{2,1,0:T(8,128)(2,1)S(1)} %get-tuple-element.27), channel_id=1, source_target_pairs={{0,1},{1,0},{2,3},{3,2},{4,5},{5,4},{6,7},{7,6},{8,9},{9,8},{10,11... | collective-permute-start | bytes 4718600 | tf_op jit(solution)/shard_map/ppermute | solution.py:202
  56.7 8.6 %collective-permute-start.9 = (bf16[4,96,512]{2,1,0:T(8,128)(2,1)S(1)}, bf16[4,96,512]{2,1,0:T(8,128)(2,1)S(1)}, u32[]{:S(2)}, u32[]{:S(2)}) collective-permute-start(bf16[4,96,512]{2,1,0:T(8,128)(2,1)S(1)} %get-tuple-element.31), channel_id=1, source_target_pairs={{0,128},{2,130},{4,132},{6,134},{8,136},{10,138},{12,140},{14,142}... | collective-permute-start | bytes 1179656 | tf_op jit(solution)/shard_map/ppermute | solution.py:225
  57.8 9.5 %collective-permute-start.11 = (bf16[4,96,512]{2,1,0:T(8,128)(2,1)S(1)}, bf16[4,96,512]{2,1,0:T(8,128)(2,1)S(1)}, u32[]{:S(2)}, u32[]{:S(2)}) collective-permute-start(bf16[4,96,512]{2,1,0:T(8,128)(2,1)S(1)} %get-tuple-element.32), channel_id=1, source_target_pairs={{0,192},{2,194},{4,196},{6,198},{8,200},{10,202},{12,204},{14,206}... | collective-permute-start | bytes 1179656 | tf_op jit(solution)/shard_map/ppermute | solution.py:225
  58.3 11.1 %collective-permute-start.10 = (bf16[4,96,512]{2,1,0:T(8,128)(2,1)S(1)}, bf16[4,96,512]{2,1,0:T(8,128)(2,1)S(1)}, u32[]{:S(2)}, u32[]{:S(2)}) collective-permute-start(bf16[4,96,512]{2,1,0:T(8,128)(2,1)S(1)} %get-tuple-element.33), channel_id=1, source_target_pairs={{0,64},{2,66},{4,68},{6,70},{8,72},{10,74},{12,76},{14,78},{1,17},... | collective-permute-start | bytes 1179656 | tf_op jit(solution)/shard_map/ppermute | solution.py:225
  69.6 5.1 %collective-permute-start.12 = (bf16[96,512]{1,0:T(8,128)(2,1)S(1)}, bf16[96,512]{1,0:T(8,128)(2,1)S(1)}, u32[]{:S(2)}, u32[]{:S(2)}) collective-permute-start(bf16[96,512]{1,0:T(8,128)(2,1)S(1)} %get-tuple-element.36), channel_id=1, source_target_pairs={{0,32},{2,34},{4,36},{6,38},{8,40},{10,42},{12,44},{14,46},{1,129}... | collective-permute-start | bytes 294920 | tf_op jit(solution)/shard_map/ppermute | solution.py:225
  69.8 5.0 %collective-permute-start.14 = (bf16[96,512]{1,0:T(8,128)(2,1)S(1)}, bf16[96,512]{1,0:T(8,128)(2,1)S(1)}, u32[]{:S(2)}, u32[]{:S(2)}) collective-permute-start(bf16[96,512]{1,0:T(8,128)(2,1)S(1)} %get-tuple-element.37), channel_id=1, source_target_pairs={{0,48},{2,50},{4,52},{6,54},{8,56},{10,58},{12,60},{14,62},{1,193}... | collective-permute-start | bytes 294920 | tf_op jit(solution)/shard_map/ppermute | solution.py:225
  70.6 5.4 %collective-permute-start.13 = (bf16[96,512]{1,0:T(8,128)(2,1)S(1)}, bf16[96,512]{1,0:T(8,128)(2,1)S(1)}, u32[]{:S(2)}, u32[]{:S(2)}) collective-permute-start(bf16[96,512]{1,0:T(8,128)(2,1)S(1)} %get-tuple-element.38), channel_id=1, source_target_pairs={{0,16},{2,18},{4,20},{6,22},{8,24},{10,26},{12,28},{14,30},{1,65},... | collective-permute-start | bytes 294920 | tf_op jit(solution)/shard_map/ppermute | solution.py:225
  76.1 17.4 %copy-start.10 = (bf16[128,512]{1,0:T(8,128)(2,1)S(1)}, bf16[128,512]{1,0:T(8,128)(2,1)}, u32[]{:S(2)}) copy-start(bf16[128,512]{1,0:T(8,128)(2,1)} %copy-done.9) | copy-start | bytes 393220
  76.2 32.0 %copy-start.11 = (s32[1,128]{1,0:T(1,128)S(1)}, s32[1,128]{1,0:T(1,128)}, u32[]{:S(2)}) copy-start(s32[1,128]{1,0:T(1,128)} %param.16) | copy-start | bytes 1540
  76.2 32.3 %copy-start.5 = (f32[256,512]{1,0:T(8,128)S(1)}, f32[256,512]{1,0:T(8,128)}, u32[]{:S(2)}) copy-start(f32[256,512]{1,0:T(8,128)} %copy-done.4) | copy-start | bytes 1572868
  89.5 13.3 %all-to-all-start.2 = ((bf16[16,32,512]{2,1,0:T(8,128)(2,1)}), bf16[16,32,512]{2,1,0:T(8,128)(2,1)S(1)}, u32[]{:S(2)}, u32[]{:S(2)}) async-start(bf16[16,32,512]{2,1,0:T(8,128)(2,1)} %broadcast_in_dim.8), calls=%async_computation.2 | async-start | bytes 1048576 | tf_op jit(solution)/shard_map/all_to_all | solution.py:242
  93.5 6.2 %collective-permute-start.15 = (bf16[128,512]{1,0:T(8,128)(2,1)S(1)}, bf16[128,512]{1,0:T(8,128)(2,1)S(1)}, u32[]{:S(2)}, u32[]{:S(2)}) collective-permute-start(bf16[128,512]{1,0:T(8,128)(2,1)S(1)} %copy-done.10), channel_id=1, source_target_pairs={{0,254},{2,0},{4,2},{6,4},{8,6},{10,8},{12,10},{14,12},{16,14},{18... | collective-permute-start | bytes 393224 | tf_op jit(solution)/shard_map/ppermute | solution.py:210
  102.8 6.6 %collective-permute-start.16 = (bf16[512,512]{1,0:T(8,128)(2,1)S(1)}, bf16[512,512]{1,0:T(8,128)(2,1)S(1)}, u32[]{:S(2)}, u32[]{:S(2)}) collective-permute-start(bf16[512,512]{1,0:T(8,128)(2,1)S(1)} %bitcast.25), channel_id=1, source_target_pairs={{0,1},{1,0},{2,3},{3,2},{4,5},{5,4},{6,7},{7,6},{8,9},{9,8},{10,11... | collective-permute-start | bytes 1572872 | tf_op jit(solution)/shard_map/ppermute | solution.py:202

commit v7 on v6

--- a/solution.py
+++ b/solution.py
@@ -289,6 +289,7 @@
     returned = ring_shift(back, -1)
     chip = (keep.astype(F32) + swap_cores(send).astype(F32)).astype(BF16)
     lines = add_along(chip.reshape(SIDE, SIDE, -1, D), True)
+    lines, returned = lax.optimization_barrier((lines, returned))
     plane = add_along(lines, False)
     column_rows = zs * OWN
     hub_part = plane[:column_rows].reshape(zs, OWN, D)
@@ -299,7 +300,6 @@
     total = jnp.sum(exchange(packed, ("z",)).astype(F32), 0)
     factor = 1.0 / math.sqrt(LOCAL_ROWS * 2 * chips)
     weight_mine = spread((total[OWN:] * factor).astype(BF16), PLANE).reshape(D, D)
-    weight_mine, returned = lax.optimization_barrier((weight_mine, returned))
     weight_other = swap_cores(weight_mine)
     grad_w_self = jnp.where(core == 0, weight_mine, weight_other).astype(F32)
     grad_w_neigh = jnp.where(core == 0, weight_other, weight_mine).astype(F32)

time: 111 us -> 110 us (level)
  blocking collectives: 12.4 us -> 25.4 us
  starting transfers between devices: 39.9 us -> 32.8 us
  waiting for transfers between devices: 40.5 us -> 34.2 us
    all_to_all x1 -> x2, blocking collectives: 12.4 us -> 25.4 us  [exchange(): return lax.all_to_all(value, axes, 0, 0, tiled=True)]
    all_to_all x2 -> x1, starting transfers between devices: 13.2 us -> 9.15 us  [exchange(): return lax.all_to_all(value, axes, 0, 0, tiled=True)]
    all_to_all x2 -> x1, waiting for transfers between devices: 7.04 us -> 4.03 us  [exchange(): return lax.all_to_all(value, axes, 0, 0, tiled=True)]
    ppermute x2, starting transfers between devices: 5.76 us -> 2.78 us  [ring_shift(): return lax.ppermute(value, CHIPS, pairs)]
    ppermute x2, waiting for transfers between devices: 1.95 us -> 0.01 us  [ring_shift(): return lax.ppermute(value, CHIPS, pairs)]
    ppermute x12, waiting for transfers between devices: 28.1 us -> 26.8 us  [hop(): return lax.ppermute(value, ALL, pairs)]
  transfers between devices with their start and end apart: 19 -> 18, of which waited for: 13 -> 11; matrix products, arithmetic and copies ran while one was open for 3% -> 4% of each run, Pallas kernels for 1% -> 1%
where the time goes in v7:
time: 110 us
  waiting for transfers between devices  34.2 us (31%)
  starting transfers between devices  32.8 us (30%)
  blocking collectives  25.4 us (23%)
  Pallas kernels  6.89 us (6%)
  local copies, waits for them, and re-layouts  3.39 us (3%)
  other arithmetic  3.31 us (3%)
  matrix products  2.18 us (2%)
  between operations  1.56 us (1%)
    ppermute x12, waiting for transfers between devices, hop(): return lax.ppermute(value, ALL, pairs)  26.8 us
    all_to_all x2, blocking collectives, exchange(): return lax.all_to_all(value, axes, 0, 0, tiled=True)  25.4 us
    ppermute x12, starting transfers between devices, hop(): return lax.ppermute(value, ALL, pairs)  11.6 us
    ppermute x3, starting transfers between devices, swap_cores(): return lax.ppermute(value, 'c', [(0, 1), (1, 0)])  9.25 us
    all_to_all x1, starting transfers between devices, exchange(): return lax.all_to_all(value, axes, 0, 0, tiled=True)  9.15 us
    pallas_call x1, Pallas kernels, layer(): pl.pallas_call(layer_kernel, out_shape=(jax.ShapeDtypeStruct((LOCAL_ROWS,...  5.52 us
    all_to_all x1, waiting for transfers between devices, exchange(): return lax.all_to_all(value, axes, 0, 0, tiled=True)  4.03 us
    ppermute x3, waiting for transfers between devices, swap_cores(): return lax.ppermute(value, 'c', [(0, 1), (1, 0)])  3.39 us
  transfers between devices with their start and end apart: 18, of which 11 were waited for; matrix products, arithmetic and copies ran while one was open for 4% of the time, Pallas kernels for 1%

profile of v7, /device:TPU:1, one launch (start us, length us, event | category | flops | bytes accessed | tf_op | source)
XLA Modules:
  0.0 109.7 jit_solution(2036644254842232479)
XLA Ops:
  0.6 1.3 %broadcast_in_dim.6 = bf16[8,8,512]{2,1,0:T(8,128)(2,1)} broadcast(bf16[8,512]{1,0:T(8,128)(2,1)} %param.11), dimensions={1,2} | broadcast | bytes 73728 | tf_op jit(solution)/shard_map/broadcast_in_dim | solution.py:247
  2.0 9.1 %all-to-all-start = ((bf16[8,8,512]{2,1,0:T(8,128)(2,1)}), bf16[8,8,512]{2,1,0:T(8,128)(2,1)S(1)}, u32[]{:S(2)}, u32[]{:S(2)}) async-start(bf16[8,8,512]{2,1,0:T(8,128)(2,1)} %broadcast_in_dim.6), calls=%async_computation | async-start | bytes 131072 | tf_op jit(solution)/shard_map/all_to_all | solution.py:242
  11.1 1.8 %convolution_convert_fusion = bf16[128,512]{1,0:T(8,128)(2,1)} fusion(bf16[256,512]{1,0:T(8,128)(2,1)} %feat_ref.3, s32[128]{0:T(128)} %bitcast.30), kind=kOutput, calls=%fused_computation.1 | convolution fusion | flops 33652736 | bytes 393728 | tf_op jit(solution)/shard_map/dot_general | solution.py:26
  13.0 1.5 %collective-permute-start.6 = (bf16[128,512]{1,0:T(8,128)(2,1)}, bf16[128,512]{1,0:T(8,128)(2,1)S(1)}, u32[]{:S(2)}, u32[]{:S(2)}) collective-permute-start(bf16[128,512]{1,0:T(8,128)(2,1)} %convolution_convert_fusion), channel_id=1, source_target_pairs={{0,2},{2,4},{4,6},{6,8},{8,10},{10,12},{12,14},{14,16},{16,18},{18... | collective-permute-start | bytes 393224 | tf_op jit(solution)/shard_map/ppermute | solution.py:210
  14.4 4.0 %all-to-all-done = bf16[8,8,512]{2,1,0:T(8,128)(2,1)S(1)} async-done(((bf16[8,8,512]{2,1,0:T(8,128)(2,1)}), bf16[8,8,512]{2,1,0:T(8,128)(2,1)S(1)}, u32[]{:S(2)}, u32[]{:S(2)}) %all-to-all-start) | async-done | bytes 65568 | tf_op jit(solution)/shard_map/all_to_all | solution.py:242
  18.5 2.7 %collective-permute-start.2 = (bf16[64,512]{1,0:T(8,128)(2,1)S(1)}, bf16[64,512]{1,0:T(8,128)(2,1)S(1)}, u32[]{:S(2)}, u32[]{:S(2)}) collective-permute-start(bf16[64,512]{1,0:T(8,128)(2,1)S(1)} %bitcast.26), channel_id=1, source_target_pairs={{0,48},{2,50},{4,52},{6,54},{8,56},{10,58},{12,60},{14,62},{1,193}... | collective-permute-start | bytes 196616 | tf_op jit(solution)/shard_map/ppermute | solution.py:225
  21.5 0.7 collective-permute-start
  22.5 3.7 %collective-permute-done.1 = bf16[64,512]{1,0:T(8,128)(2,1)S(1)} collective-permute-done((bf16[64,512]{1,0:T(8,128)(2,1)S(1)}, bf16[64,512]{1,0:T(8,128)(2,1)S(1)}, u32[]{:S(2)}, u32[]{:S(2)}) %collective-permute-start.1) | collective-permute-done | bytes 65568 | tf_op jit(solution)/shard_map/ppermute | solution.py:225
  26.6 2.7 %collective-permute-start.5 = (bf16[256,512]{1,0:T(8,128)(2,1)S(1)}, bf16[256,512]{1,0:T(8,128)(2,1)S(1)}, u32[]{:S(2)}, u32[]{:S(2)}) collective-permute-start(bf16[256,512]{1,0:T(8,128)(2,1)S(1)} %pad_maximum_fusion.1), channel_id=1, source_target_pairs={{0,192},{2,194},{4,196},{6,198},{8,200},{10,202},{12,204},{14,206}... | collective-permute-start | bytes 786440 | tf_op jit(solution)/shard_map/ppermute | solution.py:225
  29.6 0.6 collective-permute-start.3
  30.3 8.9 %collective-permute-done.3 = bf16[256,512]{1,0:T(8,128)(2,1)S(1)} collective-permute-done((bf16[256,512]{1,0:T(8,128)(2,1)S(1)}, bf16[256,512]{1,0:T(8,128)(2,1)S(1)}, u32[]{:S(2)}, u32[]{:S(2)}) %collective-permute-start.3) | collective-permute-done | bytes 262176 | tf_op jit(solution)/shard_map/ppermute | solution.py:225
  39.3 4.5 %collective-permute-start.7 = (bf16[16,64,512]{2,1,0:T(8,128)(2,1)S(1)}, bf16[16,64,512]{2,1,0:T(8,128)(2,1)S(1)}, u32[]{:S(2)}, u32[]{:S(2)}) collective-permute-start(bf16[16,64,512]{2,1,0:T(8,128)(2,1)S(1)} %bitcast.23), channel_id=1, source_target_pairs={{0,1},{1,0},{2,3},{3,2},{4,5},{5,4},{6,7},{7,6},{8,9},{9,8},{10,11... | collective-permute-start | bytes 3145736 | tf_op jit(solution)/shard_map/ppermute | solution.py:202
  44.5 1.1 %copy-done.2 = bf16[24,128,128]{2,1,0:T(8,128)(2,1)S(1)} copy-done((bf16[24,128,128]{2,1,0:T(8,128)(2,1)S(1)}, bf16[24,128,128]{2,1,0:T(8,128)(2,1)}, u32[]{:S(2)}) %copy-start.2) | copy-done | bytes 786456
  45.6 1.4 %prepare.1 = (bf16[256,3072]{1,0:T(8,128)(2,1)S(1)}, bf16[3072,256]{1,0:T(8,128)(2,1)S(1)}, f32[256,128]{1,0:T(8,128)S(1)}, f32[256,512]{1,0:T(8,128)S(1)}) custom-call(s32[1]{0:T(128)S(6)} %copy.21.count_ref, s32[1,24]{1,0:T(1,128)S(1)} %copy-done.7, bf16[24,128,128]{2,1,0:T(8,128)(2,1)S(1)} %copy-done.2, bf16[256,512]{1,0:T(8,128)(2,1)S(1)} %copy-done, ...), custom_call_target="tpu_custom_call" | custom-call | flops 134217728 | bytes 5242880 | tf_op jit(solution)/shard_map/prepare/pallas_call | solution.py:158
  47.1 5.5 %layer.1 = (bf16[256,512]{1,0:T(8,128)(2,1)}, f32[256,512]{1,0:T(8,128)S(1)}, bf16[128,512]{1,0:T(8,128)(2,1)S(1)}, bf16[16,96,512]{2,1,0:T(8,128)(2,1)S(1)}, bf16[16,96,512]{2,1,0:T(8,128)(2,1)S(1)}) custom-call(s32[1,24]{1,0:T(1,128)S(1)} %copy-done.8, s32[3]{0:T(128)S(1)} %pad_add_fusion.spot_ref, bf16[256,512]{1,0:T(8,128)(2,1)S(1)} %copy-done, ...), custom_call_target="tpu_custom_call" | custom-call | tf_op jit(solution)/shard_map/layer/pallas_call | solution.py:180
  52.6 3.4 %collective-permute-done.8 = bf16[16,96,512]{2,1,0:T(8,128)(2,1)S(1)} collective-permute-done((bf16[16,96,512]{2,1,0:T(8,128)(2,1)S(1)}, bf16[16,96,512]{2,1,0:T(8,128)(2,1)S(1)}, u32[]{:S(2)}, u32[]{:S(2)}) %collective-permute-start.8) | collective-permute-done | bytes 1572896 | tf_op jit(solution)/shard_map/ppermute | solution.py:202
  56.6 1.1 %collective-permute-start.9 = (bf16[4,96,512]{2,1,0:T(8,128)(2,1)S(1)}, bf16[4,96,512]{2,1,0:T(8,128)(2,1)S(1)}, u32[]{:S(2)}, u32[]{:S(2)}) collective-permute-start(bf16[4,96,512]{2,1,0:T(8,128)(2,1)S(1)} %get-tuple-element.31), channel_id=1, source_target_pairs={{0,128},{2,130},{4,132},{6,134},{8,136},{10,138},{12,140},{14,142}... | collective-permute-start | bytes 1179656 | tf_op jit(solution)/shard_map/ppermute | solution.py:225
  58.3 0.9 collective-permute-start.10
  59.3 1.3 %collective-permute-start.12 = (bf16[128,512]{1,0:T(8,128)(2,1)S(1)}, bf16[128,512]{1,0:T(8,128)(2,1)S(1)}, u32[]{:S(2)}, u32[]{:S(2)}) collective-permute-start(bf16[128,512]{1,0:T(8,128)(2,1)S(1)} %get-tuple-element.28), channel_id=1, source_target_pairs={{0,254},{2,0},{4,2},{6,4},{8,6},{10,8},{12,10},{14,12},{16,14},{18... | collective-permute-start | bytes 393224 | tf_op jit(solution)/shard_map/ppermute | solution.py:210
  60.6 4.6 %collective-permute-done.9 = bf16[4,96,512]{2,1,0:T(8,128)(2,1)S(1)} collective-permute-done((bf16[4,96,512]{2,1,0:T(8,128)(2,1)S(1)}, bf16[4,96,512]{2,1,0:T(8,128)(2,1)S(1)}, u32[]{:S(2)}, u32[]{:S(2)}) %collective-permute-start.9) | collective-permute-done | bytes 393248 | tf_op jit(solution)/shard_map/ppermute | solution.py:225
  65.2 2.1 %collective-permute-done.11 = bf16[4,96,512]{2,1,0:T(8,128)(2,1)S(1)} collective-permute-done((bf16[4,96,512]{2,1,0:T(8,128)(2,1)S(1)}, bf16[4,96,512]{2,1,0:T(8,128)(2,1)S(1)}, u32[]{:S(2)}, u32[]{:S(2)}) %collective-permute-start.11) | collective-permute-done | bytes 393248 | tf_op jit(solution)/shard_map/ppermute | solution.py:225
  67.3 2.1 %collective-permute-done.10 = bf16[4,96,512]{2,1,0:T(8,128)(2,1)S(1)} collective-permute-done((bf16[4,96,512]{2,1,0:T(8,128)(2,1)S(1)}, bf16[4,96,512]{2,1,0:T(8,128)(2,1)S(1)}, u32[]{:S(2)}, u32[]{:S(2)}) %collective-permute-start.10) | collective-permute-done | bytes 393248 | tf_op jit(solution)/shard_map/ppermute | solution.py:225
  69.8 0.9 collective-permute-start.15
  70.6 0.6 collective-permute-start.14
  71.3 3.5 %collective-permute-done.13 = bf16[96,512]{1,0:T(8,128)(2,1)S(1)} collective-permute-done((bf16[96,512]{1,0:T(8,128)(2,1)S(1)}, bf16[96,512]{1,0:T(8,128)(2,1)S(1)}, u32[]{:S(2)}, u32[]{:S(2)}) %collective-permute-start.13) | collective-permute-done | bytes 98336 | tf_op jit(solution)/shard_map/ppermute | solution.py:225
  74.7 1.3 %collective-permute-done.14 = bf16[96,512]{1,0:T(8,128)(2,1)S(1)} collective-permute-done((bf16[96,512]{1,0:T(8,128)(2,1)S(1)}, bf16[96,512]{1,0:T(8,128)(2,1)S(1)}, u32[]{:S(2)}, u32[]{:S(2)}) %collective-permute-start.14) | collective-permute-done | bytes 98336 | tf_op jit(solution)/shard_map/ppermute | solution.py:225
  76.2 12.4 %all_to_all.15 = bf16[8,40,512]{2,1,0:T(8,128)(2,1)S(1)} all-to-all(bf16[8,40,512]{2,1,0:T(8,128)(2,1)S(1)} %pad_maximum_fusion), channel_id=1, replica_groups=mesh['y'=4,'x'=4,'z'=8,'c'=2] {'z'}, dimensions={0} | all-to-all | bytes 655360 | tf_op jit(solution)/shard_map/all_to_all | solution.py:242
  88.7 13.0 %all_to_all.16 = bf16[16,32,512]{2,1,0:T(8,128)(2,1)S(1)} all-to-all(bf16[16,32,512]{2,1,0:T(8,128)(2,1)S(1)} %broadcast_in_dim.8), channel_id=1, replica_groups=mesh['y'=4,'x'=4,'z'=8,'c'=2] {'y','x'}, dimensions={0} | all-to-all | bytes 1048576 | tf_op jit(solution)/shard_map/all_to_all | solution.py:242
  101.7 4.7 %collective-permute-start.16 = (bf16[512,512]{1,0:T(8,128)(2,1)S(1)}, bf16[512,512]{1,0:T(8,128)(2,1)S(1)}, u32[]{:S(2)}, u32[]{:S(2)}) collective-permute-start(bf16[512,512]{1,0:T(8,128)(2,1)S(1)} %bitcast.25), channel_id=1, source_target_pairs={{0,1},{1,0},{2,3},{3,2},{4,5},{5,4},{6,7},{7,6},{8,9},{9,8},{10,11... | collective-permute-start | bytes 1572872 | tf_op jit(solution)/shard_map/ppermute | solution.py:202
  106.8 0.9 add.28
  107.6 0.6 slice.58
  108.2 1.5 %select_convert_fusion = (f32[512,512]{1,0:T(8,128)}, f32[512,512]{1,0:T(8,128)}) fusion(bf16[512,512]{1,0:T(8,128)(2,1)S(1)} %collective-permute-done.16, pred[]{:T(512)S(6)} %eq.23, bf16[16,32,512]{2,1,0:T(8,128)(2,1)S(1)} %all_to_all.16), kind=kLoop, calls=%fused_computation.4 | loop fusion | flops 1048576 | bytes 3145729 | tf_op jit(solution)/shard_map/convert_element_type | solution.py:305
  (55 shorter events, 3.6 us)
Async XLA Ops:
  2.0 42.5 %copy-start = (bf16[256,512]{1,0:T(8,128)(2,1)S(1)}, bf16[256,512]{1,0:T(8,128)(2,1)}, u32[]{:S(2)}) copy-start(bf16[256,512]{1,0:T(8,128)(2,1)} %feat_ref.3) | copy-start | bytes 786436
  2.0 42.5 %copy-start.1 = (bf16[512,512]{1,0:T(8,128)(2,1)S(1)}, bf16[512,512]{1,0:T(8,128)(2,1)}, u32[]{:S(2)}) copy-start(bf16[512,512]{1,0:T(8,128)(2,1)} %ws_ref.3) | copy-start | bytes 1572868
  2.0 42.5 %copy-start.7 = (s32[1,24]{1,0:T(1,128)S(1)}, s32[1,24]{1,0:T(1,128)}, u32[]{:S(2)}) copy-start(s32[1,24]{1,0:T(1,128)} %row_ref.1) | copy-start | bytes 292
  2.0 16.5 %all-to-all-start = ((bf16[8,8,512]{2,1,0:T(8,128)(2,1)}), bf16[8,8,512]{2,1,0:T(8,128)(2,1)S(1)}, u32[]{:S(2)}, u32[]{:S(2)}) async-start(bf16[8,8,512]{2,1,0:T(8,128)(2,1)} %broadcast_in_dim.6), calls=%async_computation | async-start | bytes 131072 | tf_op jit(solution)/shard_map/all_to_all | solution.py:242
  13.0 26.3 %collective-permute-start.6 = (bf16[128,512]{1,0:T(8,128)(2,1)}, bf16[128,512]{1,0:T(8,128)(2,1)S(1)}, u32[]{:S(2)}, u32[]{:S(2)}) collective-permute-start(bf16[128,512]{1,0:T(8,128)(2,1)} %convolution_convert_fusion), channel_id=1, source_target_pairs={{0,2},{2,4},{4,6},{6,8},{8,10},{10,12},{12,14},{14,16},{16,18},{18... | collective-permute-start | bytes 393224 | tf_op jit(solution)/shard_map/ppermute | solution.py:210
  18.5 4.1 %collective-permute-start.2 = (bf16[64,512]{1,0:T(8,128)(2,1)S(1)}, bf16[64,512]{1,0:T(8,128)(2,1)S(1)}, u32[]{:S(2)}, u32[]{:S(2)}) collective-permute-start(bf16[64,512]{1,0:T(8,128)(2,1)S(1)} %bitcast.26), channel_id=1, source_target_pairs={{0,48},{2,50},{4,52},{6,54},{8,56},{10,58},{12,60},{14,62},{1,193}... | collective-permute-start | bytes 196616 | tf_op jit(solution)/shard_map/ppermute | solution.py:225
  21.2 5.0 %collective-permute-start.1 = (bf16[64,512]{1,0:T(8,128)(2,1)S(1)}, bf16[64,512]{1,0:T(8,128)(2,1)S(1)}, u32[]{:S(2)}, u32[]{:S(2)}) collective-permute-start(bf16[64,512]{1,0:T(8,128)(2,1)S(1)} %bitcast.27), channel_id=1, source_target_pairs={{0,32},{2,34},{4,36},{6,38},{8,40},{10,42},{12,44},{14,46},{1,129}... | collective-permute-start | bytes 196616 | tf_op jit(solution)/shard_map/ppermute | solution.py:225
  21.5 5.0 %collective-permute-start = (bf16[64,512]{1,0:T(8,128)(2,1)S(1)}, bf16[64,512]{1,0:T(8,128)(2,1)S(1)}, u32[]{:S(2)}, u32[]{:S(2)}) collective-permute-start(bf16[64,512]{1,0:T(8,128)(2,1)S(1)} %bitcast.28), channel_id=1, source_target_pairs={{0,16},{2,18},{4,20},{6,22},{8,24},{10,26},{12,28},{14,30},{1,65},... | collective-permute-start | bytes 196616 | tf_op jit(solution)/shard_map/ppermute | solution.py:225
  26.6 12.6 %collective-permute-start.5 = (bf16[256,512]{1,0:T(8,128)(2,1)S(1)}, bf16[256,512]{1,0:T(8,128)(2,1)S(1)}, u32[]{:S(2)}, u32[]{:S(2)}) collective-permute-start(bf16[256,512]{1,0:T(8,128)(2,1)S(1)} %pad_maximum_fusion.1), channel_id=1, source_target_pairs={{0,192},{2,194},{4,196},{6,198},{8,200},{10,202},{12,204},{14,206}... | collective-permute-start | bytes 786440 | tf_op jit(solution)/shard_map/ppermute | solution.py:225
  29.3 9.8 %collective-permute-start.4 = (bf16[256,512]{1,0:T(8,128)(2,1)S(1)}, bf16[256,512]{1,0:T(8,128)(2,1)S(1)}, u32[]{:S(2)}, u32[]{:S(2)}) collective-permute-start(bf16[256,512]{1,0:T(8,128)(2,1)S(1)} %pad_maximum_fusion.1), channel_id=1, source_target_pairs={{0,128},{2,130},{4,132},{6,134},{8,136},{10,138},{12,140},{14,142}... | collective-permute-start | bytes 786440 | tf_op jit(solution)/shard_map/ppermute | solution.py:225
  29.6 9.5 %collective-permute-start.3 = (bf16[256,512]{1,0:T(8,128)(2,1)S(1)}, bf16[256,512]{1,0:T(8,128)(2,1)S(1)}, u32[]{:S(2)}, u32[]{:S(2)}) collective-permute-start(bf16[256,512]{1,0:T(8,128)(2,1)S(1)} %pad_maximum_fusion.1), channel_id=1, source_target_pairs={{0,64},{2,66},{4,68},{6,70},{8,72},{10,74},{12,76},{14,78},{1,17},... | collective-permute-start | bytes 786440 | tf_op jit(solution)/shard_map/ppermute | solution.py:225
  30.2 16.8 %copy-start.3 = (bf16[512,512]{1,0:T(8,128)(2,1)S(1)}, bf16[512,512]{1,0:T(8,128)(2,1)}, u32[]{:S(2)}) copy-start(bf16[512,512]{1,0:T(8,128)(2,1)} %wn_ref.1) | copy-start | bytes 1572868
  30.3 16.8 %copy-start.8 = (s32[1,24]{1,0:T(1,128)S(1)}, s32[1,24]{1,0:T(1,128)}, u32[]{:S(2)}) copy-start(s32[1,24]{1,0:T(1,128)} %col_ref.1) | copy-start | bytes 292
  39.3 7.8 %collective-permute-start.7 = (bf16[16,64,512]{2,1,0:T(8,128)(2,1)S(1)}, bf16[16,64,512]{2,1,0:T(8,128)(2,1)S(1)}, u32[]{:S(2)}, u32[]{:S(2)}) collective-permute-start(bf16[16,64,512]{2,1,0:T(8,128)(2,1)S(1)} %bitcast.23), channel_id=1, source_target_pairs={{0,1},{1,0},{2,3},{3,2},{4,5},{5,4},{6,7},{7,6},{8,9},{9,8},{10,11... | collective-permute-start | bytes 3145736 | tf_op jit(solution)/shard_map/ppermute | solution.py:202
  44.5 1.1 %copy-start.2 = (bf16[24,128,128]{2,1,0:T(8,128)(2,1)S(1)}, bf16[24,128,128]{2,1,0:T(8,128)(2,1)}, u32[]{:S(2)}) copy-start(bf16[24,128,128]{2,1,0:T(8,128)(2,1)} %adj_ref.1) | copy-start | bytes 2359300
  45.6 1.5 %copy-start.6 = (bf16[256,512]{1,0:T(8,128)(2,1)S(1)}, bf16[256,512]{1,0:T(8,128)(2,1)}, u32[]{:S(2)}) copy-start(bf16[256,512]{1,0:T(8,128)(2,1)} %og_ref.1) | copy-start | bytes 786436
  52.6 3.9 %copy-start.4 = (f32[256,512]{1,0:T(8,128)}, f32[256,512]{1,0:T(8,128)S(1)}, u32[]{:S(2)}) copy-start(f32[256,512]{1,0:T(8,128)S(1)} %get-tuple-element.25) | copy-start | bytes 1572868
  52.6 3.4 %collective-permute-start.8 = (bf16[16,96,512]{2,1,0:T(8,128)(2,1)S(1)}, bf16[16,96,512]{2,1,0:T(8,128)(2,1)S(1)}, u32[]{:S(2)}, u32[]{:S(2)}) collective-permute-start(bf16[16,96,512]{2,1,0:T(8,128)(2,1)S(1)} %get-tuple-element.27), channel_id=1, source_target_pairs={{0,1},{1,0},{2,3},{3,2},{4,5},{5,4},{6,7},{7,6},{8,9},{9,8},{10,11... | collective-permute-start | bytes 4718600 | tf_op jit(solution)/shard_map/ppermute | solution.py:202
  56.6 8.6 %collective-permute-start.9 = (bf16[4,96,512]{2,1,0:T(8,128)(2,1)S(1)}, bf16[4,96,512]{2,1,0:T(8,128)(2,1)S(1)}, u32[]{:S(2)}, u32[]{:S(2)}) collective-permute-start(bf16[4,96,512]{2,1,0:T(8,128)(2,1)S(1)} %get-tuple-element.31), channel_id=1, source_target_pairs={{0,128},{2,130},{4,132},{6,134},{8,136},{10,138},{12,140},{14,142}... | collective-permute-start | bytes 1179656 | tf_op jit(solution)/shard_map/ppermute | solution.py:225
  57.8 9.5 %collective-permute-start.11 = (bf16[4,96,512]{2,1,0:T(8,128)(2,1)S(1)}, bf16[4,96,512]{2,1,0:T(8,128)(2,1)S(1)}, u32[]{:S(2)}, u32[]{:S(2)}) collective-permute-start(bf16[4,96,512]{2,1,0:T(8,128)(2,1)S(1)} %get-tuple-element.32), channel_id=1, source_target_pairs={{0,192},{2,194},{4,196},{6,198},{8,200},{10,202},{12,204},{14,206}... | collective-permute-start | bytes 1179656 | tf_op jit(solution)/shard_map/ppermute | solution.py:225
  58.3 11.1 %collective-permute-start.10 = (bf16[4,96,512]{2,1,0:T(8,128)(2,1)S(1)}, bf16[4,96,512]{2,1,0:T(8,128)(2,1)S(1)}, u32[]{:S(2)}, u32[]{:S(2)}) collective-permute-start(bf16[4,96,512]{2,1,0:T(8,128)(2,1)S(1)} %get-tuple-element.33), channel_id=1, source_target_pairs={{0,64},{2,66},{4,68},{6,70},{8,72},{10,74},{12,76},{14,78},{1,17},... | collective-permute-start | bytes 1179656 | tf_op jit(solution)/shard_map/ppermute | solution.py:225
  59.3 10.3 %collective-permute-start.12 = (bf16[128,512]{1,0:T(8,128)(2,1)S(1)}, bf16[128,512]{1,0:T(8,128)(2,1)S(1)}, u32[]{:S(2)}, u32[]{:S(2)}) collective-permute-start(bf16[128,512]{1,0:T(8,128)(2,1)S(1)} %get-tuple-element.28), channel_id=1, source_target_pairs={{0,254},{2,0},{4,2},{6,4},{8,6},{10,8},{12,10},{14,12},{16,14},{18... | collective-permute-start | bytes 393224 | tf_op jit(solution)/shard_map/ppermute | solution.py:210
  69.6 5.1 %collective-permute-start.13 = (bf16[96,512]{1,0:T(8,128)(2,1)S(1)}, bf16[96,512]{1,0:T(8,128)(2,1)S(1)}, u32[]{:S(2)}, u32[]{:S(2)}) collective-permute-start(bf16[96,512]{1,0:T(8,128)(2,1)S(1)} %get-tuple-element.36), channel_id=1, source_target_pairs={{0,32},{2,34},{4,36},{6,38},{8,40},{10,42},{12,44},{14,46},{1,129}... | collective-permute-start | bytes 294920 | tf_op jit(solution)/shard_map/ppermute | solution.py:225
  69.8 5.0 %collective-permute-start.15 = (bf16[96,512]{1,0:T(8,128)(2,1)S(1)}, bf16[96,512]{1,0:T(8,128)(2,1)S(1)}, u32[]{:S(2)}, u32[]{:S(2)}) collective-permute-start(bf16[96,512]{1,0:T(8,128)(2,1)S(1)} %get-tuple-element.37), channel_id=1, source_target_pairs={{0,48},{2,50},{4,52},{6,54},{8,56},{10,58},{12,60},{14,62},{1,193}... | collective-permute-start | bytes 294920 | tf_op jit(solution)/shard_map/ppermute | solution.py:225
  70.6 5.4 %collective-permute-start.14 = (bf16[96,512]{1,0:T(8,128)(2,1)S(1)}, bf16[96,512]{1,0:T(8,128)(2,1)S(1)}, u32[]{:S(2)}, u32[]{:S(2)}) collective-permute-start(bf16[96,512]{1,0:T(8,128)(2,1)S(1)} %get-tuple-element.38), channel_id=1, source_target_pairs={{0,16},{2,18},{4,20},{6,22},{8,24},{10,26},{12,28},{14,30},{1,65},... | collective-permute-start | bytes 294920 | tf_op jit(solution)/shard_map/ppermute | solution.py:225
  76.1 30.3 %copy-start.9 = (s32[1,128]{1,0:T(1,128)S(1)}, s32[1,128]{1,0:T(1,128)}, u32[]{:S(2)}) copy-start(s32[1,128]{1,0:T(1,128)} %param.16) | copy-start | bytes 1540
  76.2 30.6 %copy-start.5 = (f32[256,512]{1,0:T(8,128)S(1)}, f32[256,512]{1,0:T(8,128)}, u32[]{:S(2)}) copy-start(f32[256,512]{1,0:T(8,128)} %copy-done.4) | copy-start | bytes 1572868
  101.7 6.6 %collective-permute-start.16 = (bf16[512,512]{1,0:T(8,128)(2,1)S(1)}, bf16[512,512]{1,0:T(8,128)(2,1)S(1)}, u32[]{:S(2)}, u32[]{:S(2)}) collective-permute-start(bf16[512,512]{1,0:T(8,128)(2,1)S(1)} %bitcast.25), channel_id=1, source_target_pairs={{0,1},{1,0},{2,3},{3,2},{4,5},{5,4},{6,7},{7,6},{8,9},{9,8},{10,11... | collective-permute-start | bytes 1572872 | tf_op jit(solution)/shard_map/ppermute | solution.py:202

commit v8 on v7

--- a/solution.py
+++ b/solution.py
@@ -196,6 +196,54 @@
         compiler_params=pltpu.CompilerParams(vmem_limit_bytes=16 * 1024 * 1024),
         name="layer",
     )(cols, core, feat, halo, mine, other, wide, flip, norm, pre, ws, wn, og)
+
+
+def own_half_kernel(spot_ref, value_ref, first_ref, second_ref, wide, sem):
+    wide[...] = value_ref[...].astype(F32)
+
+    @pl.when(spot_ref[0] == 0)
+    def _():
+        copy = pltpu.make_async_copy(wide, first_ref, sem)
+        copy.start()
+        copy.wait()
+
+    @pl.when(spot_ref[0] != 0)
+    def _():
+        copy = pltpu.make_async_copy(wide, second_ref, sem)
+        copy.start()
+        copy.wait()
+
+
+def other_half_kernel(spot_ref, value_ref, first_in, second_in, first_ref, second_ref, wide, sem):
+    del first_in, second_in
+    wide[...] = value_ref[...].astype(F32)
+
+    @pl.when(spot_ref[0] != 0)
+    def _():
+        copy = pltpu.make_async_copy(wide, first_ref, sem)
+        copy.start()
+        copy.wait()
+
+    @pl.when(spot_ref[0] == 0)
+    def _():
+        copy = pltpu.make_async_copy(wide, second_ref, sem)
+        copy.start()
+        copy.wait()
+
+
+def write_half(spot, value, pair):
+    anywhere = pl.BlockSpec(memory_space=pl.ANY)
+    full = jax.ShapeDtypeStruct(value.shape, F32)
+    return pl.pallas_call(
+        other_half_kernel if pair else own_half_kernel,
+        out_shape=(full, full),
+        in_specs=[SMEM, VMEM] + [anywhere] * len(pair),
+        out_specs=(anywhere, anywhere),
+        scratch_shapes=[pltpu.VMEM(value.shape, F32), pltpu.SemaphoreType.DMA],
+        input_output_aliases={2: 0, 3: 1} if pair else {},
+        compiler_params=pltpu.CompilerParams(vmem_limit_bytes=16 * 1024 * 1024),
+        name="other_half" if pair else "own_half",
+    )(spot, value, *pair)
 
 
 def swap_cores(value):
@@ -290,7 +338,9 @@
     chip = (keep.astype(F32) + swap_cores(send).astype(F32)).astype(BF16)
     lines = add_along(chip.reshape(SIDE, SIDE, -1, D), True)
     lines, returned = lax.optimization_barrier((lines, returned))
+    grad_features = base + dot(chosen, returned, ((0,), (0,)))
     plane = add_along(lines, False)
+    plane, grad_features = lax.optimization_barrier((plane, grad_features))
     column_rows = zs * OWN
     hub_part = plane[:column_rows].reshape(zs, OWN, D)
     weight_part = plane[column_rows:]
@@ -301,9 +351,8 @@
     factor = 1.0 / math.sqrt(LOCAL_ROWS * 2 * chips)
     weight_mine = spread((total[OWN:] * factor).astype(BF16), PLANE).reshape(D, D)
     weight_other = swap_cores(weight_mine)
-    grad_w_self = jnp.where(core == 0, weight_mine, weight_other).astype(F32)
-    grad_w_neigh = jnp.where(core == 0, weight_other, weight_mine).astype(F32)
-    grad_features = base + dot(chosen, returned, ((0,), (0,)))
+    halves = write_half(core.reshape(1), weight_mine, ())
+    grad_w_self, grad_w_neigh = write_half(core.reshape(1), weight_other, halves)
     return (activations, grad_features, total[:OWN], grad_w_self, grad_w_neigh)
 
 

time: 110 us -> 109 us (level)
  Pallas kernels: 6.89 us -> 8.99 us
  other arithmetic: 3.31 us -> 1.82 us
  waiting for transfers between devices: 34.2 us -> 33 us
    pallas_call x0 -> x2, Pallas kernels: none -> 2.1 us  [write_half(): pl.pallas_call(other_half_kernel if pair else own_half_kernel, out_shape=...]
    convert_element_type x1 -> x0, other arithmetic: 1.49 us -> none  [per_device(): grad_w_neigh = jnp.where(core == 0, weight_other, weight_mine).astype(F32)]
    ppermute x12, waiting for transfers between devices: 26.8 us -> 25.6 us  [hop(): return lax.ppermute(value, ALL, pairs)]
  transfers between devices with their start and end apart: 18 -> 18, of which waited for: 11 -> 11; matrix products, arithmetic and copies ran while one was open for 4% -> 4% of each run, Pallas kernels for 1% -> 2%
where the time goes in v8:
time: 109 us
  waiting for transfers between devices  33 us (30%)
  starting transfers between devices  32.8 us (30%)
  blocking collectives  25.2 us (23%)
  Pallas kernels  8.99 us (8%)
  local copies, waits for them, and re-layouts  3.38 us (3%)
  matrix products  2.18 us (2%)
  other arithmetic  1.82 us (2%)
  between operations  1.71 us (2%)
    ppermute x12, waiting for transfers between devices, hop(): return lax.ppermute(value, ALL, pairs)  25.6 us
    all_to_all x2, blocking collectives, exchange(): return lax.all_to_all(value, axes, 0, 0, tiled=True)  25.2 us
    ppermute x12, starting transfers between devices, hop(): return lax.ppermute(value, ALL, pairs)  11.6 us
    ppermute x3, starting transfers between devices, swap_cores(): return lax.ppermute(value, 'c', [(0, 1), (1, 0)])  9.25 us
    all_to_all x1, starting transfers between devices, exchange(): return lax.all_to_all(value, axes, 0, 0, tiled=True)  9.15 us
    pallas_call x1, Pallas kernels, layer(): pl.pallas_call(layer_kernel, out_shape=(jax.ShapeDtypeStruct((LOCAL_ROWS,...  5.52 us
    all_to_all x1, waiting for transfers between devices, exchange(): return lax.all_to_all(value, axes, 0, 0, tiled=True)  4.03 us
    ppermute x3, waiting for transfers between devices, swap_cores(): return lax.ppermute(value, 'c', [(0, 1), (1, 0)])  3.39 us
  transfers between devices with their start and end apart: 18, of which 11 were waited for; matrix products, arithmetic and copies ran while one was open for 4% of the time, Pallas kernels for 2%

profile of v8, /device:TPU:1, one launch (start us, length us, event | category | flops | bytes accessed | tf_op | source)
XLA Modules:
  0.0 109.1 jit_solution(2570948868976465426)
XLA Ops:
  0.6 1.3 %broadcast_in_dim.6 = bf16[8,8,512]{2,1,0:T(8,128)(2,1)} broadcast(bf16[8,512]{1,0:T(8,128)(2,1)} %param.11), dimensions={1,2} | broadcast | bytes 73728 | tf_op jit(solution)/shard_map/broadcast_in_dim | solution.py:295
  2.0 9.1 %all-to-all-start = ((bf16[8,8,512]{2,1,0:T(8,128)(2,1)}), bf16[8,8,512]{2,1,0:T(8,128)(2,1)S(1)}, u32[]{:S(2)}, u32[]{:S(2)}) async-start(bf16[8,8,512]{2,1,0:T(8,128)(2,1)} %broadcast_in_dim.6), calls=%async_computation | async-start | bytes 131072 | tf_op jit(solution)/shard_map/all_to_all | solution.py:290
  11.1 1.8 %convolution_convert_fusion = bf16[128,512]{1,0:T(8,128)(2,1)} fusion(bf16[256,512]{1,0:T(8,128)(2,1)} %feat_ref.3, s32[128]{0:T(128)} %bitcast.29), kind=kOutput, calls=%fused_computation.1 | convolution fusion | flops 33652736 | bytes 393728 | tf_op jit(solution)/shard_map/dot_general | solution.py:26
  13.0 1.5 %collective-permute-start.6 = (bf16[128,512]{1,0:T(8,128)(2,1)}, bf16[128,512]{1,0:T(8,128)(2,1)S(1)}, u32[]{:S(2)}, u32[]{:S(2)}) collective-permute-start(bf16[128,512]{1,0:T(8,128)(2,1)} %convolution_convert_fusion), channel_id=1, source_target_pairs={{0,2},{2,4},{4,6},{6,8},{8,10},{10,12},{12,14},{14,16},{16,18},{18... | collective-permute-start | bytes 393224 | tf_op jit(solution)/shard_map/ppermute | solution.py:258
  14.4 4.0 %all-to-all-done = bf16[8,8,512]{2,1,0:T(8,128)(2,1)S(1)} async-done(((bf16[8,8,512]{2,1,0:T(8,128)(2,1)}), bf16[8,8,512]{2,1,0:T(8,128)(2,1)S(1)}, u32[]{:S(2)}, u32[]{:S(2)}) %all-to-all-start) | async-done | bytes 65568 | tf_op jit(solution)/shard_map/all_to_all | solution.py:290
  18.5 2.7 %collective-permute-start.2 = (bf16[64,512]{1,0:T(8,128)(2,1)S(1)}, bf16[64,512]{1,0:T(8,128)(2,1)S(1)}, u32[]{:S(2)}, u32[]{:S(2)}) collective-permute-start(bf16[64,512]{1,0:T(8,128)(2,1)S(1)} %bitcast.25), channel_id=1, source_target_pairs={{0,48},{2,50},{4,52},{6,54},{8,56},{10,58},{12,60},{14,62},{1,193}... | collective-permute-start | bytes 196616 | tf_op jit(solution)/shard_map/ppermute | solution.py:273
  21.5 0.7 collective-permute-start
  22.5 3.7 %collective-permute-done.1 = bf16[64,512]{1,0:T(8,128)(2,1)S(1)} collective-permute-done((bf16[64,512]{1,0:T(8,128)(2,1)S(1)}, bf16[64,512]{1,0:T(8,128)(2,1)S(1)}, u32[]{:S(2)}, u32[]{:S(2)}) %collective-permute-start.1) | collective-permute-done | bytes 65568 | tf_op jit(solution)/shard_map/ppermute | solution.py:273
  26.6 2.7 %collective-permute-start.5 = (bf16[256,512]{1,0:T(8,128)(2,1)S(1)}, bf16[256,512]{1,0:T(8,128)(2,1)S(1)}, u32[]{:S(2)}, u32[]{:S(2)}) collective-permute-start(bf16[256,512]{1,0:T(8,128)(2,1)S(1)} %pad_maximum_fusion.1), channel_id=1, source_target_pairs={{0,192},{2,194},{4,196},{6,198},{8,200},{10,202},{12,204},{14,206}... | collective-permute-start | bytes 786440 | tf_op jit(solution)/shard_map/ppermute | solution.py:273
  30.3 8.9 %collective-permute-done.3 = bf16[256,512]{1,0:T(8,128)(2,1)S(1)} collective-permute-done((bf16[256,512]{1,0:T(8,128)(2,1)S(1)}, bf16[256,512]{1,0:T(8,128)(2,1)S(1)}, u32[]{:S(2)}, u32[]{:S(2)}) %collective-permute-start.3) | collective-permute-done | bytes 262176 | tf_op jit(solution)/shard_map/ppermute | solution.py:273
  39.3 4.5 %collective-permute-start.7 = (bf16[16,64,512]{2,1,0:T(8,128)(2,1)S(1)}, bf16[16,64,512]{2,1,0:T(8,128)(2,1)S(1)}, u32[]{:S(2)}, u32[]{:S(2)}) collective-permute-start(bf16[16,64,512]{2,1,0:T(8,128)(2,1)S(1)} %bitcast.23), channel_id=1, source_target_pairs={{0,1},{1,0},{2,3},{3,2},{4,5},{5,4},{6,7},{7,6},{8,9},{9,8},{10,11... | collective-permute-start | bytes 3145736 | tf_op jit(solution)/shard_map/ppermute | solution.py:250
  44.5 1.1 %copy-done.2 = bf16[24,128,128]{2,1,0:T(8,128)(2,1)S(1)} copy-done((bf16[24,128,128]{2,1,0:T(8,128)(2,1)S(1)}, bf16[24,128,128]{2,1,0:T(8,128)(2,1)}, u32[]{:S(2)}) %copy-start.2) | copy-done | bytes 786456
  45.6 1.4 %prepare.1 = (bf16[256,3072]{1,0:T(8,128)(2,1)S(1)}, bf16[3072,256]{1,0:T(8,128)(2,1)S(1)}, f32[256,128]{1,0:T(8,128)S(1)}, f32[256,512]{1,0:T(8,128)S(1)}) custom-call(s32[1]{0:T(128)S(6)} %copy.25.count_ref, s32[1,24]{1,0:T(1,128)S(1)} %copy-done.5, bf16[24,128,128]{2,1,0:T(8,128)(2,1)S(1)} %copy-done.2, bf16[256,512]{1,0:T(8,128)(2,1)S(1)} %copy-done, ...), custom_call_target="tpu_custom_call" | custom-call | flops 134217728 | bytes 5242880 | tf_op jit(solution)/shard_map/prepare/pallas_call | solution.py:158
  47.1 5.5 %layer.1 = (bf16[256,512]{1,0:T(8,128)(2,1)}, f32[256,512]{1,0:T(8,128)S(1)}, bf16[128,512]{1,0:T(8,128)(2,1)S(1)}, bf16[16,96,512]{2,1,0:T(8,128)(2,1)S(1)}, bf16[16,96,512]{2,1,0:T(8,128)(2,1)S(1)}) custom-call(s32[1,24]{1,0:T(1,128)S(1)} %copy-done.6, s32[3]{0:T(128)S(1)} %pad_add_fusion.spot_ref, bf16[256,512]{1,0:T(8,128)(2,1)S(1)} %copy-done, ...), custom_call_target="tpu_custom_call" | custom-call | tf_op jit(solution)/shard_map/layer/pallas_call | solution.py:180
  52.6 3.4 %collective-permute-done.8 = bf16[16,96,512]{2,1,0:T(8,128)(2,1)S(1)} collective-permute-done((bf16[16,96,512]{2,1,0:T(8,128)(2,1)S(1)}, bf16[16,96,512]{2,1,0:T(8,128)(2,1)S(1)}, u32[]{:S(2)}, u32[]{:S(2)}) %collective-permute-start.8) | collective-permute-done | bytes 1572896 | tf_op jit(solution)/shard_map/ppermute | solution.py:250
  56.6 1.1 %collective-permute-start.9 = (bf16[4,96,512]{2,1,0:T(8,128)(2,1)S(1)}, bf16[4,96,512]{2,1,0:T(8,128)(2,1)S(1)}, u32[]{:S(2)}, u32[]{:S(2)}) collective-permute-start(bf16[4,96,512]{2,1,0:T(8,128)(2,1)S(1)} %get-tuple-element.43), channel_id=1, source_target_pairs={{0,128},{2,130},{4,132},{6,134},{8,136},{10,138},{12,140},{14,142}... | collective-permute-start | bytes 1179656 | tf_op jit(solution)/shard_map/ppermute | solution.py:273
  58.3 0.9 collective-permute-start.10
  59.3 1.3 %collective-permute-start.12 = (bf16[128,512]{1,0:T(8,128)(2,1)S(1)}, bf16[128,512]{1,0:T(8,128)(2,1)S(1)}, u32[]{:S(2)}, u32[]{:S(2)}) collective-permute-start(bf16[128,512]{1,0:T(8,128)(2,1)S(1)} %get-tuple-element.33), channel_id=1, source_target_pairs={{0,254},{2,0},{4,2},{6,4},{8,6},{10,8},{12,10},{14,12},{16,14},{18... | collective-permute-start | bytes 393224 | tf_op jit(solution)/shard_map/ppermute | solution.py:258
  60.6 4.6 %collective-permute-done.9 = bf16[4,96,512]{2,1,0:T(8,128)(2,1)S(1)} collective-permute-done((bf16[4,96,512]{2,1,0:T(8,128)(2,1)S(1)}, bf16[4,96,512]{2,1,0:T(8,128)(2,1)S(1)}, u32[]{:S(2)}, u32[]{:S(2)}) %collective-permute-start.9) | collective-permute-done | bytes 393248 | tf_op jit(solution)/shard_map/ppermute | solution.py:273
  65.2 2.1 %collective-permute-done.11 = bf16[4,96,512]{2,1,0:T(8,128)(2,1)S(1)} collective-permute-done((bf16[4,96,512]{2,1,0:T(8,128)(2,1)S(1)}, bf16[4,96,512]{2,1,0:T(8,128)(2,1)S(1)}, u32[]{:S(2)}, u32[]{:S(2)}) %collective-permute-start.11) | collective-permute-done | bytes 393248 | tf_op jit(solution)/shard_map/ppermute | solution.py:273
  67.3 2.1 %collective-permute-done.10 = bf16[4,96,512]{2,1,0:T(8,128)(2,1)S(1)} collective-permute-done((bf16[4,96,512]{2,1,0:T(8,128)(2,1)S(1)}, bf16[4,96,512]{2,1,0:T(8,128)(2,1)S(1)}, u32[]{:S(2)}, u32[]{:S(2)}) %collective-permute-start.10) | collective-permute-done | bytes 393248 | tf_op jit(solution)/shard_map/ppermute | solution.py:273
  69.8 0.9 collective-permute-start.15
  70.6 0.6 collective-permute-start.14
  71.6 0.9 add.31
  72.5 2.2 %collective-permute-done.13 = bf16[96,512]{1,0:T(8,128)(2,1)S(1)} collective-permute-done((bf16[96,512]{1,0:T(8,128)(2,1)S(1)}, bf16[96,512]{1,0:T(8,128)(2,1)S(1)}, u32[]{:S(2)}, u32[]{:S(2)}) %collective-permute-start.13) | collective-permute-done | bytes 98336 | tf_op jit(solution)/shard_map/ppermute | solution.py:273
  74.7 1.3 %collective-permute-done.14 = bf16[96,512]{1,0:T(8,128)(2,1)S(1)} collective-permute-done((bf16[96,512]{1,0:T(8,128)(2,1)S(1)}, bf16[96,512]{1,0:T(8,128)(2,1)S(1)}, u32[]{:S(2)}, u32[]{:S(2)}) %collective-permute-start.14) | collective-permute-done | bytes 98336 | tf_op jit(solution)/shard_map/ppermute | solution.py:273
  76.2 12.2 %all_to_all.15 = bf16[8,40,512]{2,1,0:T(8,128)(2,1)S(1)} all-to-all(bf16[8,40,512]{2,1,0:T(8,128)(2,1)S(1)} %pad_maximum_fusion), channel_id=1, replica_groups=mesh['y'=4,'x'=4,'z'=8,'c'=2] {'z'}, dimensions={0} | all-to-all | bytes 655360 | tf_op jit(solution)/shard_map/all_to_all | solution.py:290
  88.5 13.0 %all_to_all.16 = bf16[16,32,512]{2,1,0:T(8,128)(2,1)S(1)} all-to-all(bf16[16,32,512]{2,1,0:T(8,128)(2,1)S(1)} %broadcast_in_dim.8), channel_id=1, replica_groups=mesh['y'=4,'x'=4,'z'=8,'c'=2] {'y','x'}, dimensions={0} | all-to-all | bytes 1048576 | tf_op jit(solution)/shard_map/all_to_all | solution.py:290
  101.5 4.7 %collective-permute-start.16 = (bf16[512,512]{1,0:T(8,128)(2,1)S(1)}, bf16[512,512]{1,0:T(8,128)(2,1)S(1)}, u32[]{:S(2)}, u32[]{:S(2)}) collective-permute-start(bf16[512,512]{1,0:T(8,128)(2,1)S(1)} %bitcast.21), channel_id=1, source_target_pairs={{0,1},{1,0},{2,3},{3,2},{4,5},{5,4},{6,7},{7,6},{8,9},{9,8},{10,11... | collective-permute-start | bytes 1572872 | tf_op jit(solution)/shard_map/ppermute | solution.py:250
  106.2 0.6 slice.56
  106.9 1.0 own_half.1
  107.9 1.1 other_half.1
  (52 shorter events, 4.2 us)
Async XLA Ops:
  2.0 42.5 %copy-start = (bf16[256,512]{1,0:T(8,128)(2,1)S(1)}, bf16[256,512]{1,0:T(8,128)(2,1)}, u32[]{:S(2)}) copy-start(bf16[256,512]{1,0:T(8,128)(2,1)} %feat_ref.3) | copy-start | bytes 786436
  2.0 42.5 %copy-start.1 = (bf16[512,512]{1,0:T(8,128)(2,1)S(1)}, bf16[512,512]{1,0:T(8,128)(2,1)}, u32[]{:S(2)}) copy-start(bf16[512,512]{1,0:T(8,128)(2,1)} %ws_ref.3) | copy-start | bytes 1572868
  2.0 42.5 %copy-start.5 = (s32[1,24]{1,0:T(1,128)S(1)}, s32[1,24]{1,0:T(1,128)}, u32[]{:S(2)}) copy-start(s32[1,24]{1,0:T(1,128)} %row_ref.1) | copy-start | bytes 292
  2.0 16.5 %all-to-all-start = ((bf16[8,8,512]{2,1,0:T(8,128)(2,1)}), bf16[8,8,512]{2,1,0:T(8,128)(2,1)S(1)}, u32[]{:S(2)}, u32[]{:S(2)}) async-start(bf16[8,8,512]{2,1,0:T(8,128)(2,1)} %broadcast_in_dim.6), calls=%async_computation | async-start | bytes 131072 | tf_op jit(solution)/shard_map/all_to_all | solution.py:290
  13.0 26.3 %collective-permute-start.6 = (bf16[128,512]{1,0:T(8,128)(2,1)}, bf16[128,512]{1,0:T(8,128)(2,1)S(1)}, u32[]{:S(2)}, u32[]{:S(2)}) collective-permute-start(bf16[128,512]{1,0:T(8,128)(2,1)} %convolution_convert_fusion), channel_id=1, source_target_pairs={{0,2},{2,4},{4,6},{6,8},{8,10},{10,12},{12,14},{14,16},{16,18},{18... | collective-permute-start | bytes 393224 | tf_op jit(solution)/shard_map/ppermute | solution.py:258
  18.5 4.1 %collective-permute-start.2 = (bf16[64,512]{1,0:T(8,128)(2,1)S(1)}, bf16[64,512]{1,0:T(8,128)(2,1)S(1)}, u32[]{:S(2)}, u32[]{:S(2)}) collective-permute-start(bf16[64,512]{1,0:T(8,128)(2,1)S(1)} %bitcast.25), channel_id=1, source_target_pairs={{0,48},{2,50},{4,52},{6,54},{8,56},{10,58},{12,60},{14,62},{1,193}... | collective-permute-start | bytes 196616 | tf_op jit(solution)/shard_map/ppermute | solution.py:273
  21.2 5.0 %collective-permute-start.1 = (bf16[64,512]{1,0:T(8,128)(2,1)S(1)}, bf16[64,512]{1,0:T(8,128)(2,1)S(1)}, u32[]{:S(2)}, u32[]{:S(2)}) collective-permute-start(bf16[64,512]{1,0:T(8,128)(2,1)S(1)} %bitcast.26), channel_id=1, source_target_pairs={{0,32},{2,34},{4,36},{6,38},{8,40},{10,42},{12,44},{14,46},{1,129}... | collective-permute-start | bytes 196616 | tf_op jit(solution)/shard_map/ppermute | solution.py:273
  21.5 5.0 %collective-permute-start = (bf16[64,512]{1,0:T(8,128)(2,1)S(1)}, bf16[64,512]{1,0:T(8,128)(2,1)S(1)}, u32[]{:S(2)}, u32[]{:S(2)}) collective-permute-start(bf16[64,512]{1,0:T(8,128)(2,1)S(1)} %bitcast.27), channel_id=1, source_target_pairs={{0,16},{2,18},{4,20},{6,22},{8,24},{10,26},{12,28},{14,30},{1,65},... | collective-permute-start | bytes 196616 | tf_op jit(solution)/shard_map/ppermute | solution.py:273
  26.6 12.6 %collective-permute-start.5 = (bf16[256,512]{1,0:T(8,128)(2,1)S(1)}, bf16[256,512]{1,0:T(8,128)(2,1)S(1)}, u32[]{:S(2)}, u32[]{:S(2)}) collective-permute-start(bf16[256,512]{1,0:T(8,128)(2,1)S(1)} %pad_maximum_fusion.1), channel_id=1, source_target_pairs={{0,192},{2,194},{4,196},{6,198},{8,200},{10,202},{12,204},{14,206}... | collective-permute-start | bytes 786440 | tf_op jit(solution)/shard_map/ppermute | solution.py:273
  29.3 9.8 %collective-permute-start.4 = (bf16[256,512]{1,0:T(8,128)(2,1)S(1)}, bf16[256,512]{1,0:T(8,128)(2,1)S(1)}, u32[]{:S(2)}, u32[]{:S(2)}) collective-permute-start(bf16[256,512]{1,0:T(8,128)(2,1)S(1)} %pad_maximum_fusion.1), channel_id=1, source_target_pairs={{0,128},{2,130},{4,132},{6,134},{8,136},{10,138},{12,140},{14,142}... | collective-permute-start | bytes 786440 | tf_op jit(solution)/shard_map/ppermute | solution.py:273
  29.6 9.5 %collective-permute-start.3 = (bf16[256,512]{1,0:T(8,128)(2,1)S(1)}, bf16[256,512]{1,0:T(8,128)(2,1)S(1)}, u32[]{:S(2)}, u32[]{:S(2)}) collective-permute-start(bf16[256,512]{1,0:T(8,128)(2,1)S(1)} %pad_maximum_fusion.1), channel_id=1, source_target_pairs={{0,64},{2,66},{4,68},{6,70},{8,72},{10,74},{12,76},{14,78},{1,17},... | collective-permute-start | bytes 786440 | tf_op jit(solution)/shard_map/ppermute | solution.py:273
  30.2 16.8 %copy-start.3 = (bf16[512,512]{1,0:T(8,128)(2,1)S(1)}, bf16[512,512]{1,0:T(8,128)(2,1)}, u32[]{:S(2)}) copy-start(bf16[512,512]{1,0:T(8,128)(2,1)} %wn_ref.1) | copy-start | bytes 1572868
  30.3 16.8 %copy-start.6 = (s32[1,24]{1,0:T(1,128)S(1)}, s32[1,24]{1,0:T(1,128)}, u32[]{:S(2)}) copy-start(s32[1,24]{1,0:T(1,128)} %col_ref.1) | copy-start | bytes 292
  39.3 7.8 %collective-permute-start.7 = (bf16[16,64,512]{2,1,0:T(8,128)(2,1)S(1)}, bf16[16,64,512]{2,1,0:T(8,128)(2,1)S(1)}, u32[]{:S(2)}, u32[]{:S(2)}) collective-permute-start(bf16[16,64,512]{2,1,0:T(8,128)(2,1)S(1)} %bitcast.23), channel_id=1, source_target_pairs={{0,1},{1,0},{2,3},{3,2},{4,5},{5,4},{6,7},{7,6},{8,9},{9,8},{10,11... | collective-permute-start | bytes 3145736 | tf_op jit(solution)/shard_map/ppermute | solution.py:250
  44.5 1.1 %copy-start.2 = (bf16[24,128,128]{2,1,0:T(8,128)(2,1)S(1)}, bf16[24,128,128]{2,1,0:T(8,128)(2,1)}, u32[]{:S(2)}) copy-start(bf16[24,128,128]{2,1,0:T(8,128)(2,1)} %adj_ref.1) | copy-start | bytes 2359300
  45.6 1.5 %copy-start.4 = (bf16[256,512]{1,0:T(8,128)(2,1)S(1)}, bf16[256,512]{1,0:T(8,128)(2,1)}, u32[]{:S(2)}) copy-start(bf16[256,512]{1,0:T(8,128)(2,1)} %og_ref.1) | copy-start | bytes 786436
  52.6 3.4 %collective-permute-start.8 = (bf16[16,96,512]{2,1,0:T(8,128)(2,1)S(1)}, bf16[16,96,512]{2,1,0:T(8,128)(2,1)S(1)}, u32[]{:S(2)}, u32[]{:S(2)}) collective-permute-start(bf16[16,96,512]{2,1,0:T(8,128)(2,1)S(1)} %get-tuple-element.32), channel_id=1, source_target_pairs={{0,1},{1,0},{2,3},{3,2},{4,5},{5,4},{6,7},{7,6},{8,9},{9,8},{10,11... | collective-permute-start | bytes 4718600 | tf_op jit(solution)/shard_map/ppermute | solution.py:250
  56.6 14.6 %copy-start.7 = (s32[1,128]{1,0:T(1,128)S(1)}, s32[1,128]{1,0:T(1,128)}, u32[]{:S(2)}) copy-start(s32[1,128]{1,0:T(1,128)} %param.16) | copy-start | bytes 1540
  56.6 8.6 %collective-permute-start.9 = (bf16[4,96,512]{2,1,0:T(8,128)(2,1)S(1)}, bf16[4,96,512]{2,1,0:T(8,128)(2,1)S(1)}, u32[]{:S(2)}, u32[]{:S(2)}) collective-permute-start(bf16[4,96,512]{2,1,0:T(8,128)(2,1)S(1)} %get-tuple-element.43), channel_id=1, source_target_pairs={{0,128},{2,130},{4,132},{6,134},{8,136},{10,138},{12,140},{14,142}... | collective-permute-start | bytes 1179656 | tf_op jit(solution)/shard_map/ppermute | solution.py:273
  57.8 9.5 %collective-permute-start.11 = (bf16[4,96,512]{2,1,0:T(8,128)(2,1)S(1)}, bf16[4,96,512]{2,1,0:T(8,128)(2,1)S(1)}, u32[]{:S(2)}, u32[]{:S(2)}) collective-permute-start(bf16[4,96,512]{2,1,0:T(8,128)(2,1)S(1)} %get-tuple-element.44), channel_id=1, source_target_pairs={{0,192},{2,194},{4,196},{6,198},{8,200},{10,202},{12,204},{14,206}... | collective-permute-start | bytes 1179656 | tf_op jit(solution)/shard_map/ppermute | solution.py:273
  58.3 11.1 %collective-permute-start.10 = (bf16[4,96,512]{2,1,0:T(8,128)(2,1)S(1)}, bf16[4,96,512]{2,1,0:T(8,128)(2,1)S(1)}, u32[]{:S(2)}, u32[]{:S(2)}) collective-permute-start(bf16[4,96,512]{2,1,0:T(8,128)(2,1)S(1)} %get-tuple-element.45), channel_id=1, source_target_pairs={{0,64},{2,66},{4,68},{6,70},{8,72},{10,74},{12,76},{14,78},{1,17},... | collective-permute-start | bytes 1179656 | tf_op jit(solution)/shard_map/ppermute | solution.py:273
  59.3 10.3 %collective-permute-start.12 = (bf16[128,512]{1,0:T(8,128)(2,1)S(1)}, bf16[128,512]{1,0:T(8,128)(2,1)S(1)}, u32[]{:S(2)}, u32[]{:S(2)}) collective-permute-start(bf16[128,512]{1,0:T(8,128)(2,1)S(1)} %get-tuple-element.33), channel_id=1, source_target_pairs={{0,254},{2,0},{4,2},{6,4},{8,6},{10,8},{12,10},{14,12},{16,14},{18... | collective-permute-start | bytes 393224 | tf_op jit(solution)/shard_map/ppermute | solution.py:258
  69.6 5.1 %collective-permute-start.13 = (bf16[96,512]{1,0:T(8,128)(2,1)S(1)}, bf16[96,512]{1,0:T(8,128)(2,1)S(1)}, u32[]{:S(2)}, u32[]{:S(2)}) collective-permute-start(bf16[96,512]{1,0:T(8,128)(2,1)S(1)} %get-tuple-element.46), channel_id=1, source_target_pairs={{0,32},{2,34},{4,36},{6,38},{8,40},{10,42},{12,44},{14,46},{1,129}... | collective-permute-start | bytes 294920 | tf_op jit(solution)/shard_map/ppermute | solution.py:273
  69.8 5.0 %collective-permute-start.15 = (bf16[96,512]{1,0:T(8,128)(2,1)S(1)}, bf16[96,512]{1,0:T(8,128)(2,1)S(1)}, u32[]{:S(2)}, u32[]{:S(2)}) collective-permute-start(bf16[96,512]{1,0:T(8,128)(2,1)S(1)} %get-tuple-element.47), channel_id=1, source_target_pairs={{0,48},{2,50},{4,52},{6,54},{8,56},{10,58},{12,60},{14,62},{1,193}... | collective-permute-start | bytes 294920 | tf_op jit(solution)/shard_map/ppermute | solution.py:273
  70.6 5.4 %collective-permute-start.14 = (bf16[96,512]{1,0:T(8,128)(2,1)S(1)}, bf16[96,512]{1,0:T(8,128)(2,1)S(1)}, u32[]{:S(2)}, u32[]{:S(2)}) collective-permute-start(bf16[96,512]{1,0:T(8,128)(2,1)S(1)} %get-tuple-element.48), channel_id=1, source_target_pairs={{0,16},{2,18},{4,20},{6,22},{8,24},{10,26},{12,28},{14,30},{1,65},... | collective-permute-start | bytes 294920 | tf_op jit(solution)/shard_map/ppermute | solution.py:273
  101.5 6.4 %collective-permute-start.16 = (bf16[512,512]{1,0:T(8,128)(2,1)S(1)}, bf16[512,512]{1,0:T(8,128)(2,1)S(1)}, u32[]{:S(2)}, u32[]{:S(2)}) collective-permute-start(bf16[512,512]{1,0:T(8,128)(2,1)S(1)} %bitcast.21), channel_id=1, source_target_pairs={{0,1},{1,0},{2,3},{3,2},{4,5},{5,4},{6,7},{7,6},{8,9},{9,8},{10,11... | collective-permute-start | bytes 1572872 | tf_op jit(solution)/shard_map/ppermute | solution.py:250
